TPU v7x, 128 devices: a whole 4x4x4 slice. The times are simulated.
128 devices in a mesh: replica: 8 (over z, x_lo), dp: 2 (over x_hi), tensor: 8 (over y, core).
Axes of the slice: x: 4 (x_hi: 2, x_lo: 2; x = x_hi * 2 + x_lo), y: 4, z: 4, core: 2. Of those that a mesh axis runs over, the one named last changes fastest.
Arguments:
- tokens: bfloat16 [8, 2048, 2048], P('replica', 'dp', 'tensor'), may hold values from -6 to 6
- grad_out: bfloat16 [8, 2048, 14336], P('replica', 'dp', 'tensor'), may hold values from -250 to 250, as said below
- weights: bfloat16 [8, 2048, 14336], P('replica', 'dp', 'tensor'), may hold values from -6 to 6
- first_moment: bfloat16 [8, 2048, 14336], P('replica', 'dp', 'tensor'), may hold values from -4 to 4
- second_moment: bfloat16 [8, 2048, 14336], P('replica', 'dp', 'tensor'), may hold values from 0.019897461 to 0.19921875
Outputs:
- new_weights: bfloat16 [8, 2048, 14336], P('replica', 'dp', 'tensor')
- new_first: bfloat16 [8, 2048, 14336], P('replica', 'dp', 'tensor')
- new_second: bfloat16 [8, 2048, 14336], P('replica', 'dp', 'tensor')
Inputs may be any that keep to these rules, and one draw needn't show every extreme that they name: `grad_out`: the upstream gradient.
All inputs are finite; a program needn't handle non-finite values.
Results may differ from a plain program's by a relative error of at most 0.0051.
Values may be sent and summed in bfloat16 or wider, within the bound.
No kernel may reach another device: no remote copies, remote signals or barrier semaphores. Data moves between devices by JAX's collectives and lax.ppermute only.
A program may use at most 192 MiB of HBM per device.

v0:
```python
import jax
import jax.numpy as jnp
from jax import lax
from jax.sharding import PartitionSpec as P

D = 2048
FF = 14336
STEP = 1


def partner(value, axis, bit):
    mask = 2**bit
    pairs = [(source, source ^ mask) for source in range(lax.axis_size(axis))]
    return lax.ppermute(value, axis, pairs)


def adamw(grad, total, weights, first_moment, second_moment):
    clip = jnp.minimum(1.0, 1.0 / jnp.sqrt(total / (D * FF) + 1e-06))
    scaled = clip * grad
    moment_one = 0.9 * first_moment.astype(jnp.float32) + 0.1 * scaled
    moment_two = 0.95 * second_moment.astype(jnp.float32) + 0.05 * scaled * scaled
    fix_one = 1.0 - 0.9**STEP
    fix_two = 1.0 - 0.95**STEP
    update = moment_one / fix_one / (jnp.sqrt(moment_two / fix_two) + 1e-08)
    old = weights.astype(jnp.float32)
    fresh = old - 0.05 * (update + 0.1 * old)
    return jnp.stack(
        [
            fresh.astype(jnp.bfloat16),
            moment_one.astype(jnp.bfloat16),
            moment_two.astype(jnp.bfloat16),
        ]
    )


def body(tokens, grad_out, weights, first_moment, second_moment):
    whole = lax.all_gather(tokens[0], "tensor", axis=1, tiled=True)
    upstream = grad_out[0]
    grad = lax.psum_scatter(
        lax.dot_general(
            whole, upstream, (((0,), (0,)), ((), ())), preferred_element_type=jnp.float32
        ),
        "dp",
        scatter_dimension=0,
        tiled=True,
    )
    local_sq = jnp.sum(grad * grad)
    bit_index = lax.axis_size("replica").bit_length() - 2
    total = lax.psum(local_sq, ("dp", "tensor"))
    states = adamw(grad, total, weights[0], first_moment[0], second_moment[0])
    others = partner(states, "replica", bit_index)
    mixed = (0.5 * (states.astype(jnp.float32) + others.astype(jnp.float32))).astype(jnp.bfloat16)
    return (mixed[0][None], mixed[1][None], mixed[2][None])


def solution(mesh):
    placed = (
        P("replica", "dp", "tensor"),
        P("replica", "dp", "tensor"),
        P("replica", "dp", "tensor"),
        P("replica", "dp", "tensor"),
        P("replica", "dp", "tensor"),
    )
    return jax.shard_map(
        body,
        mesh=mesh,
        in_specs=placed,
        out_specs=(
            P("replica", "dp", "tensor"),
            P("replica", "dp", "tensor"),
            P("replica", "dp", "tensor"),
        ),
        check_vma=False,
    )
```

profile of v0, /device:TPU:6, one launch (start us, length us, event | category | flops | bytes accessed | tf_op | source)
XLA Modules:
  0.0 540.0 jit_solution(14032004616073285268)
XLA Ops:
  7.2 0.0 all-gather.3.cloned.1.call-start
  7.2 0.7 all-gather.3.cloned.1.call-update
  7.9 0.0 reduce-scatter.2.cloned.1.call-start
  7.9 40.1 %all-gather.3.cloned.1.call-done = bf16[1,1024,2048]{2,1,0:T(8,128)(2,1)} async-done(((bf16[1,1024,256]{2,1,0:T(8,128)(2,1)}), bf16[1,1024,2048]{2,1,0:T(8,128)(2,1)}) %all-gather.3.cloned.1.call-update) | async-done | bytes 4194320 | tf_op jit(solution)/shard_map/all_gather | solution.py:37
  48.1 13.8 %fusion.4 = f32[2048,1792]{1,0:T(8,128)} fusion(bf16[1,1024,2048]{2,1,0:T(8,128)(2,1)} %all-gather.3.cloned.1.call-done, bf16[1,1024,1792]{2,1,0:T(8,128)(2,1)} %param.6), kind=kOutput, calls=%fused_computation.11 | convolution fusion | flops 7516192768 | bytes 22544384 | tf_op jit(solution)/shard_map/dot_general | solution.py:40
  61.9 0.0 reduce-scatter.2.cloned.1.call-update
  61.9 170.7 %reduce-scatter.2.cloned.1.call-done = f32[1024,1792]{1,0:T(8,128)} async-done(((f32[2048,1792]{1,0:T(8,128)}), f32[1024,1792]{1,0:T(8,128)}) %reduce-scatter.2.cloned.1.call-update) | async-done | bytes 7340048 | tf_op jit(solution)/shard_map/reduce_scatter | solution.py:39
  232.6 5.6 %multiply_reduce_fusion = f32[]{:T(128)} fusion(f32[1024,1792]{1,0:T(8,128)} %reduce-scatter.2.cloned.1.call-done), kind=kLoop, calls=%fused_computation.10 | loop fusion | flops 3670015 | bytes 7340036 | tf_op jit(solution)/shard_map/reduce_sum | solution.py:47
  238.2 37.5 %psum.7 = f32[]{:T(128)} all-reduce(f32[]{:T(128)} %multiply_reduce_fusion), channel_id=1, replica_groups=mesh['replica'=8,'dp'=2,'tensor'=8] {'dp','tensor'}, use_global_device_ids=true, to_apply=%region_2.0 | all-reduce | flops 1 | bytes 8 | tf_op jit(solution)/shard_map/psum | solution.py:49
  276.3 11.1 %fusion.9 = (bf16[1,1024,1792]{2,1,0:T(8,128)(2,1)S(1)}, bf16[1,1024,1792]{2,1,0:T(8,128)(2,1)S(1)}, bf16[1,1024,1792]{2,1,0:T(8,128)(2,1)S(1)}) fusion(bf16[1,1024,1792]{2,1,0:T(8,128)(2,1)} %param.9, f32[1024,1792]{1,0:T(8,128)} %reduce-scatter.2.cloned.1.call-done, f32[]{:T(128)S(6)} %min.3, bf16[1,1024,1792]{2,1,0:T(8,128)(2,1)} %param.8, ...), kind=kLoop, calls=%fused_computation.17 | loop fusion | flops 40370176 | bytes 29360132 | tf_op jit(solution)/shard_map/stack | solution.py:27
  287.4 1.4 pad_maximum_fusion
  288.8 3.2 collective-permute-start
  292.0 233.1 %collective-permute-done = bf16[3,1024,1792]{2,1,0:T(8,128)(2,1)S(1)} collective-permute-done((bf16[3,1024,1792]{2,1,0:T(8,128)(2,1)S(1)}, bf16[3,1024,1792]{2,1,0:T(8,128)(2,1)S(1)}, u32[]{:S(2)}, u32[]{:S(2)}) %collective-permute-start) | collective-permute-done | bytes 11010080 | tf_op jit(solution)/shard_map/ppermute | solution.py:14
  525.1 3.8 multiply_convert_fusion
  528.9 4.3 fusion.10
Async XLA Ops:
  7.2 40.9 %all-gather.3.cloned.1.call-start = ((), (), s32[]{:S(2)}) async-start(), calls=%async_computation.2 | async-start | bytes 4718592 | tf_op jit(solution)/shard_map/all_gather | solution.py:37
  7.9 224.7 %reduce-scatter.2.cloned.1.call-start = ((), (), s32[]{:S(2)}) async-start(), calls=%async_computation.1 | async-start | bytes 22020096 | tf_op jit(solution)/shard_map/reduce_scatter | solution.py:39
  288.8 236.3 %collective-permute-start = (bf16[3,1024,1792]{2,1,0:T(8,128)(2,1)S(1)}, bf16[3,1024,1792]{2,1,0:T(8,128)(2,1)S(1)}, u32[]{:S(2)}, u32[]{:S(2)}) collective-permute-start(bf16[3,1024,1792]{2,1,0:T(8,128)(2,1)S(1)} %pad_maximum_fusion), channel_id=1, source_target_pairs={{0,64},{16,80},{32,96},{48,112},{64,0},{80,16},{96,32},{112,48},{1... | collective-permute-start | bytes 33030152 | tf_op jit(solution)/shard_map/ppermute | solution.py:14
Sparse Core Ops, SparseCore 0:
  9.7 38.3 all-gather.2
  62.0 170.5 reduce-scatter.1
where the time goes:
time: 542 us; the launch traced here: 540 us
  waiting for transfers between devices  445 us (82%)
  blocking collectives  37.5 us (7%)
  other arithmetic  21.8 us (4%)
  between operations  14.8 us (3%)
  matrix products  13.8 us (3%)
    ppermute x1, waiting for transfers between devices, partner(): return lax.ppermute(value, axis, pairs)  233 us
    reduce_scatter x1, waiting for transfers between devices, body(): lax.psum_scatter(lax.dot_general(whole, upstream, (((0,), (0,)), ((), ())...  171 us
    all_gather x1, waiting for transfers between devices, body(): whole = lax.all_gather(tokens[0], 'tensor', axis=1, tiled=True)  40.1 us
    psum x1, blocking collectives, body(): total = lax.psum(local_sq, ('dp', 'tensor'))  37.5 us
    dot_general x1, matrix products, body(): lax.dot_general(whole, upstream, (((0,), (0,)), ((), ())), preferred_elem...  13.8 us
    another operation x2, other arithmetic, adamw(): jnp.stack([fresh.astype(jnp.bfloat16), moment_one.astype(jnp.bfloat16), m...  12.5 us
  transfers between devices with their start and end apart: 3, of which 3 were waited for; matrix products, arithmetic and copies ran while one was open for 0% of the time, Pallas kernels for 0%

commit v1 on v0

v1 whole, which is shorter than its diff:
```python
import jax
import jax.numpy as jnp
from jax import lax
from jax.experimental import pallas as pl
from jax.experimental.pallas import tpu as pltpu
from jax.sharding import PartitionSpec as P

D = 2048
FF = 14336
STEP = 1
COLS = 256
FIX_ONE = 1.0 - 0.9**STEP
FIX_TWO = 1.0 - 0.95**STEP
BF16 = jnp.bfloat16
F32 = jnp.float32


def across(value):
    return lax.ppermute(value, "replica", [(s, s ^ 4) for s in range(8)])


def swap_dp(value):
    return lax.ppermute(value, "dp", [(0, 1), (1, 0)])


def gather_tokens(mine):
    pairs = []
    for d in range(2):
        for t in range(8):
            stays = t // 4 == d
            pairs.append((d * 8 + t, d * 8 + t if stays else (1 - d) * 8 + (t ^ 4)))
    moved = lax.ppermute(mine, ("dp", "tensor"), pairs)
    return lax.all_gather(moved, "tensor", axis=0, tiled=False)


def group_sum(value):
    for bit in (1, 2, 4):
        value = value + lax.ppermute(value, "tensor", [(t, t ^ bit) for t in range(8)])
    return value + swap_dp(value)


def clip_of(total_ref):
    total = jnp.sum(total_ref[...], keepdims=True)
    return jnp.minimum(1.0, 1.0 / jnp.sqrt(total / (D * FF) + 1e-06))


def moments(scaled, first, second):
    one = 0.9 * first.astype(F32) + 0.1 * scaled
    two = 0.95 * second.astype(F32) + 0.05 * scaled * scaled
    return one.astype(BF16), two.astype(BF16)


def stepped(old, one, two):
    old = old.astype(F32)
    one = one.astype(F32)
    two = two.astype(F32)
    update = one / FIX_ONE / (jnp.sqrt(two / FIX_TWO) + 1e-08)
    return (old - 0.05 * (update + 0.1 * old)).astype(BF16)


def mean(a, b):
    return (0.5 * (a.astype(F32) + b.astype(F32))).astype(BF16)


def make_kernel(total_ref, grad_ref, first_ref, second_ref, out_ref):
    one, two = moments(clip_of(total_ref) * grad_ref[...], first_ref[...], second_ref[...])
    out_ref[0] = one
    out_ref[1] = two


def make(total, grad, first, second, chunk):
    rows = grad.shape[0]
    step = 256
    wide = pl.BlockSpec((step, COLS), lambda i: (i, chunk))
    return pl.pallas_call(
        make_kernel,
        grid=(rows // step,),
        out_shape=jax.ShapeDtypeStruct((2, rows, COLS), BF16),
        in_specs=[
            pl.BlockSpec((8, 128), lambda i: (0, 0)),
            pl.BlockSpec((step, COLS), lambda i: (i, 0)),
            wide,
            wide,
        ],
        out_specs=pl.BlockSpec((2, step, COLS), lambda i: (0, i, 0)),
        cost_estimate=pl.CostEstimate(flops=10 * rows * COLS, bytes_accessed=12 * rows * COLS, transcendentals=0),
    )(total, grad, first, second)


def mix_kernel(mine_ref, other_ref, old_ref, old_other_ref, *rest):
    w_ref, one_ref, two_ref = rest[-3:]
    one, two = mine_ref[0], mine_ref[1]
    one_other, two_other = other_ref[0], other_ref[1]
    w_ref[...] = mean(stepped(old_ref[...], one, two), stepped(old_other_ref[...], one_other, two_other))
    one_ref[...] = mean(one, one_other)
    two_ref[...] = mean(two, two_other)


def mix(mine, other, old, old_other, chunk, outs):
    rows, cols = old.shape
    step = 256
    wide = pl.BlockSpec((step, COLS), lambda i: (i, chunk))
    pair = pl.BlockSpec((2, step, COLS), lambda i: (0, i, 0))
    shape = jax.ShapeDtypeStruct((rows, cols), BF16)
    return pl.pallas_call(
        mix_kernel,
        grid=(rows // step,),
        out_shape=(shape, shape, shape),
        in_specs=[pair, pair, wide, wide] + [pl.BlockSpec(memory_space=pl.ANY)] * len(outs),
        out_specs=(wide, wide, wide),
        input_output_aliases={4 + i: i for i in range(len(outs))},
        cost_estimate=pl.CostEstimate(flops=40 * rows * COLS, bytes_accessed=18 * rows * COLS, transcendentals=2 * rows * COLS),
    )(mine, other, old, old_other, *outs)


def first_mix_kernel(total_ref, total_other_ref, grad_ref, grad_other_ref, first_ref, first_other_ref, second_ref, second_other_ref, old_ref, old_other_ref, w_ref, one_ref, two_ref):
    one, two = moments(clip_of(total_ref) * grad_ref[...], first_ref[...], second_ref[...])
    scaled = clip_of(total_other_ref) * grad_other_ref[...].astype(F32)
    one_other, two_other = moments(scaled, first_other_ref[...], second_other_ref[...])
    w_ref[...] = mean(stepped(old_ref[...], one, two), stepped(old_other_ref[...], one_other, two_other))
    one_ref[...] = mean(one, one_other)
    two_ref[...] = mean(two, two_other)


def first_mix(total, total_other, grad, grad_other, first, first_other, second, second_other, old, old_other, chunk):
    rows, cols = old.shape
    step = 256
    wide = pl.BlockSpec((step, COLS), lambda i: (i, chunk))
    thin = pl.BlockSpec((step, COLS), lambda i: (i, 0))
    whole = pl.BlockSpec((8, 128), lambda i: (0, 0))
    shape = jax.ShapeDtypeStruct((rows, cols), BF16)
    return pl.pallas_call(
        first_mix_kernel,
        grid=(rows // step,),
        out_shape=(shape, shape, shape),
        in_specs=[whole, whole, thin, thin, wide, thin, wide, thin, wide, wide],
        out_specs=(wide, wide, wide),
        cost_estimate=pl.CostEstimate(flops=60 * rows * COLS, bytes_accessed=22 * rows * COLS, transcendentals=2 * rows * COLS),
    )(total, total_other, grad, grad_other, first, first_other, second, second_other, old, old_other)


def body(tokens, grad_out, weights, first_moment, second_moment):
    upstream, old = grad_out[0], weights[0]
    first, second = first_moment[0], second_moment[0]
    rows, cols = old.shape
    chunks = cols // COLS
    part = lambda array, c: array[:, c * COLS : (c + 1) * COLS]

    features = gather_tokens(tokens[0])
    up_other = [swap_dp(part(upstream, c)) for c in range(chunks)]
    old_other = across(old)
    first_other = across(part(first, 0))
    second_other = across(part(second, 0))

    d = lax.axis_index("dp")
    mine = lax.dynamic_slice_in_dim(features, d * 4, 4, 0)
    theirs = lax.dynamic_slice_in_dim(features, (1 - d) * 4, 4, 0)

    def product(x, u):
        return lax.dot_general(x, u, (((1,), (0,)), ((), ())), preferred_element_type=F32).reshape(rows, -1)

    local = product(mine, upstream)
    grads, squares = [], jnp.zeros((8, 128), F32)
    for c in range(chunks):
        grad = part(local, c) + product(theirs, up_other[c])
        grads.append(grad)
        squares = squares + jnp.sum((grad * grad).reshape(rows // 8, 8, COLS // 128, 128), axis=(0, 2))
    grad_other = across(grads[0].astype(BF16))
    total = group_sum(squares)
    total_other = across(total)

    sent, received = [None], [None]
    for c in range(1, chunks):
        sent.append(make(total, grads[c], first, second, c))
        received.append(across(sent[c]))
    outs = first_mix(total, total_other, grads[0], grad_other, first, first_other, second, second_other, old, old_other, 0)
    for c in range(1, chunks):
        outs = mix(sent[c], received[c], old, old_other, c, outs)
    return tuple(out[None] for out in outs)


def solution(mesh):
    placed = P("replica", "dp", "tensor")
    return jax.shard_map(
        body,
        mesh=mesh,
        in_specs=(placed,) * 5,
        out_specs=(placed,) * 3,
        check_vma=False,
    )
```

time: 542 us -> 355 us (0.65)
  waiting for transfers between devices: 445 us -> 201 us
  Pallas kernels: 0 us -> 57.5 us
  starting transfers between devices: 3.3 us -> 47.1 us
  blocking collectives: 37.5 us -> 0 us
  other arithmetic: 21.8 us -> 4.13 us
  local copies, waits for them, and re-layouts: 4.29 us -> 12.7 us
    reduce_scatter x1 -> x0, waiting for transfers between devices: 171 us -> none  [body(): lax.psum_scatter(lax.dot_general(whole, upstream, (((0,), (0,)), ((), ())...]
    pallas_call x0 -> x13, Pallas kernels: none -> 57.5 us  [the longest x6 27 us: mix(): pl.pallas_call(mix_kernel, grid=(rows // step,), out_shape=(shape, shape,...]
    ppermute x1 -> x23, waiting for transfers between devices: 233 us -> 178 us  [the longest x11 122 us: across(): return lax.ppermute(value, 'replica', [(s, s ^ 4) for s in range(8)])]
    ppermute x1 -> x23, starting transfers between devices: 3.23 us -> 47 us  [the longest x11 25.7 us: across(): return lax.ppermute(value, 'replica', [(s, s ^ 4) for s in range(8)])]
    psum x1 -> x0, blocking collectives: 37.5 us -> none  [body(): total = lax.psum(local_sq, ('dp', 'tensor'))]
    all_gather x1, waiting for transfers between devices: 40.1 us -> 22.3 us  [gather_tokens(): return lax.all_gather(moved, 'tensor', axis=0, tiled=False)]
    another operation x2 -> x0, other arithmetic: 12.5 us -> none  [adamw(): jnp.stack([fresh.astype(jnp.bfloat16), moment_one.astype(jnp.bfloat16), m...]
    dot_general x1 -> x8, matrix products: 13.8 us -> 17.3 us  [product(): lax.dot_general(x, u, (((1,), (0,)), ((), ())), preferred_element_type=F32)]
  transfers between devices with their start and end apart: 3 -> 24, of which waited for: 3 -> 15; matrix products, arithmetic and copies ran while one was open for 0% -> 9% of each run, Pallas kernels for 0% -> 15%
where the time goes in v1:
time: 355 us; the launch traced here: 353 us
  waiting for transfers between devices  201 us (57%)
  Pallas kernels  57.5 us (16%)
  starting transfers between devices  47.1 us (13%)
  matrix products  17.3 us (5%)
  between operations  14.2 us (4%)
  local copies, waits for them, and re-layouts  12.7 us (4%)
  other arithmetic  4.13 us (1%)
    ppermute x11, waiting for transfers between devices, across(): return lax.ppermute(value, 'replica', [(s, s ^ 4) for s in range(8)])  122 us
    ppermute x8, waiting for transfers between devices, swap_dp(): return lax.ppermute(value, 'dp', [(0, 1), (1, 0)])  35.8 us
    pallas_call x6, Pallas kernels, mix(): pl.pallas_call(mix_kernel, grid=(rows // step,), out_shape=(shape, shape,...  27 us
    ppermute x11, starting transfers between devices, across(): return lax.ppermute(value, 'replica', [(s, s ^ 4) for s in range(8)])  25.7 us
    pallas_call x6, Pallas kernels, make(): pl.pallas_call(make_kernel, grid=(rows // step,), out_shape=jax.ShapeDtyp...  24.3 us
    all_gather x1, waiting for transfers between devices, gather_tokens(): return lax.all_gather(moved, 'tensor', axis=0, tiled=False)  22.3 us
    dot_general x8, matrix products, product(): lax.dot_general(x, u, (((1,), (0,)), ((), ())), preferred_element_type=F32)  17.3 us
    ppermute x1, waiting for transfers between devices, gather_tokens(): moved = lax.ppermute(mine, ('dp', 'tensor'), pairs)  13.7 us
  transfers between devices with their start and end apart: 24, of which 15 were waited for; matrix products, arithmetic and copies ran while one was open for 9% of the time, Pallas kernels for 15%

profile of v1, /device:TPU:6, one launch (start us, length us, event | category | flops | bytes accessed | tf_op | source)
XLA Modules:
  0.0 353.5 jit_solution(14894696704672356437)
XLA Ops:
  7.2 5.9 %collective-permute-start = (bf16[1024,256]{1,0:T(8,128)(2,1)}, bf16[1024,256]{1,0:T(8,128)(2,1)S(1)}, u32[]{:S(2)}, u32[]{:S(2)}) collective-permute-start(bf16[1024,256]{1,0:T(8,128)(2,1)} %bitcast.100), channel_id=1, source_target_pairs={{0,0},{1,1},{2,2},{3,3},{4,8},{5,9},{6,10},{7,11},{8,4},{9,5},{10,... | collective-permute-start | bytes 1572872 | tf_op jit(solution)/shard_map/ppermute | solution.py:32
  13.2 13.7 %collective-permute-done = bf16[1024,256]{1,0:T(8,128)(2,1)S(1)} collective-permute-done((bf16[1024,256]{1,0:T(8,128)(2,1)}, bf16[1024,256]{1,0:T(8,128)(2,1)S(1)}, u32[]{:S(2)}, u32[]{:S(2)}) %collective-permute-start) | collective-permute-done | bytes 524320 | tf_op jit(solution)/shard_map/ppermute | solution.py:32
  27.7 3.6 %fusion.31 = (bf16[1024,256]{1,0:T(8,128)(2,1)S(1)}, bf16[1024,256]{1,0:T(8,128)(2,1)}, bf16[1024,256]{1,0:T(8,128)(2,1)}, bf16[1024,256]{1,0:T(8,128)(2,1)}, bf...) fusion(bf16[1024,1792]{1,0:T(8,128)(2,1)} %bitcast.90), kind=kLoop, calls=%fused_computation.47 | loop fusion | bytes 7340032 | tf_op jit(solution)/shard_map/slice | solution.py:147
  31.3 3.5 collective-permute-start.7
  34.9 3.5 collective-permute-start.4
  38.4 22.3 %all-gather.3.cloned.1.call-done = bf16[8192,256]{1,0:T(8,128)(2,1)} async-done(((bf16[1024,256]{1,0:T(8,128)(2,1)}), bf16[8192,256]{1,0:T(8,128)(2,1)}) %all-gather.3.cloned.1.call-update) | async-done | bytes 4194320 | tf_op jit(solution)/shard_map/all_gather | solution.py:33
  60.8 1.7 dynamic-slice_bitcast_fusion
  62.5 2.4 copy.27
  64.9 6.8 %fusion.28 = f32[1024,1792]{1,0:T(8,128)S(1)} fusion(bf16[1024,1024]{1,0:T(8,128)(2,1)} %bitcast.91, bf16[1,1024,1792]{2,1,0:T(8,128)(2,1)} %param.6), kind=kOutput, calls=%fused_computation.44 | convolution fusion | flops 3758096384 | bytes 13107200 | tf_op jit(solution)/shard_map/dot_general | solution.py:160
  71.7 19.2 %collective-permute-done.1 = bf16[1024,256]{1,0:T(8,128)(2,1)} collective-permute-done((bf16[1024,256]{1,0:T(8,128)(2,1)}, bf16[1024,256]{1,0:T(8,128)(2,1)}, u32[]{:S(2)}, u32[]{:S(2)}) %collective-permute-start.1) | collective-permute-done | bytes 524320 | tf_op jit(solution)/shard_map/ppermute | solution.py:23
  90.9 3.9 %collective-permute-start.13 = (bf16[1024,1792]{1,0:T(8,128)(2,1)}, bf16[1024,1792]{1,0:T(8,128)(2,1)}, u32[]{:S(2)}, u32[]{:S(2)}) collective-permute-start(bf16[1024,1792]{1,0:T(8,128)(2,1)} %bitcast.28.old_ref), channel_id=1, source_target_pairs={{0,64},{16,80},{32,96},{48,112},{64,0},{80,16},{96,32},{112,48},{1... | collective-permute-start | bytes 11010056 | tf_op jit(solution)/shard_map/ppermute | solution.py:19
  94.8 1.8 fusion.10
  97.4 1.8 fusion
  99.2 3.5 collective-permute-start.2
  102.7 1.8 fusion.12
  104.5 1.8 fusion.2
  106.4 1.8 fusion.4
  108.2 5.3 %collective-permute-done.3 = bf16[1024,256]{1,0:T(8,128)(2,1)S(1)} collective-permute-done((bf16[1024,256]{1,0:T(8,128)(2,1)S(1)}, bf16[1024,256]{1,0:T(8,128)(2,1)S(1)}, u32[]{:S(2)}, u32[]{:S(2)}) %collective-permute-start.3) | collective-permute-done | bytes 524320 | tf_op jit(solution)/shard_map/ppermute | solution.py:23
  114.2 7.2 %collective-permute-done.2 = bf16[1024,256]{1,0:T(8,128)(2,1)S(1)} collective-permute-done((bf16[1024,256]{1,0:T(8,128)(2,1)S(1)}, bf16[1024,256]{1,0:T(8,128)(2,1)S(1)}, u32[]{:S(2)}, u32[]{:S(2)}) %collective-permute-start.2) | collective-permute-done | bytes 524320 | tf_op jit(solution)/shard_map/ppermute | solution.py:23
  122.2 3.1 bitcast_reduce_fusion.5
  128.1 2.0 collective-permute-done.9
  131.8 3.5 collective-permute-done.10
  136.3 4.0 %collective-permute-done.11 = f32[8,128]{1,0:T(8,128)S(1)} collective-permute-done((f32[8,128]{1,0:T(8,128)S(1)}, f32[8,128]{1,0:T(8,128)S(1)}, u32[]{:S(2)}, u32[]{:S(2)}) %collective-permute-start.11) | collective-permute-done | bytes 4128 | tf_op jit(solution)/shard_map/ppermute | solution.py:23
  141.0 4.0 %shard_map.81.mine_ref = bf16[2,1024,256]{2,1,0:T(8,128)(2,1)} custom-call(f32[8,128]{1,0:T(8,128)} %add.75.total_ref, f32[1024,256]{1,0:T(8,128)} %get-tuple-element.48.grad_ref, bf16[1024,1792]{1,0:T(8,128)(2,1)} %bitcast.71, bf16[1024,1792]{1,0:T(8,128)(2,1)} %bitcast.79), custom_call_target="tpu_custom_call" | custom-call | flops 2621440 | bytes 3145728 | tf_op jit(solution)/shard_map/pallas_call | solution.py:75
  146.4 3.3 collective-permute-start.21
  151.1 3.2 collective-permute-start.20
  154.4 54.6 %collective-permute-done.21.first_other_ref = bf16[1024,256]{1,0:T(8,128)(2,1)} collective-permute-done((bf16[1024,256]{1,0:T(8,128)(2,1)S(1)}, bf16[1024,256]{1,0:T(8,128)(2,1)}, u32[]{:S(2)}, u32[]{:S(2)}) %collective-permute-start.21) | collective-permute-done | bytes 524320 | tf_op jit(solution)/shard_map/ppermute | solution.py:19
  209.0 3.5 collective-permute-start.19
  212.6 4.0 %shard_map.80.mine_ref = bf16[2,1024,256]{2,1,0:T(8,128)(2,1)} custom-call(f32[8,128]{1,0:T(8,128)} %add.75.total_ref, f32[1024,256]{1,0:T(8,128)} %get-tuple-element.68.grad_ref, bf16[1024,1792]{1,0:T(8,128)(2,1)} %bitcast.73, bf16[1024,1792]{1,0:T(8,128)(2,1)} %bitcast.81), custom_call_target="tpu_custom_call" | custom-call | flops 2621440 | bytes 3145728 | tf_op jit(solution)/shard_map/pallas_call | solution.py:75
  216.6 3.6 %collective-permute-done.22.second_other_ref = bf16[1024,256]{1,0:T(8,128)(2,1)S(1)} collective-permute-done((bf16[1024,256]{1,0:T(8,128)(2,1)S(1)}, bf16[1024,256]{1,0:T(8,128)(2,1)S(1)}, u32[]{:S(2)}, u32[]{:S(2)}) %collective-permute-start.22) | collective-permute-done | bytes 524320 | tf_op jit(solution)/shard_map/ppermute | solution.py:19
  220.2 3.5 collective-permute-start.17
  223.7 4.1 %shard_map.79.mine_ref = bf16[2,1024,256]{2,1,0:T(8,128)(2,1)} custom-call(f32[8,128]{1,0:T(8,128)} %add.75.total_ref, f32[1024,256]{1,0:T(8,128)} %get-tuple-element.66.grad_ref, bf16[1024,1792]{1,0:T(8,128)(2,1)} %bitcast.74, bf16[1024,1792]{1,0:T(8,128)(2,1)} %bitcast.82), custom_call_target="tpu_custom_call" | custom-call | flops 2621440 | bytes 3145728 | tf_op jit(solution)/shard_map/pallas_call | solution.py:75
  228.1 4.1 %shard_map.78.mine_ref = bf16[2,1024,256]{2,1,0:T(8,128)(2,1)} custom-call(f32[8,128]{1,0:T(8,128)} %add.75.total_ref, f32[1024,256]{1,0:T(8,128)} %get-tuple-element.64.grad_ref, bf16[1024,1792]{1,0:T(8,128)(2,1)} %bitcast.75, bf16[1024,1792]{1,0:T(8,128)(2,1)} %bitcast.83), custom_call_target="tpu_custom_call" | custom-call | flops 2621440 | bytes 3145728 | tf_op jit(solution)/shard_map/pallas_call | solution.py:75
  232.1 3.4 collective-permute-start.15
  235.5 4.1 %shard_map.77.mine_ref = bf16[2,1024,256]{2,1,0:T(8,128)(2,1)} custom-call(f32[8,128]{1,0:T(8,128)} %add.75.total_ref, f32[1024,256]{1,0:T(8,128)} %get-tuple-element.62.grad_ref, bf16[1024,1792]{1,0:T(8,128)(2,1)} %bitcast.76, bf16[1024,1792]{1,0:T(8,128)(2,1)} %bitcast.84), custom_call_target="tpu_custom_call" | custom-call | flops 2621440 | bytes 3145728 | tf_op jit(solution)/shard_map/pallas_call | solution.py:75
  239.9 4.0 %shard_map.76.mine_ref = bf16[2,1024,256]{2,1,0:T(8,128)(2,1)} custom-call(f32[8,128]{1,0:T(8,128)} %add.75.total_ref, f32[1024,256]{1,0:T(8,128)} %get-tuple-element.60.grad_ref, bf16[1024,1792]{1,0:T(8,128)(2,1)} %bitcast.77, bf16[1024,1792]{1,0:T(8,128)(2,1)} %bitcast.85), custom_call_target="tpu_custom_call" | custom-call | flops 2621440 | bytes 3145728 | tf_op jit(solution)/shard_map/pallas_call | solution.py:75
  243.9 3.6 %collective-permute-start.12 = (bf16[2,1024,256]{2,1,0:T(8,128)(2,1)}, bf16[2,1024,256]{2,1,0:T(8,128)(2,1)S(1)}, u32[]{:S(2)}, u32[]{:S(2)}) collective-permute-start(bf16[2,1024,256]{2,1,0:T(8,128)(2,1)} %shard_map.76.mine_ref), channel_id=1, source_target_pairs={{0,64},{16,80},{32,96},{48,112},{64,0},{80,16},{96,32},{112,48},{1... | collective-permute-start | bytes 3145736 | tf_op jit(solution)/shard_map/ppermute | solution.py:19
  247.6 6.3 %shard_map.82 = (bf16[1024,1792]{1,0:T(8,128)(2,1)}, bf16[1024,1792]{1,0:T(8,128)(2,1)}, bf16[1024,1792]{1,0:T(8,128)(2,1)}) custom-call(f32[8,128]{1,0:T(8,128)} %add.75.total_ref, f32[8,128]{1,0:T(8,128)} %copy-done.8, f32[1024,256]{1,0:T(8,128)} %copy-done, bf16[1024,256]{1,0:T(8,128)(2,1)} %collective-permute-done.20.grad_other_ref, ...), custom_call_target="tpu_custom_call" | custom-call | flops 15728640 | bytes 5767168 | tf_op jit(solution)/shard_map/pallas_call | solution.py:132
  253.8 4.5 %shard_map.83 = (bf16[1024,1792]{1,0:T(8,128)(2,1)}, bf16[1024,1792]{1,0:T(8,128)(2,1)}, bf16[1024,1792]{1,0:T(8,128)(2,1)}) custom-call(bf16[2,1024,256]{2,1,0:T(8,128)(2,1)} %shard_map.81.mine_ref, bf16[2,1024,256]{2,1,0:T(8,128)(2,1)} %copy-done.1, ...), custom_call_target="tpu_custom_call", output_to_operand_aliasing={{0}: (4, {}), {1}: (5, {}), {2}: (6, {})} | custom-call | flops 10485760 | bytes 4718592 | tf_op jit(solution)/shard_map/pallas_call | solution.py:105
  258.3 4.5 %shard_map.84 = (bf16[1024,1792]{1,0:T(8,128)(2,1)}, bf16[1024,1792]{1,0:T(8,128)(2,1)}, bf16[1024,1792]{1,0:T(8,128)(2,1)}) custom-call(bf16[2,1024,256]{2,1,0:T(8,128)(2,1)} %shard_map.80.mine_ref, bf16[2,1024,256]{2,1,0:T(8,128)(2,1)} %collective-permute-done.17.other_ref, ...), custom_call_target="tpu_custom_call", output_to_operand_aliasing={{0}: (4, {}), {1}: (5, {}), {2}: (6, {})} | custom-call | flops 10485760 | bytes 4718592 | tf_op jit(solution)/shard_map/pallas_call | solution.py:105
  262.8 13.7 %collective-permute-done.16.other_ref = bf16[2,1024,256]{2,1,0:T(8,128)(2,1)} collective-permute-done((bf16[2,1024,256]{2,1,0:T(8,128)(2,1)}, bf16[2,1024,256]{2,1,0:T(8,128)(2,1)}, u32[]{:S(2)}, u32[]{:S(2)}) %collective-permute-start.16) | collective-permute-done | bytes 1048608 | tf_op jit(solution)/shard_map/ppermute | solution.py:19
  276.5 4.5 %shard_map.85 = (bf16[1024,1792]{1,0:T(8,128)(2,1)}, bf16[1024,1792]{1,0:T(8,128)(2,1)}, bf16[1024,1792]{1,0:T(8,128)(2,1)}) custom-call(bf16[2,1024,256]{2,1,0:T(8,128)(2,1)} %shard_map.79.mine_ref, bf16[2,1024,256]{2,1,0:T(8,128)(2,1)} %collective-permute-done.16.other_ref, ...), custom_call_target="tpu_custom_call", output_to_operand_aliasing={{0}: (4, {}), {1}: (5, {}), {2}: (6, {})} | custom-call | flops 10485760 | bytes 4718592 | tf_op jit(solution)/shard_map/pallas_call | solution.py:105
  281.0 18.0 %collective-permute-done.15.other_ref = bf16[2,1024,256]{2,1,0:T(8,128)(2,1)} collective-permute-done((bf16[2,1024,256]{2,1,0:T(8,128)(2,1)}, bf16[2,1024,256]{2,1,0:T(8,128)(2,1)}, u32[]{:S(2)}, u32[]{:S(2)}) %collective-permute-start.15) | collective-permute-done | bytes 1048608 | tf_op jit(solution)/shard_map/ppermute | solution.py:19
  299.0 4.5 %shard_map.86 = (bf16[1024,1792]{1,0:T(8,128)(2,1)}, bf16[1024,1792]{1,0:T(8,128)(2,1)}, bf16[1024,1792]{1,0:T(8,128)(2,1)}) custom-call(bf16[2,1024,256]{2,1,0:T(8,128)(2,1)} %shard_map.78.mine_ref, bf16[2,1024,256]{2,1,0:T(8,128)(2,1)} %collective-permute-done.15.other_ref, ...), custom_call_target="tpu_custom_call", output_to_operand_aliasing={{0}: (4, {}), {1}: (5, {}), {2}: (6, {})} | custom-call | flops 10485760 | bytes 4718592 | tf_op jit(solution)/shard_map/pallas_call | solution.py:105
  303.5 17.9 %collective-permute-done.14.other_ref = bf16[2,1024,256]{2,1,0:T(8,128)(2,1)S(1)} collective-permute-done((bf16[2,1024,256]{2,1,0:T(8,128)(2,1)}, bf16[2,1024,256]{2,1,0:T(8,128)(2,1)S(1)}, u32[]{:S(2)}, u32[]{:S(2)}) %collective-permute-start.14) | collective-permute-done | bytes 1048608 | tf_op jit(solution)/shard_map/ppermute | solution.py:19
  322.4 4.5 %shard_map.87 = (bf16[1024,1792]{1,0:T(8,128)(2,1)}, bf16[1024,1792]{1,0:T(8,128)(2,1)}, bf16[1024,1792]{1,0:T(8,128)(2,1)}) custom-call(bf16[2,1024,256]{2,1,0:T(8,128)(2,1)} %shard_map.77.mine_ref, bf16[2,1024,256]{2,1,0:T(8,128)(2,1)} %copy-done.3, ...), custom_call_target="tpu_custom_call", output_to_operand_aliasing={{0}: (4, {}), {1}: (5, {}), {2}: (6, {})} | custom-call | flops 10485760 | bytes 4718592 | tf_op jit(solution)/shard_map/pallas_call | solution.py:105
  326.9 14.3 %collective-permute-done.12.other_ref = bf16[2,1024,256]{2,1,0:T(8,128)(2,1)S(1)} collective-permute-done((bf16[2,1024,256]{2,1,0:T(8,128)(2,1)}, bf16[2,1024,256]{2,1,0:T(8,128)(2,1)S(1)}, u32[]{:S(2)}, u32[]{:S(2)}) %collective-permute-start.12) | collective-permute-done | bytes 1048608 | tf_op jit(solution)/shard_map/ppermute | solution.py:19
  342.1 4.5 %shard_map.88 = (bf16[1024,1792]{1,0:T(8,128)(2,1)}, bf16[1024,1792]{1,0:T(8,128)(2,1)}, bf16[1024,1792]{1,0:T(8,128)(2,1)}) custom-call(bf16[2,1024,256]{2,1,0:T(8,128)(2,1)} %shard_map.76.mine_ref, bf16[2,1024,256]{2,1,0:T(8,128)(2,1)} %copy-done.2, ...), custom_call_target="tpu_custom_call", output_to_operand_aliasing={{0}: (4, {}), {1}: (5, {}), {2}: (6, {})} | custom-call | flops 10485760 | bytes 4718592 | tf_op jit(solution)/shard_map/pallas_call | solution.py:105
  (53 shorter events, 14.8 us)
Async XLA Ops:
  7.2 53.6 %all-gather.3.cloned.1.call-start = ((), (), s32[]{:S(2)}) async-start(), calls=%async_computation | async-start | bytes 4718592 | tf_op jit(solution)/shard_map/all_gather | solution.py:33
  7.2 19.7 %collective-permute-start = (bf16[1024,256]{1,0:T(8,128)(2,1)}, bf16[1024,256]{1,0:T(8,128)(2,1)S(1)}, u32[]{:S(2)}, u32[]{:S(2)}) collective-permute-start(bf16[1024,256]{1,0:T(8,128)(2,1)} %bitcast.100), channel_id=1, source_target_pairs={{0,0},{1,1},{2,2},{3,3},{4,8},{5,9},{6,10},{7,11},{8,4},{9,5},{10,... | collective-permute-start | bytes 1572872 | tf_op jit(solution)/shard_map/ppermute | solution.py:32
  26.9 0.8 copy-start.6
  31.3 65.7 %collective-permute-start.6 = (bf16[1024,256]{1,0:T(8,128)(2,1)}, bf16[1024,256]{1,0:T(8,128)(2,1)}, u32[]{:S(2)}, u32[]{:S(2)}) collective-permute-start(bf16[1024,256]{1,0:T(8,128)(2,1)} %get-tuple-element.70), channel_id=1, source_target_pairs={{0,8},{8,0},{1,9},{9,1},{2,10},{10,2},{3,11},{11,3},{4,12},{12,4},... | collective-permute-start | bytes 1572872 | tf_op jit(solution)/shard_map/ppermute | solution.py:23
  31.3 67.9 %collective-permute-start.7 = (bf16[1024,256]{1,0:T(8,128)(2,1)}, bf16[1024,256]{1,0:T(8,128)(2,1)}, u32[]{:S(2)}, u32[]{:S(2)}) collective-permute-start(bf16[1024,256]{1,0:T(8,128)(2,1)} %get-tuple-element.75), channel_id=1, source_target_pairs={{0,8},{8,0},{1,9},{9,1},{2,10},{10,2},{3,11},{11,3},{4,12},{12,4},... | collective-permute-start | bytes 1572872 | tf_op jit(solution)/shard_map/ppermute | solution.py:23
  34.9 69.7 %collective-permute-start.5 = (bf16[1024,256]{1,0:T(8,128)(2,1)}, bf16[1024,256]{1,0:T(8,128)(2,1)}, u32[]{:S(2)}, u32[]{:S(2)}) collective-permute-start(bf16[1024,256]{1,0:T(8,128)(2,1)} %get-tuple-element.71), channel_id=1, source_target_pairs={{0,8},{8,0},{1,9},{9,1},{2,10},{10,2},{3,11},{11,3},{4,12},{12,4},... | collective-permute-start | bytes 1572872 | tf_op jit(solution)/shard_map/ppermute | solution.py:23
  34.9 71.4 %collective-permute-start.4 = (bf16[1024,256]{1,0:T(8,128)(2,1)}, bf16[1024,256]{1,0:T(8,128)(2,1)}, u32[]{:S(2)}, u32[]{:S(2)}) collective-permute-start(bf16[1024,256]{1,0:T(8,128)(2,1)} %get-tuple-element.72), channel_id=1, source_target_pairs={{0,8},{8,0},{1,9},{9,1},{2,10},{10,2},{3,11},{11,3},{4,12},{12,4},... | collective-permute-start | bytes 1572872 | tf_op jit(solution)/shard_map/ppermute | solution.py:23
  38.4 52.5 %collective-permute-start.1 = (bf16[1024,256]{1,0:T(8,128)(2,1)}, bf16[1024,256]{1,0:T(8,128)(2,1)}, u32[]{:S(2)}, u32[]{:S(2)}) collective-permute-start(bf16[1024,256]{1,0:T(8,128)(2,1)} %get-tuple-element.74), channel_id=1, source_target_pairs={{0,8},{8,0},{1,9},{9,1},{2,10},{10,2},{3,11},{11,3},{4,12},{12,4},... | collective-permute-start | bytes 1572872 | tf_op jit(solution)/shard_map/ppermute | solution.py:23
  64.9 29.9 %copy-start.4 = (bf16[8192,256]{1,0:T(8,128)(2,1)S(1)}, bf16[8192,256]{1,0:T(8,128)(2,1)}, u32[]{:S(2)}) copy-start(bf16[8192,256]{1,0:T(8,128)(2,1)} %all-gather.3.cloned.1.call-done) | copy-start | bytes 12582916
  90.9 136.9 %collective-permute-start.13 = (bf16[1024,1792]{1,0:T(8,128)(2,1)}, bf16[1024,1792]{1,0:T(8,128)(2,1)}, u32[]{:S(2)}, u32[]{:S(2)}) collective-permute-start(bf16[1024,1792]{1,0:T(8,128)(2,1)} %bitcast.28.old_ref), channel_id=1, source_target_pairs={{0,64},{16,80},{32,96},{48,112},{64,0},{80,16},{96,32},{112,48},{1... | collective-permute-start | bytes 11010056 | tf_op jit(solution)/shard_map/ppermute | solution.py:19
  96.7 7.8 %copy-start = (f32[1024,256]{1,0:T(8,128)}, f32[1024,256]{1,0:T(8,128)S(1)}, u32[]{:S(2)}) copy-start(f32[1024,256]{1,0:T(8,128)S(1)} %get-tuple-element.46.grad_ref) | copy-start | bytes 3145732
  97.0 16.4 %collective-permute-start.3 = (bf16[1024,256]{1,0:T(8,128)(2,1)S(1)}, bf16[1024,256]{1,0:T(8,128)(2,1)S(1)}, u32[]{:S(2)}, u32[]{:S(2)}) collective-permute-start(bf16[1024,256]{1,0:T(8,128)(2,1)S(1)} %get-tuple-element.73), channel_id=1, source_target_pairs={{0,8},{8,0},{1,9},{9,1},{2,10},{10,2},{3,11},{11,3},{4,12},{12,4},... | collective-permute-start | bytes 1572872 | tf_op jit(solution)/shard_map/ppermute | solution.py:23
  99.2 22.2 %collective-permute-start.2 = (bf16[1024,256]{1,0:T(8,128)(2,1)S(1)}, bf16[1024,256]{1,0:T(8,128)(2,1)S(1)}, u32[]{:S(2)}, u32[]{:S(2)}) collective-permute-start(bf16[1024,256]{1,0:T(8,128)(2,1)S(1)} %get-tuple-element.69), channel_id=1, source_target_pairs={{0,8},{8,0},{1,9},{9,1},{2,10},{10,2},{3,11},{11,3},{4,12},{12,4},... | collective-permute-start | bytes 1572872 | tf_op jit(solution)/shard_map/ppermute | solution.py:23
  125.3 1.2 collective-permute-start.8
  126.5 3.6 %collective-permute-start.9 = (f32[8,128]{1,0:T(8,128)S(1)}, f32[8,128]{1,0:T(8,128)S(1)}, u32[]{:S(2)}, u32[]{:S(2)}) collective-permute-start(f32[8,128]{1,0:T(8,128)S(1)} %add.72), channel_id=1, source_target_pairs={{0,2},{1,3},{2,0},{3,1},{4,6},{5,7},{6,4},{7,5},{8,10},{9,11},{10,... | collective-permute-start | bytes 12296 | tf_op jit(solution)/shard_map/ppermute | solution.py:38
  130.2 5.1 %collective-permute-start.10 = (f32[8,128]{1,0:T(8,128)S(1)}, f32[8,128]{1,0:T(8,128)S(1)}, u32[]{:S(2)}, u32[]{:S(2)}) collective-permute-start(f32[8,128]{1,0:T(8,128)S(1)} %add.73), channel_id=1, source_target_pairs={{0,4},{1,5},{2,6},{3,7},{4,0},{5,1},{6,2},{7,3},{8,12},{9,13},{10,... | collective-permute-start | bytes 12296 | tf_op jit(solution)/shard_map/ppermute | solution.py:38
  135.3 5.1 %collective-permute-start.11 = (f32[8,128]{1,0:T(8,128)S(1)}, f32[8,128]{1,0:T(8,128)S(1)}, u32[]{:S(2)}, u32[]{:S(2)}) collective-permute-start(f32[8,128]{1,0:T(8,128)S(1)} %add.74), channel_id=1, source_target_pairs={{0,8},{8,0},{1,9},{9,1},{2,10},{10,2},{3,11},{11,3},{4,12},{12,4},... | collective-permute-start | bytes 12296 | tf_op jit(solution)/shard_map/ppermute | solution.py:23
  141.0 68.1 %copy-start.7 = (f32[8,128]{1,0:T(8,128)S(1)}, f32[8,128]{1,0:T(8,128)}, u32[]{:S(2)}) copy-start(f32[8,128]{1,0:T(8,128)} %add.75.total_ref) | copy-start | bytes 12292
  145.0 98.9 %collective-permute-start.18 = (bf16[2,1024,256]{2,1,0:T(8,128)(2,1)}, bf16[2,1024,256]{2,1,0:T(8,128)(2,1)S(1)}, u32[]{:S(2)}, u32[]{:S(2)}) collective-permute-start(bf16[2,1024,256]{2,1,0:T(8,128)(2,1)} %shard_map.81.mine_ref), channel_id=1, source_target_pairs={{0,64},{16,80},{32,96},{48,112},{64,0},{80,16},{96,32},{112,48},{1... | collective-permute-start | bytes 3145736 | tf_op jit(solution)/shard_map/ppermute | solution.py:19
  146.4 62.7 %collective-permute-start.21 = (bf16[1024,256]{1,0:T(8,128)(2,1)S(1)}, bf16[1024,256]{1,0:T(8,128)(2,1)}, u32[]{:S(2)}, u32[]{:S(2)}) collective-permute-start(bf16[1024,256]{1,0:T(8,128)(2,1)S(1)} %slice.78), channel_id=1, source_target_pairs={{0,64},{16,80},{32,96},{48,112},{64,0},{80,16},{96,32},{112,48},{1... | collective-permute-start | bytes 1572872 | tf_op jit(solution)/shard_map/ppermute | solution.py:19
  150.8 69.4 %collective-permute-start.22 = (bf16[1024,256]{1,0:T(8,128)(2,1)S(1)}, bf16[1024,256]{1,0:T(8,128)(2,1)S(1)}, u32[]{:S(2)}, u32[]{:S(2)}) collective-permute-start(bf16[1024,256]{1,0:T(8,128)(2,1)S(1)} %slice.79), channel_id=1, source_target_pairs={{0,64},{16,80},{32,96},{48,112},{64,0},{80,16},{96,32},{112,48},{1... | collective-permute-start | bytes 1572872 | tf_op jit(solution)/shard_map/ppermute | solution.py:19
  151.1 88.5 %collective-permute-start.20 = (bf16[1024,256]{1,0:T(8,128)(2,1)S(1)}, bf16[1024,256]{1,0:T(8,128)(2,1)}, u32[]{:S(2)}, u32[]{:S(2)}) collective-permute-start(bf16[1024,256]{1,0:T(8,128)(2,1)S(1)} %get-tuple-element.45), channel_id=1, source_target_pairs={{0,64},{16,80},{32,96},{48,112},{64,0},{80,16},{96,32},{112,48},{1... | collective-permute-start | bytes 1572872 | tf_op jit(solution)/shard_map/ppermute | solution.py:19
  209.0 23.1 %collective-permute-start.19 = (f32[8,128]{1,0:T(8,128)S(1)}, f32[8,128]{1,0:T(8,128)S(1)}, u32[]{:S(2)}, u32[]{:S(2)}) collective-permute-start(f32[8,128]{1,0:T(8,128)S(1)} %copy-done.7), channel_id=1, source_target_pairs={{0,64},{16,80},{32,96},{48,112},{64,0},{80,16},{96,32},{112,48},{1... | collective-permute-start | bytes 12296 | tf_op jit(solution)/shard_map/ppermute | solution.py:19
  220.2 7.6 %copy-start.5 = (bf16[1024,256]{1,0:T(8,128)(2,1)}, bf16[1024,256]{1,0:T(8,128)(2,1)S(1)}, u32[]{:S(2)}) copy-start(bf16[1024,256]{1,0:T(8,128)(2,1)S(1)} %collective-permute-done.22.second_other_ref) | copy-start | bytes 1572868
  220.2 38.2 %collective-permute-start.17 = (bf16[2,1024,256]{2,1,0:T(8,128)(2,1)}, bf16[2,1024,256]{2,1,0:T(8,128)(2,1)}, u32[]{:S(2)}, u32[]{:S(2)}) collective-permute-start(bf16[2,1024,256]{2,1,0:T(8,128)(2,1)} %shard_map.80.mine_ref), channel_id=1, source_target_pairs={{0,64},{16,80},{32,96},{48,112},{64,0},{80,16},{96,32},{112,48},{1... | collective-permute-start | bytes 3145736 | tf_op jit(solution)/shard_map/ppermute | solution.py:19
  227.8 48.8 %collective-permute-start.16 = (bf16[2,1024,256]{2,1,0:T(8,128)(2,1)}, bf16[2,1024,256]{2,1,0:T(8,128)(2,1)}, u32[]{:S(2)}, u32[]{:S(2)}) collective-permute-start(bf16[2,1024,256]{2,1,0:T(8,128)(2,1)} %shard_map.79.mine_ref), channel_id=1, source_target_pairs={{0,64},{16,80},{32,96},{48,112},{64,0},{80,16},{96,32},{112,48},{1... | collective-permute-start | bytes 3145736 | tf_op jit(solution)/shard_map/ppermute | solution.py:19
  232.1 7.5 %copy-start.8 = (f32[8,128]{1,0:T(8,128)}, f32[8,128]{1,0:T(8,128)S(1)}, u32[]{:S(2)}) copy-start(f32[8,128]{1,0:T(8,128)S(1)} %collective-permute-done.19.total_other_ref) | copy-start | bytes 12292
  232.1 66.9 %collective-permute-start.15 = (bf16[2,1024,256]{2,1,0:T(8,128)(2,1)}, bf16[2,1024,256]{2,1,0:T(8,128)(2,1)}, u32[]{:S(2)}, u32[]{:S(2)}) collective-permute-start(bf16[2,1024,256]{2,1,0:T(8,128)(2,1)} %shard_map.78.mine_ref), channel_id=1, source_target_pairs={{0,64},{16,80},{32,96},{48,112},{64,0},{80,16},{96,32},{112,48},{1... | collective-permute-start | bytes 3145736 | tf_op jit(solution)/shard_map/ppermute | solution.py:19
  239.6 81.8 %collective-permute-start.14 = (bf16[2,1024,256]{2,1,0:T(8,128)(2,1)}, bf16[2,1024,256]{2,1,0:T(8,128)(2,1)S(1)}, u32[]{:S(2)}, u32[]{:S(2)}) collective-permute-start(bf16[2,1024,256]{2,1,0:T(8,128)(2,1)} %shard_map.77.mine_ref), channel_id=1, source_target_pairs={{0,64},{16,80},{32,96},{48,112},{64,0},{80,16},{96,32},{112,48},{1... | collective-permute-start | bytes 3145736 | tf_op jit(solution)/shard_map/ppermute | solution.py:19
  243.9 9.9 %copy-start.1 = (bf16[2,1024,256]{2,1,0:T(8,128)(2,1)}, bf16[2,1024,256]{2,1,0:T(8,128)(2,1)S(1)}, u32[]{:S(2)}) copy-start(bf16[2,1024,256]{2,1,0:T(8,128)(2,1)S(1)} %collective-permute-done.18.other_ref) | copy-start | bytes 3145732
  243.9 97.2 %collective-permute-start.12 = (bf16[2,1024,256]{2,1,0:T(8,128)(2,1)}, bf16[2,1024,256]{2,1,0:T(8,128)(2,1)S(1)}, u32[]{:S(2)}, u32[]{:S(2)}) collective-permute-start(bf16[2,1024,256]{2,1,0:T(8,128)(2,1)} %shard_map.76.mine_ref), channel_id=1, source_target_pairs={{0,64},{16,80},{32,96},{48,112},{64,0},{80,16},{96,32},{112,48},{1... | collective-permute-start | bytes 3145736 | tf_op jit(solution)/shard_map/ppermute | solution.py:19
  321.4 1.0 copy-start.3
  341.1 1.0 copy-start.2
Sparse Core Ops, SparseCore 0:
  27.8 32.8 all-gather.2

commit v2 on v1

v2 whole, which is shorter than its diff:
```python
import jax
import jax.numpy as jnp
from jax import lax
from jax.experimental import pallas as pl
from jax.experimental.pallas import tpu as pltpu
from jax.sharding import PartitionSpec as P

D = 2048
FF = 14336
STEP = 1
FIX_ONE = 1.0 - 0.9**STEP
FIX_TWO = 1.0 - 0.95**STEP
BF16 = jnp.bfloat16
ANYWHERE = pl.BlockSpec(memory_space=pl.ANY)
F32 = jnp.float32


def across(value):
    return lax.ppermute(value, "replica", [(s, s ^ 4) for s in range(8)])


def swap_dp(value):
    return lax.ppermute(value, "dp", [(0, 1), (1, 0)])


def nothing_kernel(*refs):
    del refs


def corner(value):
    return pl.BlockSpec((1,) * (value.ndim - 2) + (16 if value.dtype == BF16 else 8, 128), lambda i: (0,) * value.ndim)


def gate(values, earlier):
    return pl.pallas_call(
        nothing_kernel,
        grid=(1,),
        out_shape=[jax.ShapeDtypeStruct(value.shape, value.dtype) for value in values],
        in_specs=[ANYWHERE] * len(values) + [corner(value) for value in earlier],
        out_specs=[ANYWHERE] * len(values),
        input_output_aliases={i: i for i in range(len(values))},
        cost_estimate=pl.CostEstimate(flops=0, bytes_accessed=4096, transcendentals=0),
    )(*values, *earlier)


def turned(value, bits):
    return lax.ppermute(value, "tensor", [(t, t ^ bits) for t in range(8)])


def settle(mine):
    pairs = []
    for d in range(2):
        for t in range(8):
            stays = t // 4 == d
            pairs.append((d * 8 + t, d * 8 + t if stays else (1 - d) * 8 + (t ^ 4)))
    return lax.ppermute(mine, ("dp", "tensor"), pairs)


def along_y(value):
    copies = jnp.broadcast_to(value, (4, *value.shape))
    return lax.all_to_all(copies, "tensor", 0, 0, tiled=True, axis_index_groups=[[0, 2, 4, 6], [1, 3, 5, 7]])


def assemble_kernel(slot_ref, near_ref, far_ref, out_ref):
    for k in range(4):
        out_ref[slot_ref[k]] = near_ref[k]
        out_ref[slot_ref[4 + k]] = far_ref[k]


def assemble(near, far):
    core = lax.axis_index("tensor") % 2
    flip = 4 * lax.axis_index("dp")
    slots = jnp.stack([(2 * y + core) ^ flip for y in range(4)] + [(2 * y + 1 - core) ^ flip for y in range(4)])
    whole = pl.BlockSpec(memory_space=pltpu.VMEM)
    return pl.pallas_call(
        assemble_kernel,
        out_shape=jax.ShapeDtypeStruct((8, *near.shape[1:]), BF16),
        in_specs=[pl.BlockSpec(memory_space=pltpu.SMEM), whole, whole],
        out_specs=whole,
        cost_estimate=pl.CostEstimate(flops=0, bytes_accessed=8 * near.size, transcendentals=0),
        compiler_params=pltpu.CompilerParams(vmem_limit_bytes=24 * 2**20),
    )(slots.astype(jnp.int32), near, far)


def group_sum(value):
    for bits in (1, 2, 4):
        value = value + turned(value, bits)
    return value + swap_dp(value)


def clip_of(total_ref):
    total = jnp.sum(total_ref[...], keepdims=True)
    return jnp.minimum(1.0, 1.0 / jnp.sqrt(total / (D * FF) + 1e-06))


def moments(scaled, first, second):
    one = 0.9 * first.astype(F32) + 0.1 * scaled
    two = 0.95 * second.astype(F32) + 0.05 * scaled * scaled
    return one.astype(BF16), two.astype(BF16)


def stepped(old, one, two):
    old = old.astype(F32)
    update = (one.astype(F32) * (1.0 / FIX_ONE)) / (jnp.sqrt(two.astype(F32) * (1.0 / FIX_TWO)) + 1e-08)
    return (old - 0.05 * (update + 0.1 * old)).astype(BF16)


def mean(a, b):
    return (0.5 * (a.astype(F32) + b.astype(F32))).astype(BF16)


def make_kernel(total_ref, grad_ref, first_ref, second_ref, old_ref, pair_ref, step_ref):
    one, two = moments(clip_of(total_ref) * grad_ref[...], first_ref[...], second_ref[...])
    pair_ref[0] = one
    pair_ref[1] = two
    step_ref[...] = stepped(old_ref[...], one, two)


def mix_kernel(pair_ref, step_ref, pair_other_ref, old_other_ref, *rest):
    w_ref, one_ref, two_ref, flag_ref = rest[-4:]
    flag_ref[...] = jnp.zeros_like(flag_ref)
    one_other, two_other = pair_other_ref[0], pair_other_ref[1]
    w_ref[...] = mean(step_ref[...], stepped(old_other_ref[...], one_other, two_other))
    one_ref[...] = mean(pair_ref[0], one_other)
    two_ref[...] = mean(pair_ref[1], two_other)


def early_kernel(
    total_ref,
    grad_ref,
    scaled_other_ref,
    first_ref,
    second_ref,
    first_other_ref,
    second_other_ref,
    old_ref,
    old_other_ref,
    *rest,
):
    w_ref, one_ref, two_ref = rest[-3:]
    one, two = moments(clip_of(total_ref) * grad_ref[...], first_ref[...], second_ref[...])
    scaled_other = scaled_other_ref[...].astype(F32)
    one_other, two_other = moments(scaled_other, first_other_ref[...], second_other_ref[...])
    w_ref[...] = mean(stepped(old_ref[...], one, two), stepped(old_other_ref[...], one_other, two_other))
    one_ref[...] = mean(one, one_other)
    two_ref[...] = mean(two, two_other)


STEP_ROWS = 512
TOTAL = pl.BlockSpec((8, 128), lambda i: (0, 0))


def columns(width, at=0):
    return pl.BlockSpec((STEP_ROWS, width), lambda i: (i, at // width))


def pair_of(width):
    return pl.BlockSpec((2, STEP_ROWS, width), lambda i: (0, i, 0))


def cost(rows, width, flops, size):
    return pl.CostEstimate(flops=flops * rows * width, bytes_accessed=size * rows * width, transcendentals=0)


def make(total, grad, within, first, second, old, at, width):
    rows = grad.shape[0]
    wide = columns(width, at)
    return pl.pallas_call(
        make_kernel,
        grid=(rows // STEP_ROWS,),
        out_shape=(jax.ShapeDtypeStruct((2, rows, width), BF16), jax.ShapeDtypeStruct((rows, width), BF16)),
        in_specs=[TOTAL, columns(width, within), wide, wide, wide],
        out_specs=(pair_of(width), columns(width)),
        cost_estimate=cost(rows, width, 30, 16),
    )(total, grad, first, second, old)


def mix(pair, step, pair_other, old_other, at, within, width, shape, outs):
    rows = shape[0]
    wide = columns(width, at)
    whole = jax.ShapeDtypeStruct(shape, BF16)
    return pl.pallas_call(
        mix_kernel,
        grid=(rows // STEP_ROWS,),
        out_shape=(whole, whole, whole, jax.ShapeDtypeStruct((8, 128), F32)),
        in_specs=[pair_of(width), columns(width), pair_of(width), columns(width, within)] + [ANYWHERE] * len(outs),
        out_specs=(wide, wide, wide, TOTAL),
        input_output_aliases={4 + i: i for i in range(len(outs))},
        cost_estimate=cost(rows, width, 30, 18),
    )(pair, step, pair_other, old_other, *outs)


def early(total, grad, scaled_other, first, second, other, old, old_other, width, outs):
    rows, cols = old.shape
    wide = columns(width)
    shape = jax.ShapeDtypeStruct((rows, cols), BF16)
    return pl.pallas_call(
        early_kernel,
        grid=(rows // STEP_ROWS,),
        out_shape=(shape, shape, shape),
        in_specs=[TOTAL] + [wide] * 5 + [columns(width, width), wide, wide] + [ANYWHERE] * 3,
        out_specs=(wide, wide, wide),
        input_output_aliases={9 + i: i for i in range(3)},
        cost_estimate=cost(rows, width, 60, 22),
    )(total, grad, scaled_other, first, second, other, other, old, old_other, *outs)


def scale_kernel(total_ref, grad_ref, out_ref):
    out_ref[...] = (clip_of(total_ref) * grad_ref[...]).astype(BF16)


def scale(total, grad, width):
    rows = grad.shape[0]
    return pl.pallas_call(
        scale_kernel,
        grid=(rows // STEP_ROWS,),
        out_shape=jax.ShapeDtypeStruct((rows, width), BF16),
        in_specs=[TOTAL, columns(width)],
        out_specs=columns(width),
        cost_estimate=cost(rows, width, 2, 6),
    )(total, grad)


def finish_kernel(x_ref, u_ref, local_ref, grad_ref, squares_ref):
    grad = local_ref[...] + jnp.dot(x_ref[0], u_ref[...], preferred_element_type=F32)
    grad_ref[...] = grad
    width = grad.shape[1]
    square = grad * grad
    lanes = sum(square[:, k : k + 128] for k in range(0, width, 128))

    @pl.when(pl.program_id(0) == 0)
    def _():
        squares_ref[...] = jnp.zeros_like(squares_ref)

    squares_ref[...] += jnp.sum(lanes.reshape(-1, 8, 128), axis=0)


def finish(x, u, local, piece):
    blocks, step, depth = x.shape
    at, width = piece
    return pl.pallas_call(
        finish_kernel,
        grid=(blocks,),
        out_shape=(jax.ShapeDtypeStruct((blocks * step, width), F32), jax.ShapeDtypeStruct((8, 128), F32)),
        in_specs=[
            pl.BlockSpec((1, step, depth), lambda i: (i, 0, 0)),
            pl.BlockSpec((depth, width), lambda i: (0, 0)),
            pl.BlockSpec((step, width), lambda i: (i, at // width)),
        ],
        out_specs=(pl.BlockSpec((step, width), lambda i: (i, 0)), pl.BlockSpec((8, 128), lambda i: (0, 0))),
        cost_estimate=pl.CostEstimate(flops=2 * blocks * step * depth * width, bytes_accessed=10 * blocks * step * width, transcendentals=0),
        compiler_params=pltpu.CompilerParams(vmem_limit_bytes=32 * 2**20),
    )(x, u, local)


EARLY = 256
UP = ((1536, 256), (0, 1024), (1024, 512))
OLD = ((0, 1280), (1280, 512))
LATE = ((256, 256), (512, 256), (768, 256), (1024, 256), (1280, 256), (1536, 128), (1664, 128))


def part(value, piece):
    return value[:, piece[0] : piece[0] + piece[1]]


def holder(pieces, at):
    index = next(i for i, (start, width) in enumerate(pieces) if start <= at < start + width)
    return index, at - pieces[index][0]


def body(tokens, grad_out, weights, first_moment, second_moment):
    upstream, old = grad_out[0], weights[0]
    first, second = first_moment[0], second_moment[0]
    rows = old.shape[0]

    settled = settle(tokens[0])
    up_other = [swap_dp(part(upstream, piece)) for piece in UP[:2]]
    old_other = [across(part(old, OLD[0]))]

    (settled,) = gate((settled,), (up_other[0],))
    near = along_y(settled)
    last = jnp.concatenate([first[:, :EARLY], second[:, :EARLY], part(old, OLD[1])], axis=1)
    near, up_last, last = gate((near, part(upstream, UP[2]), last), (up_other[1], old_other[0]))
    far = turned(near, 1)
    up_other.append(swap_dp(up_last))
    old_other.append(across(last))

    features = assemble(near, far)
    local = lax.dot_general(features[:4], upstream, (((1,), (0,)), ((), ())), preferred_element_type=F32).reshape(rows, -1)
    turned_features = jnp.swapaxes(features[4:], 1, 2)
    grads, squares = [], jnp.zeros((8, 128), F32)
    for piece, other in zip(UP, up_other):
        grad, square = finish(turned_features, other, local, piece)
        grads.append(grad)
        squares = squares + square
    total = group_sum(squares)

    scaled = scale(total, grads[1], EARLY)
    scaled_other = across(scaled)
    pairs, steps, received, flags = [], [], [scaled_other], []
    outs = ()
    for i in range(len(LATE) + 3):
        if i < len(LATE):
            at, width = LATE[i]
            chunk, within = holder(UP, at)
            pair, step = make(total, grads[chunk], within, first, second, old, at, width)
            (pair,) = gate((pair,), (received[i - 2] if i >= 2 else old_other[1],) + ((flags[i - 4],) if i >= 4 else ()))
            pairs.append(pair)
            steps.append(step)
            received.append(across(pair))
        if i >= 3:
            j = i - 3
            at, width = LATE[j]
            chunk, within = holder(OLD, at)
            within += 2 * EARLY * chunk
            *outs, flag = mix(pairs[j], steps[j], received[j + 1], old_other[chunk], at, within, width, old.shape, outs)
            flags.append(flag)
        if i == 3:
            outs = early(total, grads[1], scaled_other, first, second, old_other[1], old, old_other[0], EARLY, outs)
    return tuple(out[None] for out in outs)


def solution(mesh):
    placed = P("replica", "dp", "tensor")
    return jax.shard_map(
        body,
        mesh=mesh,
        in_specs=(placed,) * 5,
        out_specs=(placed,) * 3,
        check_vma=False,
    )
```

time: 355 us -> 293 us (0.83)
  waiting for transfers between devices: 201 us -> 132 us
  local copies, waits for them, and re-layouts: 12.7 us -> 34.6 us
  between operations: 14.2 us -> 0.88 us
  Pallas kernels: 57.5 us -> 70.7 us
  matrix products: 17.3 us -> 6.68 us
    ppermute x11 -> x10, waiting for transfers between devices: 122 us -> 74.5 us  [across(): return lax.ppermute(value, 'replica', [(s, s ^ 4) for s in range(8)])]
    all_gather x1 -> x0, waiting for transfers between devices: 22.3 us -> none  [gather_tokens(): return lax.all_gather(moved, 'tensor', axis=0, tiled=False)]
    all_to_all x0 -> x1, waiting for transfers between devices: none -> 16.6 us  [along_y(): lax.all_to_all(copies, 'tensor', 0, 0, tiled=True, axis_index_groups=[[0,...]
    unnamed x18 -> x37, local copies, waits for them, and re-layouts: 2.8 us -> 17.1 us
    ppermute x8 -> x4, waiting for transfers between devices: 35.8 us -> 22.1 us  [swap_dp(): return lax.ppermute(value, 'dp', [(0, 1), (1, 0)])]
    pallas_call x13 -> x29, Pallas kernels: 57.5 us -> 70.7 us  [the longest x7 26.1 us: make(): pl.pallas_call(make_kernel, grid=(rows // STEP_ROWS,), out_shape=(jax.Sha...]
    dot_general x8 -> x1, matrix products: 17.3 us -> 6.68 us  [body(): lax.dot_general(features[:4], upstream, (((1,), (0,)), ((), ())), preferr...]
    slice x3 -> x7, local copies, waits for them, and re-layouts: 5.78 us -> 11 us  [the longest x5 8.82 us: part(): return value[:, piece[0]:piece[0] + piece[1]]]
  transfers between devices with their start and end apart: 24 -> 20, of which waited for: 15 -> 14; matrix products, arithmetic and copies ran while one was open for 9% -> 9% of each run, Pallas kernels for 15% -> 23%
where the time goes in v2:
time: 293 us; the launch traced here: 292 us
  waiting for transfers between devices  132 us (45%)
  Pallas kernels  70.7 us (24%)
  starting transfers between devices  44.9 us (15%)
  local copies, waits for them, and re-layouts  34.6 us (12%)
  matrix products  6.68 us (2%)
    ppermute x10, waiting for transfers between devices, across(): return lax.ppermute(value, 'replica', [(s, s ^ 4) for s in range(8)])  74.5 us
    pallas_call x7, Pallas kernels, make(): pl.pallas_call(make_kernel, grid=(rows // STEP_ROWS,), out_shape=(jax.Sha...  26.1 us
    ppermute x4, waiting for transfers between devices, swap_dp(): return lax.ppermute(value, 'dp', [(0, 1), (1, 0)])  22.1 us
    pallas_call x7, Pallas kernels, mix(): pl.pallas_call(mix_kernel, grid=(rows // STEP_ROWS,), out_shape=(whole, w...  20.9 us
    ppermute x10, starting transfers between devices, across(): return lax.ppermute(value, 'replica', [(s, s ^ 4) for s in range(8)])  20.8 us
    unnamed x37, local copies, waits for them, and re-layouts  17.1 us
    all_to_all x1, waiting for transfers between devices, along_y(): lax.all_to_all(copies, 'tensor', 0, 0, tiled=True, axis_index_groups=[[0,...  16.6 us
    ppermute x1, waiting for transfers between devices, settle(): return lax.ppermute(mine, ('dp', 'tensor'), pairs)  13.9 us
  transfers between devices with their start and end apart: 20, of which 14 were waited for; matrix products, arithmetic and copies ran while one was open for 9% of the time, Pallas kernels for 23%

profile of v2, /device:TPU:6, one launch (start us, length us, event | category | flops | bytes accessed | tf_op | source)
XLA Modules:
  0.0 291.8 jit_solution(1992590165574811820)
XLA Ops:
  0.7 3.6 %slice.42 = bf16[1024,1280]{1,0:T(8,128)(2,1)} slice(bf16[1024,1792]{1,0:T(8,128)(2,1)} %bitcast.26), slice={[0:1024], [0:1280]} | slice | bytes 5242880 | tf_op jit(solution)/shard_map/slice | solution.py:263
  4.2 3.9 %collective-permute-start.3 = (bf16[1024,1280]{1,0:T(8,128)(2,1)}, bf16[1024,1280]{1,0:T(8,128)(2,1)}, u32[]{:S(2)}, u32[]{:S(2)}) collective-permute-start(bf16[1024,1280]{1,0:T(8,128)(2,1)} %slice.42), channel_id=1, source_target_pairs={{0,64},{16,80},{32,96},{48,112},{64,0},{80,16},{96,32},{112,48},{1... | collective-permute-start | bytes 7864328 | tf_op jit(solution)/shard_map/ppermute | solution.py:19
  9.6 6.7 %collective-permute-start = (bf16[1024,256]{1,0:T(8,128)(2,1)S(1)}, bf16[1024,256]{1,0:T(8,128)(2,1)S(1)}, u32[]{:S(2)}, u32[]{:S(2)}) collective-permute-start(bf16[1024,256]{1,0:T(8,128)(2,1)S(1)} %bitcast.61), channel_id=1, source_target_pairs={{0,0},{1,1},{2,2},{3,3},{4,8},{5,9},{6,10},{7,11},{8,4},{9,5},{10,... | collective-permute-start | bytes 1572872 | tf_op jit(solution)/shard_map/ppermute | solution.py:56
  17.9 6.6 %collective-permute-done.1.refs_1_.u_ref = bf16[1024,256]{1,0:T(8,128)(2,1)S(1)} collective-permute-done((bf16[1024,256]{1,0:T(8,128)(2,1)S(1)}, bf16[1024,256]{1,0:T(8,128)(2,1)S(1)}, u32[]{:S(2)}, u32[]{:S(2)}) %collective-permute-start.1) | collective-permute-done | bytes 524320 | tf_op jit(solution)/shard_map/ppermute | solution.py:23
  24.6 13.9 %collective-permute-done.refs_0_ = bf16[1024,256]{1,0:T(8,128)(2,1)S(1)} collective-permute-done((bf16[1024,256]{1,0:T(8,128)(2,1)S(1)}, bf16[1024,256]{1,0:T(8,128)(2,1)S(1)}, u32[]{:S(2)}, u32[]{:S(2)}) %collective-permute-start) | collective-permute-done | bytes 524320 | tf_op jit(solution)/shard_map/ppermute | solution.py:56
  39.9 2.5 broadcast_in_dim.12
  42.4 3.6 %all-to-all-start = ((bf16[4,1024,256]{2,1,0:T(8,128)(2,1)}), bf16[4,1024,256]{2,1,0:T(8,128)(2,1)S(1)}, u32[]{:S(2)}, u32[]{:S(2)}) async-start(bf16[4,1024,256]{2,1,0:T(8,128)(2,1)} %broadcast_in_dim.12), calls=%async_computation | async-start | bytes 4194304 | tf_op jit(solution)/shard_map/all_to_all | solution.py:61
  47.3 2.3 slice.37.refs_1_
  53.3 16.6 %all-to-all-done.refs_0_ = bf16[4,1024,256]{2,1,0:T(8,128)(2,1)S(1)} async-done(((bf16[4,1024,256]{2,1,0:T(8,128)(2,1)}), bf16[4,1024,256]{2,1,0:T(8,128)(2,1)S(1)}, u32[]{:S(2)}, u32[]{:S(2)}) %all-to-all-start) | async-done | bytes 2097184 | tf_op jit(solution)/shard_map/all_to_all | solution.py:61
  69.9 6.9 %collective-permute-done.2.refs_3_.u_ref = bf16[1024,1024]{1,0:T(8,128)(2,1)} collective-permute-done((bf16[1024,1024]{1,0:T(8,128)(2,1)}, bf16[1024,1024]{1,0:T(8,128)(2,1)}, u32[]{:S(2)}, u32[]{:S(2)}) %collective-permute-start.2) | collective-permute-done | bytes 2097184 | tf_op jit(solution)/shard_map/ppermute | solution.py:23
  77.8 4.0 %collective-permute-start.5 = (bf16[1024,512]{1,0:T(8,128)(2,1)}, bf16[1024,512]{1,0:T(8,128)(2,1)S(1)}, u32[]{:S(2)}, u32[]{:S(2)}) collective-permute-start(bf16[1024,512]{1,0:T(8,128)(2,1)} %get-tuple-element.56), channel_id=1, source_target_pairs={{0,8},{8,0},{1,9},{9,1},{2,10},{10,2},{3,11},{11,3},{4,12},{12,4},... | collective-permute-start | bytes 3145736 | tf_op jit(solution)/shard_map/ppermute | solution.py:23
  85.9 2.4 copy.42
  88.2 3.0 %copy.43 = bf16[4,1024,256]{1,2,0:T(8,128)(2,1)S(1)} copy(bf16[4,1024,256]{2,1,0:T(8,128)(2,1)} %get-tuple-element.104) | data formatting | bytes 4194304
  91.2 6.7 %fusion.local_ref = f32[1024,1792]{1,0:T(8,128)S(1)} fusion(bf16[1024,1024]{1,0:T(8,128)(2,1)} %bitcast.60, bf16[1,1024,1792]{2,1,0:T(8,128)(2,1)} %param.6), kind=kOutput, calls=%fused_computation.3 | convolution fusion | flops 3758096384 | bytes 13107200 | tf_op jit(solution)/shard_map/dot_general | solution.py:289
  100.4 5.2 %collective-permute-done.5.u_ref = bf16[1024,512]{1,0:T(8,128)(2,1)S(1)} collective-permute-done((bf16[1024,512]{1,0:T(8,128)(2,1)}, bf16[1024,512]{1,0:T(8,128)(2,1)S(1)}, u32[]{:S(2)}, u32[]{:S(2)}) %collective-permute-start.5) | collective-permute-done | bytes 1048608 | tf_op jit(solution)/shard_map/ppermute | solution.py:23
  105.6 2.1 shard_map.81
  109.0 4.8 %shard_map.80 = (f32[1024,1024]{1,0:T(8,128)S(1)}, f32[8,128]{1,0:T(8,128)S(1)}) custom-call(bf16[4,256,1024]{2,1,0:T(8,128)(2,1)S(1)} %bitcast.25, bf16[1024,1024]{1,0:T(8,128)(2,1)} %collective-permute-done.2.refs_3_.u_ref, f32[1024,1792]{1,0:T(8,128)S(1)} %fusion.local_ref), custom_call_target="tpu_custom_call" | custom-call | flops 2147483648 | bytes 10485760 | tf_op jit(solution)/shard_map/pallas_call | solution.py:241
  113.9 2.0 copy-done
  118.6 2.0 collective-permute-done.7
  120.6 5.0 %collective-permute-start.8 = (f32[8,128]{1,0:T(8,128)S(1)}, f32[8,128]{1,0:T(8,128)S(1)}, u32[]{:S(2)}, u32[]{:S(2)}) collective-permute-start(f32[8,128]{1,0:T(8,128)S(1)} %add.34), channel_id=1, source_target_pairs={{0,4},{1,5},{2,6},{3,7},{4,0},{5,1},{6,2},{7,3},{8,12},{9,13},{10,... | collective-permute-start | bytes 12296 | tf_op jit(solution)/shard_map/ppermute | solution.py:47
  127.2 1.7 collective-permute-start.9
  129.0 3.4 %collective-permute-done.9 = f32[8,128]{1,0:T(8,128)S(1)} collective-permute-done((f32[8,128]{1,0:T(8,128)S(1)}, f32[8,128]{1,0:T(8,128)S(1)}, u32[]{:S(2)}, u32[]{:S(2)}) %collective-permute-start.9) | collective-permute-done | bytes 4128 | tf_op jit(solution)/shard_map/ppermute | solution.py:23
  133.0 4.1 %shard_map.84 = (bf16[2,1024,256]{2,1,0:T(8,128)(2,1)}, bf16[1024,256]{1,0:T(8,128)(2,1)}) custom-call(f32[8,128]{1,0:T(8,128)} %add.36.total_ref, f32[1024,1024]{1,0:T(8,128)} %copy-done, bf16[1024,1792]{1,0:T(8,128)(2,1)} %bitcast.46, bf16[1024,1792]{1,0:T(8,128)(2,1)} %bitcast.37, bf16[1024,1792]{1,0:T(8,128)(2,1)} %bitcast.28), custom_call_target="tpu_custom_call" | custom-call | flops 7864320 | bytes 4194304 | tf_op jit(solution)/shard_map/pallas_call | solution.py:168
  137.7 3.2 %collective-permute-start.11 = (bf16[2,1024,256]{2,1,0:T(8,128)(2,1)}, bf16[2,1024,256]{2,1,0:T(8,128)(2,1)S(1)}, u32[]{:S(2)}, u32[]{:S(2)}) collective-permute-start(bf16[2,1024,256]{2,1,0:T(8,128)(2,1)} %shard_map.85.pair_ref), channel_id=1, source_target_pairs={{0,64},{16,80},{32,96},{48,112},{64,0},{80,16},{96,32},{112,48},{1... | collective-permute-start | bytes 3145736 | tf_op jit(solution)/shard_map/ppermute | solution.py:19
  141.0 4.1 %shard_map.90 = (bf16[2,1024,256]{2,1,0:T(8,128)(2,1)}, bf16[1024,256]{1,0:T(8,128)(2,1)}) custom-call(f32[8,128]{1,0:T(8,128)} %add.36.total_ref, f32[1024,1024]{1,0:T(8,128)} %copy-done, bf16[1024,1792]{1,0:T(8,128)(2,1)} %bitcast.47, bf16[1024,1792]{1,0:T(8,128)(2,1)} %bitcast.38, bf16[1024,1792]{1,0:T(8,128)(2,1)} %bitcast.29), custom_call_target="tpu_custom_call" | custom-call | flops 7864320 | bytes 4194304 | tf_op jit(solution)/shard_map/pallas_call | solution.py:168
  146.0 2.1 shard_map.88
  148.1 3.2 %collective-permute-start.13 = (bf16[1024,256]{1,0:T(8,128)(2,1)}, bf16[1024,256]{1,0:T(8,128)(2,1)S(1)}, u32[]{:S(2)}, u32[]{:S(2)}) collective-permute-start(bf16[1024,256]{1,0:T(8,128)(2,1)} %shard_map.88), channel_id=1, source_target_pairs={{0,64},{16,80},{32,96},{48,112},{64,0},{80,16},{96,32},{112,48},{1... | collective-permute-start | bytes 1572872 | tf_op jit(solution)/shard_map/ppermute | solution.py:19
  151.4 4.1 %shard_map.87 = (bf16[2,1024,256]{2,1,0:T(8,128)(2,1)}, bf16[1024,256]{1,0:T(8,128)(2,1)}) custom-call(f32[8,128]{1,0:T(8,128)} %add.36.total_ref, f32[1024,1024]{1,0:T(8,128)} %copy-done, bf16[1024,1792]{1,0:T(8,128)(2,1)} %bitcast.48, bf16[1024,1792]{1,0:T(8,128)(2,1)} %bitcast.39, bf16[1024,1792]{1,0:T(8,128)(2,1)} %bitcast.30), custom_call_target="tpu_custom_call" | custom-call | flops 7864320 | bytes 4194304 | tf_op jit(solution)/shard_map/pallas_call | solution.py:168
  155.4 40.6 %collective-permute-done.13.refs_1_.scaled_other_ref = bf16[1024,256]{1,0:T(8,128)(2,1)S(1)} collective-permute-done((bf16[1024,256]{1,0:T(8,128)(2,1)}, bf16[1024,256]{1,0:T(8,128)(2,1)S(1)}, u32[]{:S(2)}, u32[]{:S(2)}) %collective-permute-start.13) | collective-permute-done | bytes 524320 | tf_op jit(solution)/shard_map/ppermute | solution.py:19
  197.5 2.8 collective-permute-start.14
  200.3 4.1 %shard_map.83 = (bf16[2,1024,256]{2,1,0:T(8,128)(2,1)}, bf16[1024,256]{1,0:T(8,128)(2,1)}) custom-call(f32[8,128]{1,0:T(8,128)} %add.36.total_ref, f32[1024,512]{1,0:T(8,128)} %copy-done.3, bf16[1024,1792]{1,0:T(8,128)(2,1)} %bitcast.49, bf16[1024,1792]{1,0:T(8,128)(2,1)} %bitcast.40, bf16[1024,1792]{1,0:T(8,128)(2,1)} %bitcast.31), custom_call_target="tpu_custom_call" | custom-call | flops 7864320 | bytes 4194304 | tf_op jit(solution)/shard_map/pallas_call | solution.py:168
  206.8 4.0 %shard_map.99 = (bf16[2,1024,256]{2,1,0:T(8,128)(2,1)}, bf16[1024,256]{1,0:T(8,128)(2,1)}) custom-call(f32[8,128]{1,0:T(8,128)} %add.36.total_ref, f32[1024,512]{1,0:T(8,128)} %copy-done.3, bf16[1024,1792]{1,0:T(8,128)(2,1)} %bitcast.50, bf16[1024,1792]{1,0:T(8,128)(2,1)} %bitcast.41, bf16[1024,1792]{1,0:T(8,128)(2,1)} %bitcast.32), custom_call_target="tpu_custom_call" | custom-call | flops 7864320 | bytes 4194304 | tf_op jit(solution)/shard_map/pallas_call | solution.py:168
  210.8 3.2 %shard_map.92 = (bf16[1024,1792]{1,0:T(8,128)(2,1)}, bf16[1024,1792]{1,0:T(8,128)(2,1)}, bf16[1024,1792]{1,0:T(8,128)(2,1)}, f32[8,128]{1,0:T(8,128)}) custom-call(bf16[2,1024,256]{2,1,0:T(8,128)(2,1)} %shard_map.85.pair_ref, bf16[1024,256]{1,0:T(8,128)(2,1)} %get-tuple-element.69.step_ref, bf16[2,1024,256]{2,1,0:T(8,128)(2,1)} %copy-done.7, ...), custom_call_target="tpu_custom_call" | custom-call | flops 7864320 | bytes 4718592 | tf_op jit(solution)/shard_map/pallas_call | solution.py:182
  215.7 2.8 collective-permute-start.18
  218.6 2.9 shard_map.97
  221.4 2.9 shard_map.82
  224.3 6.3 %shard_map.93 = (bf16[1024,1792]{1,0:T(8,128)(2,1)}, bf16[1024,1792]{1,0:T(8,128)(2,1)}, bf16[1024,1792]{1,0:T(8,128)(2,1)}) custom-call(f32[8,128]{1,0:T(8,128)} %add.36.total_ref, f32[1024,1024]{1,0:T(8,128)} %copy-done, bf16[1024,256]{1,0:T(8,128)(2,1)} %copy-done.12, ...), custom_call_target="tpu_custom_call", output_to_operand_aliasing={{0}: (9, {}), {1}: (10, {}), {2}: (11, {})} | custom-call | flops 15728640 | bytes 5767168 | tf_op jit(solution)/shard_map/pallas_call | solution.py:197
  230.6 3.2 %shard_map.94 = (bf16[1024,1792]{1,0:T(8,128)(2,1)}, bf16[1024,1792]{1,0:T(8,128)(2,1)}, bf16[1024,1792]{1,0:T(8,128)(2,1)}, f32[8,128]{1,0:T(8,128)}) custom-call(bf16[2,1024,256]{2,1,0:T(8,128)(2,1)} %shard_map.91.pair_ref, bf16[1024,256]{1,0:T(8,128)(2,1)} %get-tuple-element.68.step_ref, ...), custom_call_target="tpu_custom_call", output_to_operand_aliasing={{0}: (4, {}), {1}: (5, {}), {2}: (6, {})} | custom-call | flops 7864320 | bytes 4718592 | tf_op jit(solution)/shard_map/pallas_call | solution.py:182
  236.2 3.2 %shard_map.95 = (bf16[1024,1792]{1,0:T(8,128)(2,1)}, bf16[1024,1792]{1,0:T(8,128)(2,1)}, bf16[1024,1792]{1,0:T(8,128)(2,1)}, f32[8,128]{1,0:T(8,128)}) custom-call(bf16[2,1024,256]{2,1,0:T(8,128)(2,1)} %shard_map.89.pair_ref, bf16[1024,256]{1,0:T(8,128)(2,1)} %get-tuple-element.66.step_ref, ...), custom_call_target="tpu_custom_call", output_to_operand_aliasing={{0}: (4, {}), {1}: (5, {}), {2}: (6, {})} | custom-call | flops 7864320 | bytes 4718592 | tf_op jit(solution)/shard_map/pallas_call | solution.py:182
  239.4 8.3 %collective-permute-done.12.refs_1_.pair_other_ref = bf16[2,1024,256]{2,1,0:T(8,128)(2,1)S(1)} collective-permute-done((bf16[2,1024,256]{2,1,0:T(8,128)(2,1)}, bf16[2,1024,256]{2,1,0:T(8,128)(2,1)S(1)}, u32[]{:S(2)}, u32[]{:S(2)}) %collective-permute-start.12) | collective-permute-done | bytes 1048608 | tf_op jit(solution)/shard_map/ppermute | solution.py:19
  249.5 2.8 collective-permute-start.16
  252.3 3.2 %shard_map.101 = (bf16[1024,1792]{1,0:T(8,128)(2,1)}, bf16[1024,1792]{1,0:T(8,128)(2,1)}, bf16[1024,1792]{1,0:T(8,128)(2,1)}, f32[8,128]{1,0:T(8,128)}) custom-call(bf16[2,1024,256]{2,1,0:T(8,128)(2,1)} %shard_map.86.pair_ref, bf16[1024,256]{1,0:T(8,128)(2,1)} %get-tuple-element.87.step_ref, ...), custom_call_target="tpu_custom_call", output_to_operand_aliasing={{0}: (4, {}), {1}: (5, {}), {2}: (6, {})} | custom-call | flops 7864320 | bytes 4718592 | tf_op jit(solution)/shard_map/pallas_call | solution.py:182
  255.5 14.7 %collective-permute-done.18.pair_other_ref = bf16[2,1024,256]{2,1,0:T(8,128)(2,1)S(1)} collective-permute-done((bf16[2,1024,256]{2,1,0:T(8,128)(2,1)}, bf16[2,1024,256]{2,1,0:T(8,128)(2,1)S(1)}, u32[]{:S(2)}, u32[]{:S(2)}) %collective-permute-start.18) | collective-permute-done | bytes 1048608 | tf_op jit(solution)/shard_map/ppermute | solution.py:19
  271.2 3.2 %shard_map.102 = (bf16[1024,1792]{1,0:T(8,128)(2,1)}, bf16[1024,1792]{1,0:T(8,128)(2,1)}, bf16[1024,1792]{1,0:T(8,128)(2,1)}, f32[8,128]{1,0:T(8,128)}) custom-call(bf16[2,1024,256]{2,1,0:T(8,128)(2,1)} %shard_map.100.pair_ref, bf16[1024,256]{1,0:T(8,128)(2,1)} %get-tuple-element.86.step_ref, ...), custom_call_target="tpu_custom_call", output_to_operand_aliasing={{0}: (4, {}), {1}: (5, {}), {2}: (6, {})} | custom-call | flops 7864320 | bytes 4718592 | tf_op jit(solution)/shard_map/pallas_call | solution.py:182
  274.4 7.0 %collective-permute-done.17.pair_other_ref = bf16[2,1024,128]{2,1,0:T(8,128)(2,1)S(1)} collective-permute-done((bf16[2,1024,128]{2,1,0:T(8,128)(2,1)}, bf16[2,1024,128]{2,1,0:T(8,128)(2,1)S(1)}, u32[]{:S(2)}, u32[]{:S(2)}) %collective-permute-start.17) | collective-permute-done | bytes 524320 | tf_op jit(solution)/shard_map/ppermute | solution.py:19
  282.3 2.4 shard_map.103
  284.6 3.9 %collective-permute-done.16.pair_other_ref = bf16[2,1024,128]{2,1,0:T(8,128)(2,1)S(1)} collective-permute-done((bf16[2,1024,128]{2,1,0:T(8,128)(2,1)}, bf16[2,1024,128]{2,1,0:T(8,128)(2,1)S(1)}, u32[]{:S(2)}, u32[]{:S(2)}) %collective-permute-start.16) | collective-permute-done | bytes 524320 | tf_op jit(solution)/shard_map/ppermute | solution.py:19
  289.3 2.4 shard_map.104
  (76 shorter events, 37.3 us)
Async XLA Ops:
  0.6 7.5 %copy-start.11 = (bf16[1,1024,1792]{2,1,0:T(8,128)(2,1)S(1)}, bf16[1,1024,1792]{2,1,0:T(8,128)(2,1)}, u32[]{:S(2)}) copy-start(bf16[1,1024,1792]{2,1,0:T(8,128)(2,1)} %param.6) | copy-start | bytes 11010052
  0.6 9.0 %copy-start.17 = (bf16[1,1024,256]{2,1,0:T(8,128)(2,1)S(1)}, bf16[1,1024,256]{2,1,0:T(8,128)(2,1)}, u32[]{:S(2)}) copy-start(bf16[1,1024,256]{2,1,0:T(8,128)(2,1)} %param.5) | copy-start | bytes 1572868
  4.2 72.6 %collective-permute-start.3 = (bf16[1024,1280]{1,0:T(8,128)(2,1)}, bf16[1024,1280]{1,0:T(8,128)(2,1)}, u32[]{:S(2)}, u32[]{:S(2)}) collective-permute-start(bf16[1024,1280]{1,0:T(8,128)(2,1)} %slice.42), channel_id=1, source_target_pairs={{0,64},{16,80},{32,96},{48,112},{64,0},{80,16},{96,32},{112,48},{1... | collective-permute-start | bytes 7864328 | tf_op jit(solution)/shard_map/ppermute | solution.py:19
  8.1 16.4 %collective-permute-start.1 = (bf16[1024,256]{1,0:T(8,128)(2,1)S(1)}, bf16[1024,256]{1,0:T(8,128)(2,1)S(1)}, u32[]{:S(2)}, u32[]{:S(2)}) collective-permute-start(bf16[1024,256]{1,0:T(8,128)(2,1)S(1)} %slice.36), channel_id=1, source_target_pairs={{0,8},{8,0},{1,9},{9,1},{2,10},{10,2},{3,11},{11,3},{4,12},{12,4},... | collective-permute-start | bytes 1572872 | tf_op jit(solution)/shard_map/ppermute | solution.py:23
  9.6 28.8 %collective-permute-start = (bf16[1024,256]{1,0:T(8,128)(2,1)S(1)}, bf16[1024,256]{1,0:T(8,128)(2,1)S(1)}, u32[]{:S(2)}, u32[]{:S(2)}) collective-permute-start(bf16[1024,256]{1,0:T(8,128)(2,1)S(1)} %bitcast.61), channel_id=1, source_target_pairs={{0,0},{1,1},{2,2},{3,3},{4,8},{5,9},{6,10},{7,11},{8,4},{9,5},{10,... | collective-permute-start | bytes 1572872 | tf_op jit(solution)/shard_map/ppermute | solution.py:56
  17.9 58.9 %collective-permute-start.2 = (bf16[1024,1024]{1,0:T(8,128)(2,1)}, bf16[1024,1024]{1,0:T(8,128)(2,1)}, u32[]{:S(2)}, u32[]{:S(2)}) collective-permute-start(bf16[1024,1024]{1,0:T(8,128)(2,1)} %slice.41), channel_id=1, source_target_pairs={{0,8},{8,0},{1,9},{9,1},{2,10},{10,2},{3,11},{11,3},{4,12},{12,4},... | collective-permute-start | bytes 6291464 | tf_op jit(solution)/shard_map/ppermute | solution.py:23
  24.6 13.9 %copy-start.5 = (bf16[1024,256]{1,0:T(8,128)(2,1)}, bf16[1024,256]{1,0:T(8,128)(2,1)S(1)}, u32[]{:S(2)}) copy-start(bf16[1024,256]{1,0:T(8,128)(2,1)S(1)} %collective-permute-done.1.refs_1_.u_ref) | copy-start | bytes 1572868
  38.4 0.8 copy-start.13
  42.4 27.5 %all-to-all-start = ((bf16[4,1024,256]{2,1,0:T(8,128)(2,1)}), bf16[4,1024,256]{2,1,0:T(8,128)(2,1)S(1)}, u32[]{:S(2)}, u32[]{:S(2)}) async-start(bf16[4,1024,256]{2,1,0:T(8,128)(2,1)} %broadcast_in_dim.12), calls=%async_computation | async-start | bytes 4194304 | tf_op jit(solution)/shard_map/all_to_all | solution.py:61
  69.9 6.9 %copy-start.1 = (bf16[4,1024,256]{2,1,0:T(8,128)(2,1)}, bf16[4,1024,256]{2,1,0:T(8,128)(2,1)S(1)}, u32[]{:S(2)}) copy-start(bf16[4,1024,256]{2,1,0:T(8,128)(2,1)S(1)} %all-to-all-done.refs_0_) | copy-start | bytes 6291460
  77.5 4.4 %collective-permute-start.4 = (bf16[4,1024,256]{2,1,0:T(8,128)(2,1)}, bf16[4,1024,256]{2,1,0:T(8,128)(2,1)S(1)}, u32[]{:S(2)}, u32[]{:S(2)}) collective-permute-start(bf16[4,1024,256]{2,1,0:T(8,128)(2,1)} %get-tuple-element.53.near_ref), channel_id=1, source_target_pairs={{0,1},{1,0},{2,3},{3,2},{4,5},{5,4},{6,7},{7,6},{8,9},{9,8},{10,11... | collective-permute-start | bytes 6291464 | tf_op jit(solution)/shard_map/ppermute | solution.py:47
  77.5 59.6 %collective-permute-start.10 = (bf16[1024,1024]{1,0:T(8,128)(2,1)}, bf16[1024,1024]{1,0:T(8,128)(2,1)}, u32[]{:S(2)}, u32[]{:S(2)}) collective-permute-start(bf16[1024,1024]{1,0:T(8,128)(2,1)} %get-tuple-element.64), channel_id=1, source_target_pairs={{0,64},{16,80},{32,96},{48,112},{64,0},{80,16},{96,32},{112,48},{1... | collective-permute-start | bytes 6291464 | tf_op jit(solution)/shard_map/ppermute | solution.py:19
  77.8 27.8 %collective-permute-start.5 = (bf16[1024,512]{1,0:T(8,128)(2,1)}, bf16[1024,512]{1,0:T(8,128)(2,1)S(1)}, u32[]{:S(2)}, u32[]{:S(2)}) collective-permute-start(bf16[1024,512]{1,0:T(8,128)(2,1)} %get-tuple-element.56), channel_id=1, source_target_pairs={{0,8},{8,0},{1,9},{9,1},{2,10},{10,2},{3,11},{11,3},{4,12},{12,4},... | collective-permute-start | bytes 3145736 | tf_op jit(solution)/shard_map/ppermute | solution.py:23
  81.9 1.6 copy-start.2
  91.2 6.7 %copy-start.6 = (bf16[1024,256]{1,0:T(8,128)(2,1)S(1)}, bf16[1024,256]{1,0:T(8,128)(2,1)}, u32[]{:S(2)}) copy-start(bf16[1024,256]{1,0:T(8,128)(2,1)} %copy-done.5) | copy-start | bytes 1572868
  99.4 1.0 copy-start.4
  107.7 1.3 copy-start.3
  113.8 2.0 copy-start
  115.8 1.2 collective-permute-start.6
  117.0 3.6 %collective-permute-start.7 = (f32[8,128]{1,0:T(8,128)S(1)}, f32[8,128]{1,0:T(8,128)S(1)}, u32[]{:S(2)}, u32[]{:S(2)}) collective-permute-start(f32[8,128]{1,0:T(8,128)S(1)} %add.33), channel_id=1, source_target_pairs={{0,2},{1,3},{2,0},{3,1},{4,6},{5,7},{6,4},{7,5},{8,10},{9,11},{10,... | collective-permute-start | bytes 12296 | tf_op jit(solution)/shard_map/ppermute | solution.py:47
  120.6 6.6 %collective-permute-start.8 = (f32[8,128]{1,0:T(8,128)S(1)}, f32[8,128]{1,0:T(8,128)S(1)}, u32[]{:S(2)}, u32[]{:S(2)}) collective-permute-start(f32[8,128]{1,0:T(8,128)S(1)} %add.34), channel_id=1, source_target_pairs={{0,4},{1,5},{2,6},{3,7},{4,0},{5,1},{6,2},{7,3},{8,12},{9,13},{10,... | collective-permute-start | bytes 12296 | tf_op jit(solution)/shard_map/ppermute | solution.py:47
  127.2 5.1 %collective-permute-start.9 = (f32[8,128]{1,0:T(8,128)S(1)}, f32[8,128]{1,0:T(8,128)S(1)}, u32[]{:S(2)}, u32[]{:S(2)}) collective-permute-start(f32[8,128]{1,0:T(8,128)S(1)} %add.35), channel_id=1, source_target_pairs={{0,8},{8,0},{1,9},{9,1},{2,10},{10,2},{3,11},{11,3},{4,12},{12,4},... | collective-permute-start | bytes 12296 | tf_op jit(solution)/shard_map/ppermute | solution.py:23
  137.7 66.7 %collective-permute-start.11 = (bf16[2,1024,256]{2,1,0:T(8,128)(2,1)}, bf16[2,1024,256]{2,1,0:T(8,128)(2,1)S(1)}, u32[]{:S(2)}, u32[]{:S(2)}) collective-permute-start(bf16[2,1024,256]{2,1,0:T(8,128)(2,1)} %shard_map.85.pair_ref), channel_id=1, source_target_pairs={{0,64},{16,80},{32,96},{48,112},{64,0},{80,16},{96,32},{112,48},{1... | collective-permute-start | bytes 3145736 | tf_op jit(solution)/shard_map/ppermute | solution.py:19
  145.7 68.3 %collective-permute-start.15 = (bf16[2,1024,256]{2,1,0:T(8,128)(2,1)}, bf16[2,1024,256]{2,1,0:T(8,128)(2,1)S(1)}, u32[]{:S(2)}, u32[]{:S(2)}) collective-permute-start(bf16[2,1024,256]{2,1,0:T(8,128)(2,1)} %shard_map.91.pair_ref), channel_id=1, source_target_pairs={{0,64},{16,80},{32,96},{48,112},{64,0},{80,16},{96,32},{112,48},{1... | collective-permute-start | bytes 3145736 | tf_op jit(solution)/shard_map/ppermute | solution.py:19
  148.1 47.9 %collective-permute-start.13 = (bf16[1024,256]{1,0:T(8,128)(2,1)}, bf16[1024,256]{1,0:T(8,128)(2,1)S(1)}, u32[]{:S(2)}, u32[]{:S(2)}) collective-permute-start(bf16[1024,256]{1,0:T(8,128)(2,1)} %shard_map.88), channel_id=1, source_target_pairs={{0,64},{16,80},{32,96},{48,112},{64,0},{80,16},{96,32},{112,48},{1... | collective-permute-start | bytes 1572872 | tf_op jit(solution)/shard_map/ppermute | solution.py:19
  196.0 0.8 copy-start.12
  197.5 36.4 %collective-permute-start.14 = (bf16[2,1024,256]{2,1,0:T(8,128)(2,1)}, bf16[2,1024,256]{2,1,0:T(8,128)(2,1)S(1)}, u32[]{:S(2)}, u32[]{:S(2)}) collective-permute-start(bf16[2,1024,256]{2,1,0:T(8,128)(2,1)} %shard_map.89.pair_ref), channel_id=1, source_target_pairs={{0,64},{16,80},{32,96},{48,112},{64,0},{80,16},{96,32},{112,48},{1... | collective-permute-start | bytes 3145736 | tf_op jit(solution)/shard_map/ppermute | solution.py:19
  204.4 1.0 copy-start.7
  206.1 41.7 %collective-permute-start.12 = (bf16[2,1024,256]{2,1,0:T(8,128)(2,1)}, bf16[2,1024,256]{2,1,0:T(8,128)(2,1)S(1)}, u32[]{:S(2)}, u32[]{:S(2)}) collective-permute-start(bf16[2,1024,256]{2,1,0:T(8,128)(2,1)} %shard_map.86.pair_ref), channel_id=1, source_target_pairs={{0,64},{16,80},{32,96},{48,112},{64,0},{80,16},{96,32},{112,48},{1... | collective-permute-start | bytes 3145736 | tf_op jit(solution)/shard_map/ppermute | solution.py:19
  214.0 1.0 copy-start.10
  215.7 54.5 %collective-permute-start.18 = (bf16[2,1024,256]{2,1,0:T(8,128)(2,1)}, bf16[2,1024,256]{2,1,0:T(8,128)(2,1)S(1)}, u32[]{:S(2)}, u32[]{:S(2)}) collective-permute-start(bf16[2,1024,256]{2,1,0:T(8,128)(2,1)} %shard_map.100.pair_ref), channel_id=1, source_target_pairs={{0,64},{16,80},{32,96},{48,112},{64,0},{80,16},{96,32},{112,48},{1... | collective-permute-start | bytes 3145736 | tf_op jit(solution)/shard_map/ppermute | solution.py:19
  233.8 1.0 copy-start.9
  235.5 45.9 %collective-permute-start.17 = (bf16[2,1024,128]{2,1,0:T(8,128)(2,1)}, bf16[2,1024,128]{2,1,0:T(8,128)(2,1)S(1)}, u32[]{:S(2)}, u32[]{:S(2)}) collective-permute-start(bf16[2,1024,128]{2,1,0:T(8,128)(2,1)} %shard_map.98.pair_ref), channel_id=1, source_target_pairs={{0,64},{16,80},{32,96},{48,112},{64,0},{80,16},{96,32},{112,48},{1... | collective-permute-start | bytes 1572872 | tf_op jit(solution)/shard_map/ppermute | solution.py:19
  247.8 1.0 copy-start.8
  249.5 39.1 %collective-permute-start.16 = (bf16[2,1024,128]{2,1,0:T(8,128)(2,1)}, bf16[2,1024,128]{2,1,0:T(8,128)(2,1)S(1)}, u32[]{:S(2)}, u32[]{:S(2)}) collective-permute-start(bf16[2,1024,128]{2,1,0:T(8,128)(2,1)} %shard_map.96.pair_ref), channel_id=1, source_target_pairs={{0,64},{16,80},{32,96},{48,112},{64,0},{80,16},{96,32},{112,48},{1... | collective-permute-start | bytes 1572872 | tf_op jit(solution)/shard_map/ppermute | solution.py:19
  270.2 1.0 copy-start.14
  281.5 0.8 copy-start.15
  288.5 0.8 copy-start.16

commit v3 on v2

v3 whole, which is shorter than its diff:
```python
import jax
import jax.numpy as jnp
from jax import lax
from jax.experimental import pallas as pl
from jax.experimental.pallas import tpu as pltpu
from jax.sharding import PartitionSpec as P

D = 2048
FF = 14336
STEP = 1
FIX_ONE = 1.0 - 0.9**STEP
FIX_TWO = 1.0 - 0.95**STEP
BF16 = jnp.bfloat16
ANYWHERE = pl.BlockSpec(memory_space=pl.ANY)
SLIGHT = pl.CostEstimate(flops=0, bytes_accessed=4096, transcendentals=0)
F32 = jnp.float32


def across(value):
    return lax.ppermute(value, "replica", [(s, s ^ 4) for s in range(8)])


def swap_dp(value):
    return lax.ppermute(value, "dp", [(0, 1), (1, 0)])


def nothing_kernel(*refs):
    del refs


def corner(value):
    if value.ndim > 2:
        return pl.BlockSpec(memory_space=pltpu.VMEM)
    return pl.BlockSpec((1,) * (value.ndim - 2) + (16 if value.dtype == BF16 else 8, 128), lambda i: (0,) * value.ndim)


def gate(values, earlier, size=4096):
    return pl.pallas_call(
        nothing_kernel,
        grid=(1,),
        out_shape=[jax.ShapeDtypeStruct(value.shape, value.dtype) for value in values],
        in_specs=[ANYWHERE] * len(values) + [corner(value) for value in earlier],
        out_specs=[ANYWHERE] * len(values),
        input_output_aliases={i: i for i in range(len(values))},
        cost_estimate=pl.CostEstimate(flops=0, bytes_accessed=size, transcendentals=0),
    )(*values, *earlier)


def turned(value, bits):
    return lax.ppermute(value, "tensor", [(t, t ^ bits) for t in range(8)])


def settle(mine):
    pairs = []
    for d in range(2):
        for t in range(8):
            stays = t // 4 == d
            pairs.append((d * 8 + t, d * 8 + t if stays else (1 - d) * 8 + (t ^ 6)))
    return lax.ppermute(mine, ("dp", "tensor"), pairs)


def along_y(value):
    copies = jnp.broadcast_to(value, (4, *value.shape))
    return lax.all_to_all(copies, "tensor", 0, 0, tiled=True, axis_index_groups=[[0, 2, 4, 6], [1, 3, 5, 7]])


def assemble_kernel(slot_ref, near_ref, low_ref, high_ref, out_ref):
    for k in range(4):
        out_ref[slot_ref[k]] = near_ref[k]
    for k in range(2):
        out_ref[slot_ref[4 + k]] = low_ref[k]
        out_ref[slot_ref[6 + k]] = high_ref[k]


def assemble(near, low, high):
    core = lax.axis_index("tensor") % 2
    flip = 4 * lax.axis_index("dp")
    places = jnp.stack([(2 * y + core) ^ flip for y in range(4)] + [(2 * y + 1 - core) ^ flip for y in range(4)])
    slots = places ^ (places // 4 * 2)
    whole = pl.BlockSpec(memory_space=pltpu.VMEM)
    return pl.pallas_call(
        assemble_kernel,
        out_shape=jax.ShapeDtypeStruct((8, *near.shape[1:]), BF16),
        in_specs=[pl.BlockSpec(memory_space=pltpu.SMEM)] + [whole] * 3,
        out_specs=whole,
        cost_estimate=SLIGHT,
        compiler_params=pltpu.CompilerParams(vmem_limit_bytes=24 * 2**20),
    )(slots.astype(jnp.int32), near, low, high)


def add_kernel(one_ref, two_ref, *rest):
    rest[-1][...] = one_ref[...] + two_ref[...]


def group_sum(value, earlier):
    value = value + turned(value, 1)
    value = value + turned(value, 2) + turned(value, 4) + turned(value, 6)
    return pl.pallas_call(
        add_kernel,
        grid=(1,),
        out_shape=jax.ShapeDtypeStruct(value.shape, F32),
        in_specs=[corner(value)] * 2 + [corner(item) for item in earlier],
        out_specs=corner(value),
        cost_estimate=SLIGHT,
    )(value, swap_dp(value), *earlier)


def clip_of(total_ref):
    total = jnp.sum(total_ref[...], keepdims=True)
    return jnp.minimum(1.0, 1.0 / jnp.sqrt(total / (D * FF) + 1e-06))


def moments(scaled, first, second):
    one = 0.9 * first.astype(F32) + 0.1 * scaled
    two = 0.95 * second.astype(F32) + 0.05 * scaled * scaled
    return one.astype(BF16), two.astype(BF16)


def stepped(old, one, two):
    old = old.astype(F32)
    update = (one.astype(F32) * (1.0 / FIX_ONE)) / (jnp.sqrt(two.astype(F32) * (1.0 / FIX_TWO)) + 1e-08)
    return (old - 0.05 * (update + 0.1 * old)).astype(BF16)


def mean(a, b):
    return (0.5 * (a.astype(F32) + b.astype(F32))).astype(BF16)


def make_kernel(total_ref, grad_ref, first_ref, second_ref, old_ref, pair_ref, step_ref):
    one, two = moments(clip_of(total_ref) * grad_ref[...], first_ref[...], second_ref[...])
    pair_ref[0] = one
    pair_ref[1] = two
    step_ref[...] = stepped(old_ref[...], one, two)


def make_first_kernel(total_ref, grad_ref, first_ref, second_ref, old_ref, pair_ref, step_ref):
    rows = grad_ref.shape[0]
    clip = clip_of(total_ref)
    one, two = moments(clip * grad_ref[...], first_ref[...], second_ref[...])
    pair_ref[0, :rows] = one
    pair_ref[1, :rows] = two
    step_ref[...] = stepped(old_ref[...], one, two)
    clip = jnp.broadcast_to(clip, (16, grad_ref.shape[1]))
    high = clip.astype(BF16)
    pair_ref[0, rows:] = high
    pair_ref[1, rows:] = (clip - high.astype(F32)).astype(BF16)


def make_first(total, grad, within, first, second, old, at, width):
    rows = grad.shape[0]
    chosen = lambda start: pl.BlockSpec((rows, width), lambda i: (0, start // width))
    return pl.pallas_call(
        make_first_kernel,
        grid=(1,),
        out_shape=(jax.ShapeDtypeStruct((2, rows + 16, width), BF16), jax.ShapeDtypeStruct((rows, width), BF16)),
        in_specs=[TOTAL, chosen(within), chosen(at), chosen(at), chosen(at)],
        out_specs=(pl.BlockSpec((2, rows + 16, width), lambda i: (0, 0, 0)), chosen(0)),
        cost_estimate=cost(rows, width, 30, 16),
        compiler_params=pltpu.CompilerParams(vmem_limit_bytes=56 * 2**20),
    )(total, grad, first, second, old)


def mix_kernel(pair_ref, step_ref, pair_other_ref, old_other_ref, *rest):
    w_ref, one_ref, two_ref, flag_ref = rest[-4:]
    flag_ref[...] = jnp.zeros_like(flag_ref)
    depth = step_ref.shape[0]
    here = pl.ds(pl.multiple_of(pl.program_id(0) * depth, depth), depth)
    one_other, two_other = pair_other_ref[0, here], pair_other_ref[1, here]
    w_ref[...] = mean(step_ref[...], stepped(old_other_ref[...], one_other, two_other))
    one_ref[...] = mean(pair_ref[0], one_other)
    two_ref[...] = mean(pair_ref[1], two_other)


def early_kernel(
    total_ref,
    clip_other_ref,
    grad_ref,
    grad_other_ref,
    first_ref,
    second_ref,
    first_other_ref,
    second_other_ref,
    old_ref,
    old_other_ref,
    *rest,
):
    w_ref, one_ref, two_ref = rest[-3:]
    one, two = moments(clip_of(total_ref) * grad_ref[...], first_ref[...], second_ref[...])
    clip_other = clip_other_ref[0, :1, :1].astype(F32) + clip_other_ref[1, :1, :1].astype(F32)
    scaled_other = clip_other * grad_other_ref[...].astype(F32)
    one_other, two_other = moments(scaled_other, first_other_ref[...], second_other_ref[...])
    w_ref[...] = mean(stepped(old_ref[...], one, two), stepped(old_other_ref[...], one_other, two_other))
    one_ref[...] = mean(one, one_other)
    two_ref[...] = mean(two, two_other)


STEP_ROWS = 512
TOTAL = pl.BlockSpec((8, 128), lambda i: (0, 0))


def columns(width, at=0):
    return pl.BlockSpec((STEP_ROWS, width), lambda i: (i, at // width))


def pair_of(width):
    return pl.BlockSpec((2, STEP_ROWS, width), lambda i: (0, i, 0))


def cost(rows, width, flops, size):
    return pl.CostEstimate(flops=flops * rows * width, bytes_accessed=size * rows * width, transcendentals=0)


def make(total, grad, within, first, second, old, at, width):
    rows = grad.shape[0]
    wide = columns(width, at)
    return pl.pallas_call(
        make_kernel,
        grid=(rows // STEP_ROWS,),
        out_shape=(jax.ShapeDtypeStruct((2, rows, width), BF16), jax.ShapeDtypeStruct((rows, width), BF16)),
        in_specs=[TOTAL, columns(width, within), wide, wide, wide],
        out_specs=(pair_of(width), columns(width)),
        cost_estimate=cost(rows, width, 30, 16),
    )(total, grad, first, second, old)


def mix(pair, step, pair_other, old_other, at, width, shape, outs):
    rows = shape[0]
    depth = rows if width == 128 else STEP_ROWS
    wide = pl.BlockSpec((depth, width), lambda i: (i, at // width))
    whole = jax.ShapeDtypeStruct(shape, BF16)
    return pl.pallas_call(
        mix_kernel,
        grid=(rows // depth,),
        out_shape=(whole, whole, whole, jax.ShapeDtypeStruct((8, 128), F32)),
        in_specs=[
            pl.BlockSpec((2, depth, width), lambda i: (0, i, 0)),
            pl.BlockSpec((depth, width), lambda i: (i, 0)),
            pl.BlockSpec(memory_space=pltpu.VMEM),
            wide,
        ]
        + [ANYWHERE] * len(outs),
        out_specs=(wide, wide, wide, TOTAL),
        input_output_aliases={4 + i: i for i in range(len(outs))},
        cost_estimate=cost(rows, width, 30, 18),
    )(pair, step, pair_other, old_other, *outs)


def early(total, pair_other, grad, grad_other, first, second, other, old, old_other, width, outs):
    rows, cols = old.shape
    wide = columns(width)
    shape = jax.ShapeDtypeStruct((rows, cols), BF16)
    return pl.pallas_call(
        early_kernel,
        grid=(rows // STEP_ROWS,),
        out_shape=(shape, shape, shape),
        in_specs=[TOTAL, pl.BlockSpec((2, 16, 128), lambda i: (0, rows // 16, 0))] + [wide] * 5 + [columns(width, width), wide, wide] + [ANYWHERE] * 3,
        out_specs=(wide, wide, wide),
        input_output_aliases={10 + i: i for i in range(3)},
        cost_estimate=cost(rows, width, 60, 22),
    )(total, pair_other, grad, grad_other, first, second, other, other, old, old_other, *outs)


def times(x, u):
    return lax.dot_general(x, u, (((0,), (0,)), ((), ())), preferred_element_type=F32)


def local_kernel(x_ref, u_ref, out_ref):
    out_ref[...] = times(x_ref[0], u_ref[...])


def local_product(x, u):
    blocks, depth, step = x.shape
    width = u.shape[1]
    return pl.pallas_call(
        local_kernel,
        grid=(blocks // 2,),
        out_shape=jax.ShapeDtypeStruct((blocks // 2 * step, width), F32),
        in_specs=[pl.BlockSpec((1, depth, step), lambda i: (i, 0, 0)), pl.BlockSpec((depth, width), lambda i: (0, 0))],
        out_specs=pl.BlockSpec((step, width), lambda i: (i, 0)),
        cost_estimate=SLIGHT,
        compiler_params=pltpu.CompilerParams(vmem_limit_bytes=32 * 2**20),
    )(x, u)


def finish_kernel(x_ref, u_ref, local_ref, *rest):
    grad_ref, squares_ref = rest[-2:]
    grad = local_ref[...] + times(x_ref[0], u_ref[...])
    grad_ref[...] = grad
    square = grad * grad
    lanes = sum(square[:, k : k + 128] for k in range(0, grad.shape[1], 128))

    @pl.when(pl.program_id(0) == 0)
    def _():
        squares_ref[...] = jnp.zeros_like(squares_ref)

    squares_ref[...] += jnp.sum(lanes.reshape(-1, 8, 128), axis=0)


def finish(x, u, local, earlier):
    blocks, depth, step = x.shape
    width = u.shape[1]
    rows = pl.BlockSpec((step, width), lambda i: (i, 0))
    return pl.pallas_call(
        finish_kernel,
        grid=(blocks // 2,),
        out_shape=(jax.ShapeDtypeStruct((blocks // 2 * step, width), F32), jax.ShapeDtypeStruct((8, 128), F32)),
        in_specs=[pl.BlockSpec((1, depth, step), lambda i: (blocks // 2 + i, 0, 0)), pl.BlockSpec((depth, width), lambda i: (0, 0)), rows] + [corner(value) for value in earlier],
        out_specs=(rows, pl.BlockSpec((8, 128), lambda i: (0, 0))),
        cost_estimate=SLIGHT,
        compiler_params=pltpu.CompilerParams(vmem_limit_bytes=32 * 2**20),
    )(x, u, local, *earlier)


EARLY = 256
UP = ((0, 768), (768, 768), (1536, 256))
LATE = ((256, 256), (512, 256), (768, 384), (1152, 384), (1536, 128), (1664, 128))


def part(value, piece):
    return value[:, piece[0] : piece[0] + piece[1]]


def holder(pieces, at):
    index = next(i for i, (start, width) in enumerate(pieces) if start <= at < start + width)
    return index, at - pieces[index][0]


def body(tokens, grad_out, weights, first_moment, second_moment):
    upstream, old = grad_out[0], weights[0]
    first, second = first_moment[0], second_moment[0]

    settled = settle(tokens[0])
    up = [part(upstream, piece) for piece in UP]
    up_other = [swap_dp(piece) for piece in up]
    old_other = across(old)
    state_other = across(jnp.concatenate([first[:, :EARLY], second[:, :EARLY]], axis=1))

    (near,) = gate((along_y(settled),), (up_other[0],))
    features = assemble(near, turned(near[:2], 1), turned(near[2:], 1))
    grads, squares = [], jnp.zeros((8, 128), F32)
    for i, (piece, other) in enumerate(zip(up, up_other)):
        grad, square = finish(features, other, local_product(features, piece), (old_other,) if i == 2 else ())
        grads.append(grad)
        squares = squares + square
    grad_other = across(grads[0][:, :EARLY].astype(BF16))
    total = group_sum(squares, (state_other,))

    pairs, steps, received, flags = [], [], [], []
    outs = ()
    for i in range(len(LATE) + 2):
        if i < len(LATE):
            at, width = LATE[i]
            chunk, within = holder(UP, at)
            build = make if i else make_first
            pair, step = build(total, grads[chunk], within, first, second, old, at, width)
            if i == 0:
                (pair,) = gate((pair,), (grad_other,))
            elif i > 1:
                (pair,) = gate((pair,), (received[i - 2],) + ((flags[i - 3],) if i > 2 else ()))
            pairs.append(pair)
            steps.append(step)
            received.append(across(pair))
        if i >= 2:
            j = i - 2
            at, width = LATE[j]
            *outs, flag = mix(pairs[j], steps[j], received[j], old_other, at, width, old.shape, outs)
            flags.append(flag)
        if i == 3:
            outs = early(total, received[0], grads[0], grad_other, first, second, state_other, old, old_other, EARLY, outs)
    return tuple(out[None] for out in outs)


def solution(mesh):
    placed = P("replica", "dp", "tensor")
    return jax.shard_map(
        body,
        mesh=mesh,
        in_specs=(placed,) * 5,
        out_specs=(placed,) * 3,
        check_vma=False,
    )
```

time: 293 us -> 268 us (0.915)
  waiting for transfers between devices: 132 us -> 114 us
  local copies, waits for them, and re-layouts: 34.6 us -> 23.8 us
  Pallas kernels: 70.7 us -> 80.8 us
  matrix products: 6.68 us -> 0 us
    all_to_all x1, waiting for transfers between devices: 16.6 us -> 0.01 us  [along_y(): lax.all_to_all(copies, 'tensor', 0, 0, tiled=True, axis_index_groups=[[0,...]
    pallas_call x11 -> x14, Pallas kernels: 31.4 us -> 45.6 us  [the longest x6 21.2 us: mix(): pl.pallas_call(mix_kernel, grid=(rows // depth,), out_shape=(whole, whole...]
    ppermute x4, waiting for transfers between devices: 22.1 us -> 30.3 us  [swap_dp(): return lax.ppermute(value, 'dp', [(0, 1), (1, 0)])]
    ppermute x1, waiting for transfers between devices: 13.9 us -> 7.04 us  [settle(): return lax.ppermute(mine, ('dp', 'tensor'), pairs)]
    dot_general x1 -> x0, matrix products: 6.68 us -> none  [body(): lax.dot_general(features[:4], upstream, (((1,), (0,)), ((), ())), preferr...]
    pallas_call x7 -> x5, Pallas kernels: 26.1 us -> 20.9 us  [make(): pl.pallas_call(make_kernel, grid=(rows // STEP_ROWS,), out_shape=(jax.Sha...]
    unnamed x37 -> x32, local copies, waits for them, and re-layouts: 17.1 us -> 12.5 us
    slice x5 -> x2, local copies, waits for them, and re-layouts: 8.82 us -> 4.83 us  [part(): return value[:, piece[0]:piece[0] + piece[1]]]
  transfers between devices with their start and end apart: 20 -> 21, of which waited for: 14 -> 17; matrix products, arithmetic and copies ran while one was open for 9% -> 5% of each run, Pallas kernels for 23% -> 29%
where the time goes in v3:
time: 268 us; the launch traced here: 267 us
  waiting for transfers between devices  114 us (43%)
  Pallas kernels  80.8 us (30%)
  starting transfers between devices  46.6 us (17%)
  local copies, waits for them, and re-layouts  23.8 us (9%)
    ppermute x9, waiting for transfers between devices, across(): return lax.ppermute(value, 'replica', [(s, s ^ 4) for s in range(8)])  71.5 us
    ppermute x4, waiting for transfers between devices, swap_dp(): return lax.ppermute(value, 'dp', [(0, 1), (1, 0)])  30.3 us
    ppermute x9, starting transfers between devices, across(): return lax.ppermute(value, 'replica', [(s, s ^ 4) for s in range(8)])  23.9 us
    pallas_call x6, Pallas kernels, mix(): pl.pallas_call(mix_kernel, grid=(rows // depth,), out_shape=(whole, whole...  21.2 us
    pallas_call x5, Pallas kernels, make(): pl.pallas_call(make_kernel, grid=(rows // STEP_ROWS,), out_shape=(jax.Sha...  20.9 us
    unnamed x32, local copies, waits for them, and re-layouts  12.5 us
    pallas_call x3, Pallas kernels, finish(): pl.pallas_call(finish_kernel, grid=(blocks // 2,), out_shape=(jax.ShapeDt...  10.5 us
    ppermute x4, starting transfers between devices, swap_dp(): return lax.ppermute(value, 'dp', [(0, 1), (1, 0)])  8.1 us
  transfers between devices with their start and end apart: 21, of which 17 were waited for; matrix products, arithmetic and copies ran while one was open for 5% of the time, Pallas kernels for 29%

profile of v3, /device:TPU:6, one launch (start us, length us, event | category | flops | bytes accessed | tf_op | source)
XLA Modules:
  0.0 266.7 jit_solution(11964574417158986249)
XLA Ops:
  0.6 5.8 %collective-permute-start = (bf16[1024,256]{1,0:T(8,128)(2,1)}, bf16[1024,256]{1,0:T(8,128)(2,1)S(1)}, u32[]{:S(2)}, u32[]{:S(2)}) collective-permute-start(bf16[1024,256]{1,0:T(8,128)(2,1)} %bitcast.45), channel_id=1, source_target_pairs={{0,0},{1,1},{2,2},{3,3},{4,10},{5,11},{6,8},{7,9},{8,6},{9,7},{10,... | collective-permute-start | bytes 1572872 | tf_op jit(solution)/shard_map/ppermute | solution.py:59
  6.4 4.0 %collective-permute-start.6 = (bf16[1024,1792]{1,0:T(8,128)(2,1)}, bf16[1024,1792]{1,0:T(8,128)(2,1)}, u32[]{:S(2)}, u32[]{:S(2)}) collective-permute-start(bf16[1024,1792]{1,0:T(8,128)(2,1)} %bitcast.32), channel_id=1, source_target_pairs={{0,64},{16,80},{32,96},{48,112},{64,0},{80,16},{96,32},{112,48},{1... | collective-permute-start | bytes 11010056 | tf_op jit(solution)/shard_map/ppermute | solution.py:20
  10.4 3.8 %fusion = (bf16[1024,768]{1,0:T(8,128)(2,1)}, bf16[1024,768]{1,0:T(8,128)(2,1)}) fusion(bf16[1024,1792]{1,0:T(8,128)(2,1)} %bitcast.43), kind=kLoop, calls=%fused_computation.9 | loop fusion | bytes 6291456 | tf_op jit(solution)/shard_map/slice | solution.py:320
  14.1 7.0 %collective-permute-done = bf16[1024,256]{1,0:T(8,128)(2,1)S(1)} collective-permute-done((bf16[1024,256]{1,0:T(8,128)(2,1)}, bf16[1024,256]{1,0:T(8,128)(2,1)S(1)}, u32[]{:S(2)}, u32[]{:S(2)}) %collective-permute-start) | collective-permute-done | bytes 524320 | tf_op jit(solution)/shard_map/ppermute | solution.py:59
  22.6 3.6 %all-to-all-start = ((bf16[4,1024,256]{2,1,0:T(8,128)(2,1)}), bf16[4,1024,256]{2,1,0:T(8,128)(2,1)S(1)}, u32[]{:S(2)}, u32[]{:S(2)}) async-start(bf16[4,1024,256]{2,1,0:T(8,128)(2,1)} %broadcast_in_dim.12), calls=%async_computation | async-start | bytes 4194304 | tf_op jit(solution)/shard_map/all_to_all | solution.py:64
  26.2 2.1 collective-permute-start.4
  28.3 25.0 %collective-permute-done.1.refs_1_.u_ref = bf16[1024,768]{1,0:T(8,128)(2,1)} collective-permute-done((bf16[1024,768]{1,0:T(8,128)(2,1)}, bf16[1024,768]{1,0:T(8,128)(2,1)}, u32[]{:S(2)}, u32[]{:S(2)}) %collective-permute-start.1) | collective-permute-done | bytes 1572896 | tf_op jit(solution)/shard_map/ppermute | solution.py:24
  55.3 2.6 fusion.1
  61.7 3.3 %collective-permute-start.12 = (bf16[1024,512]{1,0:T(8,128)(2,1)}, bf16[1024,512]{1,0:T(8,128)(2,1)}, u32[]{:S(2)}, u32[]{:S(2)}) collective-permute-start(bf16[1024,512]{1,0:T(8,128)(2,1)} %pad_maximum_fusion), channel_id=1, source_target_pairs={{0,64},{16,80},{32,96},{48,112},{64,0},{80,16},{96,32},{112,48},{1... | collective-permute-start | bytes 3145736 | tf_op jit(solution)/shard_map/ppermute | solution.py:20
  67.1 4.0 %collective-permute-start.5 = (bf16[1024,256]{1,0:T(8,128)(2,1)S(1)}, bf16[1024,256]{1,0:T(8,128)(2,1)S(1)}, u32[]{:S(2)}, u32[]{:S(2)}) collective-permute-start(bf16[1024,256]{1,0:T(8,128)(2,1)S(1)} %slice.37.u_ref), channel_id=1, source_target_pairs={{0,8},{8,0},{1,9},{9,1},{2,10},{10,2},{3,11},{11,3},{4,12},{12,4},... | collective-permute-start | bytes 1572872 | tf_op jit(solution)/shard_map/ppermute | solution.py:24
  72.5 1.5 shard_map.77.x_ref
  74.0 3.9 %shard_map.78.local_ref = f32[1024,768]{1,0:T(8,128)S(1)} custom-call(bf16[8,1024,256]{2,1,0:T(8,128)(2,1)S(1)} %shard_map.77.x_ref, bf16[1024,768]{1,0:T(8,128)(2,1)} %get-tuple-element.88.u_ref), custom_call_target="tpu_custom_call" | custom-call | bytes 4096 | tf_op jit(solution)/shard_map/pallas_call | solution.py:274
  77.9 4.2 %shard_map.79 = (f32[1024,768]{1,0:T(8,128)S(1)}, f32[8,128]{1,0:T(8,128)S(1)}) custom-call(bf16[8,1024,256]{2,1,0:T(8,128)(2,1)S(1)} %shard_map.77.x_ref, bf16[1024,768]{1,0:T(8,128)(2,1)} %collective-permute-done.1.refs_1_.u_ref, f32[1024,768]{1,0:T(8,128)S(1)} %shard_map.78.local_ref), custom_call_target="tpu_custom_call" | custom-call | bytes 4096 | tf_op jit(solution)/shard_map/pallas_call | solution.py:303
  82.3 2.5 shard_map.80.local_ref
  87.0 4.0 %shard_map.81 = (f32[1024,768]{1,0:T(8,128)S(1)}, f32[8,128]{1,0:T(8,128)S(1)}) custom-call(bf16[8,1024,256]{2,1,0:T(8,128)(2,1)S(1)} %shard_map.77.x_ref, bf16[1024,768]{1,0:T(8,128)(2,1)} %collective-permute-done.4.u_ref, f32[1024,768]{1,0:T(8,128)S(1)} %shard_map.80.local_ref), custom_call_target="tpu_custom_call" | custom-call | bytes 4096 | tf_op jit(solution)/shard_map/pallas_call | solution.py:303
  91.0 1.7 copy-done.3
  92.7 3.7 %collective-permute-done.5.u_ref = bf16[1024,256]{1,0:T(8,128)(2,1)S(1)} collective-permute-done((bf16[1024,256]{1,0:T(8,128)(2,1)S(1)}, bf16[1024,256]{1,0:T(8,128)(2,1)S(1)}, u32[]{:S(2)}, u32[]{:S(2)}) %collective-permute-start.5) | collective-permute-done | bytes 524320 | tf_op jit(solution)/shard_map/ppermute | solution.py:24
  96.4 2.3 shard_map.83
  100.9 2.8 %collective-permute-start.10 = (f32[8,128]{1,0:T(8,128)S(1)}, f32[8,128]{1,0:T(8,128)S(1)}, u32[]{:S(2)}, u32[]{:S(2)}) collective-permute-start(f32[8,128]{1,0:T(8,128)S(1)} %add.34), channel_id=1, source_target_pairs={{0,6},{1,7},{2,4},{3,5},{4,2},{5,3},{6,0},{7,1},{8,14},{9,15},{10,... | collective-permute-start | bytes 12296 | tf_op jit(solution)/shard_map/ppermute | solution.py:50
  104.0 1.5 collective-permute-start.9
  105.7 1.6 collective-permute-done.8
  107.2 1.9 collective-permute-done.9
  109.1 2.0 collective-permute-start.11
  111.2 2.2 collective-permute-done.12.rest_0_.first_other_ref.second_other_ref
  116.1 4.8 %shard_map.88 = (bf16[2,1040,256]{2,1,0:T(8,128)(2,1)}, bf16[1024,256]{1,0:T(8,128)(2,1)}) custom-call(f32[8,128]{1,0:T(8,128)} %shard_map.84.total_ref, f32[1024,768]{1,0:T(8,128)} %copy-done.2, bf16[1024,1792]{1,0:T(8,128)(2,1)} %bitcast.25, bf16[1024,1792]{1,0:T(8,128)(2,1)} %bitcast.17, bf16[1024,1792]{1,0:T(8,128)(2,1)} %bitcast.33), custom_call_target="tpu_custom_call" | custom-call | flops 7864320 | bytes 4194304 | tf_op jit(solution)/shard_map/pallas_call | solution.py:152
  120.9 2.4 collective-permute-done.14.refs_1_.grad_other_ref
  124.8 3.2 %collective-permute-start.15 = (bf16[2,1040,256]{2,1,0:T(8,128)(2,1)}, bf16[2,1040,256]{2,1,0:T(8,128)(2,1)S(1)}, u32[]{:S(2)}, u32[]{:S(2)}) collective-permute-start(bf16[2,1040,256]{2,1,0:T(8,128)(2,1)} %shard_map.89.pair_ref), channel_id=1, source_target_pairs={{0,64},{16,80},{32,96},{48,112},{64,0},{80,16},{96,32},{112,48},{1... | collective-permute-start | bytes 3194888 | tf_op jit(solution)/shard_map/ppermute | solution.py:20
  128.0 4.1 %shard_map.87 = (bf16[2,1024,256]{2,1,0:T(8,128)(2,1)}, bf16[1024,256]{1,0:T(8,128)(2,1)}) custom-call(f32[8,128]{1,0:T(8,128)} %shard_map.84.total_ref, f32[1024,768]{1,0:T(8,128)} %copy-done.2, bf16[1024,1792]{1,0:T(8,128)(2,1)} %bitcast.26, bf16[1024,1792]{1,0:T(8,128)(2,1)} %bitcast.18, bf16[1024,1792]{1,0:T(8,128)(2,1)} %bitcast.34), custom_call_target="tpu_custom_call" | custom-call | flops 7864320 | bytes 4194304 | tf_op jit(solution)/shard_map/pallas_call | solution.py:216
  132.5 5.6 %shard_map.92 = (bf16[2,1024,384]{2,1,0:T(8,128)(2,1)}, bf16[1024,384]{1,0:T(8,128)(2,1)}) custom-call(f32[8,128]{1,0:T(8,128)} %shard_map.84.total_ref, f32[1024,768]{1,0:T(8,128)} %copy-done.3, bf16[1024,1792]{1,0:T(8,128)(2,1)} %bitcast.27, bf16[1024,1792]{1,0:T(8,128)(2,1)} %bitcast.19, bf16[1024,1792]{1,0:T(8,128)(2,1)} %bitcast.35), custom_call_target="tpu_custom_call" | custom-call | flops 11796480 | bytes 6291456 | tf_op jit(solution)/shard_map/pallas_call | solution.py:216
  138.1 14.9 %collective-permute-done.15.pair_other_ref.refs_1_.clip_other_ref = bf16[2,1040,256]{2,1,0:T(8,128)(2,1)S(1)} collective-permute-done((bf16[2,1040,256]{2,1,0:T(8,128)(2,1)}, bf16[2,1040,256]{2,1,0:T(8,128)(2,1)S(1)}, u32[]{:S(2)}, u32[]{:S(2)}) %collective-permute-start.15) | collective-permute-done | bytes 1064992 | tf_op jit(solution)/shard_map/ppermute | solution.py:20
  155.2 3.2 %collective-permute-start.17 = (bf16[2,1024,384]{2,1,0:T(8,128)(2,1)}, bf16[2,1024,384]{2,1,0:T(8,128)(2,1)S(1)}, u32[]{:S(2)}, u32[]{:S(2)}) collective-permute-start(bf16[2,1024,384]{2,1,0:T(8,128)(2,1)} %shard_map.93.pair_ref), channel_id=1, source_target_pairs={{0,64},{16,80},{32,96},{48,112},{64,0},{80,16},{96,32},{112,48},{1... | collective-permute-start | bytes 4718600 | tf_op jit(solution)/shard_map/ppermute | solution.py:20
  158.4 5.4 %shard_map.86 = (bf16[2,1024,384]{2,1,0:T(8,128)(2,1)}, bf16[1024,384]{1,0:T(8,128)(2,1)}) custom-call(f32[8,128]{1,0:T(8,128)} %shard_map.84.total_ref, f32[1024,768]{1,0:T(8,128)} %copy-done.3, bf16[1024,1792]{1,0:T(8,128)(2,1)} %bitcast.28, bf16[1024,1792]{1,0:T(8,128)(2,1)} %bitcast.20, bf16[1024,1792]{1,0:T(8,128)(2,1)} %bitcast.36), custom_call_target="tpu_custom_call" | custom-call | flops 11796480 | bytes 6291456 | tf_op jit(solution)/shard_map/pallas_call | solution.py:216
  163.8 3.5 %shard_map.90 = (bf16[1024,1792]{1,0:T(8,128)(2,1)}, bf16[1024,1792]{1,0:T(8,128)(2,1)}, bf16[1024,1792]{1,0:T(8,128)(2,1)}, f32[8,128]{1,0:T(8,128)}) custom-call(bf16[2,1040,256]{2,1,0:T(8,128)(2,1)} %shard_map.89.pair_ref, bf16[1024,256]{1,0:T(8,128)(2,1)} %get-tuple-element.55.step_ref, bf16[2,1040,256]{2,1,0:T(8,128)(2,1)} %copy-done.8, ...), custom_call_target="tpu_custom_call" | custom-call | flops 7864320 | bytes 4718592 | tf_op jit(solution)/shard_map/pallas_call | solution.py:231
  167.3 8.2 %collective-permute-done.13.refs_1_.pair_other_ref = bf16[2,1024,256]{2,1,0:T(8,128)(2,1)} collective-permute-done((bf16[2,1024,256]{2,1,0:T(8,128)(2,1)}, bf16[2,1024,256]{2,1,0:T(8,128)(2,1)}, u32[]{:S(2)}, u32[]{:S(2)}) %collective-permute-start.13) | collective-permute-done | bytes 1048608 | tf_op jit(solution)/shard_map/ppermute | solution.py:20
  176.8 3.2 %collective-permute-start.16 = (bf16[2,1024,384]{2,1,0:T(8,128)(2,1)}, bf16[2,1024,384]{2,1,0:T(8,128)(2,1)S(1)}, u32[]{:S(2)}, u32[]{:S(2)}) collective-permute-start(bf16[2,1024,384]{2,1,0:T(8,128)(2,1)} %shard_map.91.pair_ref), channel_id=1, source_target_pairs={{0,64},{16,80},{32,96},{48,112},{64,0},{80,16},{96,32},{112,48},{1... | collective-permute-start | bytes 4718600 | tf_op jit(solution)/shard_map/ppermute | solution.py:20
  180.0 2.9 %shard_map.98 = (bf16[2,1024,128]{2,1,0:T(8,128)(2,1)}, bf16[1024,128]{1,0:T(8,128)(2,1)}) custom-call(f32[8,128]{1,0:T(8,128)} %shard_map.84.total_ref, f32[1024,256]{1,0:T(8,128)} %copy-done.5, bf16[1024,1792]{1,0:T(8,128)(2,1)} %bitcast.29, bf16[1024,1792]{1,0:T(8,128)(2,1)} %bitcast.21, bf16[1024,1792]{1,0:T(8,128)(2,1)} %bitcast.37), custom_call_target="tpu_custom_call" | custom-call | flops 3932160 | bytes 2097152 | tf_op jit(solution)/shard_map/pallas_call | solution.py:216
  182.9 2.9 %shard_map.85 = (bf16[2,1024,128]{2,1,0:T(8,128)(2,1)}, bf16[1024,128]{1,0:T(8,128)(2,1)}) custom-call(f32[8,128]{1,0:T(8,128)} %shard_map.84.total_ref, f32[1024,256]{1,0:T(8,128)} %copy-done.5, bf16[1024,1792]{1,0:T(8,128)(2,1)} %bitcast.30, bf16[1024,1792]{1,0:T(8,128)(2,1)} %bitcast.22, bf16[1024,1792]{1,0:T(8,128)(2,1)} %bitcast.38), custom_call_target="tpu_custom_call" | custom-call | flops 3932160 | bytes 2097152 | tf_op jit(solution)/shard_map/pallas_call | solution.py:216
  185.7 3.4 %shard_map.94 = (bf16[1024,1792]{1,0:T(8,128)(2,1)}, bf16[1024,1792]{1,0:T(8,128)(2,1)}, bf16[1024,1792]{1,0:T(8,128)(2,1)}, f32[8,128]{1,0:T(8,128)}) custom-call(bf16[2,1024,256]{2,1,0:T(8,128)(2,1)} %get-tuple-element.53.pair_ref, bf16[1024,256]{1,0:T(8,128)(2,1)} %get-tuple-element.59.step_ref, ...), custom_call_target="tpu_custom_call", output_to_operand_aliasing={{0}: (4, {}), {1}: (5, {}), {2}: (6, {})} | custom-call | flops 7864320 | bytes 4718592 | tf_op jit(solution)/shard_map/pallas_call | solution.py:231
  189.2 6.2 %shard_map.95 = (bf16[1024,1792]{1,0:T(8,128)(2,1)}, bf16[1024,1792]{1,0:T(8,128)(2,1)}, bf16[1024,1792]{1,0:T(8,128)(2,1)}) custom-call(f32[8,128]{1,0:T(8,128)} %shard_map.84.total_ref, bf16[2,1040,256]{2,1,0:T(8,128)(2,1)} %copy-done.8, f32[1024,768]{1,0:T(8,128)} %copy-done.2, ...), custom_call_target="tpu_custom_call", output_to_operand_aliasing={{0}: (10, {}), {1}: (11, {}), {2}: (12, {})} | custom-call | flops 15728640 | bytes 5767168 | tf_op jit(solution)/shard_map/pallas_call | solution.py:252
  195.4 13.8 %collective-permute-done.17.pair_other_ref.refs_1_ = bf16[2,1024,384]{2,1,0:T(8,128)(2,1)S(1)} collective-permute-done((bf16[2,1024,384]{2,1,0:T(8,128)(2,1)}, bf16[2,1024,384]{2,1,0:T(8,128)(2,1)S(1)}, u32[]{:S(2)}, u32[]{:S(2)}) %collective-permute-start.17) | collective-permute-done | bytes 1572896 | tf_op jit(solution)/shard_map/ppermute | solution.py:20
  211.7 3.2 %collective-permute-start.19 = (bf16[2,1024,128]{2,1,0:T(8,128)(2,1)}, bf16[2,1024,128]{2,1,0:T(8,128)(2,1)S(1)}, u32[]{:S(2)}, u32[]{:S(2)}) collective-permute-start(bf16[2,1024,128]{2,1,0:T(8,128)(2,1)} %shard_map.99.pair_ref), channel_id=1, source_target_pairs={{0,64},{16,80},{32,96},{48,112},{64,0},{80,16},{96,32},{112,48},{1... | collective-permute-start | bytes 1572872 | tf_op jit(solution)/shard_map/ppermute | solution.py:20
  215.0 4.5 %shard_map.96 = (bf16[1024,1792]{1,0:T(8,128)(2,1)}, bf16[1024,1792]{1,0:T(8,128)(2,1)}, bf16[1024,1792]{1,0:T(8,128)(2,1)}, f32[8,128]{1,0:T(8,128)}) custom-call(bf16[2,1024,384]{2,1,0:T(8,128)(2,1)} %shard_map.93.pair_ref, bf16[1024,384]{1,0:T(8,128)(2,1)} %get-tuple-element.58.step_ref, ...), custom_call_target="tpu_custom_call", output_to_operand_aliasing={{0}: (4, {}), {1}: (5, {}), {2}: (6, {})} | custom-call | flops 11796480 | bytes 7077888 | tf_op jit(solution)/shard_map/pallas_call | solution.py:231
  219.5 23.4 %collective-permute-done.16.refs_1_.pair_other_ref = bf16[2,1024,384]{2,1,0:T(8,128)(2,1)S(1)} collective-permute-done((bf16[2,1024,384]{2,1,0:T(8,128)(2,1)}, bf16[2,1024,384]{2,1,0:T(8,128)(2,1)S(1)}, u32[]{:S(2)}, u32[]{:S(2)}) %collective-permute-start.16) | collective-permute-done | bytes 1572896 | tf_op jit(solution)/shard_map/ppermute | solution.py:20
  245.4 3.2 %collective-permute-start.18 = (bf16[2,1024,128]{2,1,0:T(8,128)(2,1)}, bf16[2,1024,128]{2,1,0:T(8,128)(2,1)S(1)}, u32[]{:S(2)}, u32[]{:S(2)}) collective-permute-start(bf16[2,1024,128]{2,1,0:T(8,128)(2,1)} %shard_map.97.pair_ref), channel_id=1, source_target_pairs={{0,64},{16,80},{32,96},{48,112},{64,0},{80,16},{96,32},{112,48},{1... | collective-permute-start | bytes 1572872 | tf_op jit(solution)/shard_map/ppermute | solution.py:20
  248.7 4.5 %shard_map.100 = (bf16[1024,1792]{1,0:T(8,128)(2,1)}, bf16[1024,1792]{1,0:T(8,128)(2,1)}, bf16[1024,1792]{1,0:T(8,128)(2,1)}, f32[8,128]{1,0:T(8,128)}) custom-call(bf16[2,1024,384]{2,1,0:T(8,128)(2,1)} %shard_map.91.pair_ref, bf16[1024,384]{1,0:T(8,128)(2,1)} %get-tuple-element.74.step_ref, ...), custom_call_target="tpu_custom_call", output_to_operand_aliasing={{0}: (4, {}), {1}: (5, {}), {2}: (6, {})} | custom-call | flops 11796480 | bytes 7077888 | tf_op jit(solution)/shard_map/pallas_call | solution.py:231
  254.9 2.6 shard_map.101
  257.5 5.7 %collective-permute-done.18.pair_other_ref = bf16[2,1024,128]{2,1,0:T(8,128)(2,1)S(1)} collective-permute-done((bf16[2,1024,128]{2,1,0:T(8,128)(2,1)}, bf16[2,1024,128]{2,1,0:T(8,128)(2,1)S(1)}, u32[]{:S(2)}, u32[]{:S(2)}) %collective-permute-start.18) | collective-permute-done | bytes 524320 | tf_op jit(solution)/shard_map/ppermute | solution.py:20
  264.0 2.6 shard_map.102
  (66 shorter events, 31.2 us)
Async XLA Ops:
  0.6 20.5 %collective-permute-start = (bf16[1024,256]{1,0:T(8,128)(2,1)}, bf16[1024,256]{1,0:T(8,128)(2,1)S(1)}, u32[]{:S(2)}, u32[]{:S(2)}) collective-permute-start(bf16[1024,256]{1,0:T(8,128)(2,1)} %bitcast.45), channel_id=1, source_target_pairs={{0,0},{1,1},{2,2},{3,3},{4,10},{5,11},{6,8},{7,9},{8,6},{9,7},{10,... | collective-permute-start | bytes 1572872 | tf_op jit(solution)/shard_map/ppermute | solution.py:59
  6.4 90.0 %collective-permute-start.6 = (bf16[1024,1792]{1,0:T(8,128)(2,1)}, bf16[1024,1792]{1,0:T(8,128)(2,1)}, u32[]{:S(2)}, u32[]{:S(2)}) collective-permute-start(bf16[1024,1792]{1,0:T(8,128)(2,1)} %bitcast.32), channel_id=1, source_target_pairs={{0,64},{16,80},{32,96},{48,112},{64,0},{80,16},{96,32},{112,48},{1... | collective-permute-start | bytes 11010056 | tf_op jit(solution)/shard_map/ppermute | solution.py:20
  14.1 39.2 %collective-permute-start.1 = (bf16[1024,768]{1,0:T(8,128)(2,1)}, bf16[1024,768]{1,0:T(8,128)(2,1)}, u32[]{:S(2)}, u32[]{:S(2)}) collective-permute-start(bf16[1024,768]{1,0:T(8,128)(2,1)} %get-tuple-element.88.u_ref), channel_id=1, source_target_pairs={{0,8},{8,0},{1,9},{9,1},{2,10},{10,2},{3,11},{11,3},{4,12},{12,4},... | collective-permute-start | bytes 4718600 | tf_op jit(solution)/shard_map/ppermute | solution.py:24
  22.6 30.7 %all-to-all-start = ((bf16[4,1024,256]{2,1,0:T(8,128)(2,1)}), bf16[4,1024,256]{2,1,0:T(8,128)(2,1)S(1)}, u32[]{:S(2)}, u32[]{:S(2)}) async-start(bf16[4,1024,256]{2,1,0:T(8,128)(2,1)} %broadcast_in_dim.12), calls=%async_computation | async-start | bytes 4194304 | tf_op jit(solution)/shard_map/all_to_all | solution.py:64
  26.2 60.7 %collective-permute-start.4 = (bf16[1024,768]{1,0:T(8,128)(2,1)}, bf16[1024,768]{1,0:T(8,128)(2,1)}, u32[]{:S(2)}, u32[]{:S(2)}) collective-permute-start(bf16[1024,768]{1,0:T(8,128)(2,1)} %get-tuple-element.87.u_ref), channel_id=1, source_target_pairs={{0,8},{8,0},{1,9},{9,1},{2,10},{10,2},{3,11},{11,3},{4,12},{12,4},... | collective-permute-start | bytes 4718600 | tf_op jit(solution)/shard_map/ppermute | solution.py:24
  53.3 1.3 copy-start
  57.9 13.3 %copy-start.1 = (bf16[4,1024,256]{2,1,0:T(8,128)(2,1)S(1)}, bf16[4,1024,256]{2,1,0:T(8,128)(2,1)}, u32[]{:S(2)}) copy-start(bf16[4,1024,256]{2,1,0:T(8,128)(2,1)} %shard_map.76.near_ref) | copy-start | bytes 6291460
  57.9 8.2 %collective-permute-start.2 = (bf16[2,1024,256]{2,1,0:T(8,128)(2,1)S(1)}, bf16[2,1024,256]{2,1,0:T(8,128)(2,1)S(1)}, u32[]{:S(2)}, u32[]{:S(2)}) collective-permute-start(bf16[2,1024,256]{2,1,0:T(8,128)(2,1)S(1)} %get-tuple-element.90), channel_id=1, source_target_pairs={{0,1},{1,0},{2,3},{3,2},{4,5},{5,4},{6,7},{7,6},{8,9},{9,8},{10,11... | collective-permute-start | bytes 3145736 | tf_op jit(solution)/shard_map/ppermute | solution.py:50
  57.9 13.3 %collective-permute-start.3 = (bf16[2,1024,256]{2,1,0:T(8,128)(2,1)}, bf16[2,1024,256]{2,1,0:T(8,128)(2,1)}, u32[]{:S(2)}, u32[]{:S(2)}) collective-permute-start(bf16[2,1024,256]{2,1,0:T(8,128)(2,1)} %get-tuple-element.89), channel_id=1, source_target_pairs={{0,1},{1,0},{2,3},{3,2},{4,5},{5,4},{6,7},{7,6},{8,9},{9,8},{10,11... | collective-permute-start | bytes 3145736 | tf_op jit(solution)/shard_map/ppermute | solution.py:50
  61.7 51.6 %collective-permute-start.12 = (bf16[1024,512]{1,0:T(8,128)(2,1)}, bf16[1024,512]{1,0:T(8,128)(2,1)}, u32[]{:S(2)}, u32[]{:S(2)}) collective-permute-start(bf16[1024,512]{1,0:T(8,128)(2,1)} %pad_maximum_fusion), channel_id=1, source_target_pairs={{0,64},{16,80},{32,96},{48,112},{64,0},{80,16},{96,32},{112,48},{1... | collective-permute-start | bytes 3145736 | tf_op jit(solution)/shard_map/ppermute | solution.py:20
  66.2 1.0 copy-start.6
  67.1 29.3 %collective-permute-start.5 = (bf16[1024,256]{1,0:T(8,128)(2,1)S(1)}, bf16[1024,256]{1,0:T(8,128)(2,1)S(1)}, u32[]{:S(2)}, u32[]{:S(2)}) collective-permute-start(bf16[1024,256]{1,0:T(8,128)(2,1)S(1)} %slice.37.u_ref), channel_id=1, source_target_pairs={{0,8},{8,0},{1,9},{9,1},{2,10},{10,2},{3,11},{11,3},{4,12},{12,4},... | collective-permute-start | bytes 1572872 | tf_op jit(solution)/shard_map/ppermute | solution.py:24
  71.2 1.2 copy-start.7
  77.9 4.4 %copy-start.4 = (bf16[1024,768]{1,0:T(8,128)(2,1)S(1)}, bf16[1024,768]{1,0:T(8,128)(2,1)}, u32[]{:S(2)}) copy-start(bf16[1024,768]{1,0:T(8,128)(2,1)} %get-tuple-element.87.u_ref) | copy-start | bytes 4718596
  82.1 2.7 %copy-start.2 = (f32[1024,768]{1,0:T(8,128)}, f32[1024,768]{1,0:T(8,128)S(1)}, u32[]{:S(2)}) copy-start(f32[1024,768]{1,0:T(8,128)S(1)} %get-tuple-element.52.grad_ref) | copy-start | bytes 9437188
  82.2 41.2 %collective-permute-start.14 = (bf16[1024,256]{1,0:T(8,128)(2,1)S(1)}, bf16[1024,256]{1,0:T(8,128)(2,1)S(1)}, u32[]{:S(2)}, u32[]{:S(2)}) collective-permute-start(bf16[1024,256]{1,0:T(8,128)(2,1)S(1)} %slice.42), channel_id=1, source_target_pairs={{0,64},{16,80},{32,96},{48,112},{64,0},{80,16},{96,32},{112,48},{1... | collective-permute-start | bytes 1572872 | tf_op jit(solution)/shard_map/ppermute | solution.py:20
  91.0 1.7 copy-start.3
  98.7 1.0 copy-start.5
  99.7 1.2 collective-permute-start.7
  100.9 4.8 %collective-permute-start.10 = (f32[8,128]{1,0:T(8,128)S(1)}, f32[8,128]{1,0:T(8,128)S(1)}, u32[]{:S(2)}, u32[]{:S(2)}) collective-permute-start(f32[8,128]{1,0:T(8,128)S(1)} %add.34), channel_id=1, source_target_pairs={{0,6},{1,7},{2,4},{3,5},{4,2},{5,3},{6,0},{7,1},{8,14},{9,15},{10,... | collective-permute-start | bytes 12296 | tf_op jit(solution)/shard_map/ppermute | solution.py:50
  103.6 3.6 %collective-permute-start.8 = (f32[8,128]{1,0:T(8,128)S(1)}, f32[8,128]{1,0:T(8,128)S(1)}, u32[]{:S(2)}, u32[]{:S(2)}) collective-permute-start(f32[8,128]{1,0:T(8,128)S(1)} %add.34), channel_id=1, source_target_pairs={{0,2},{1,3},{2,0},{3,1},{4,6},{5,7},{6,4},{7,5},{8,10},{9,11},{10,... | collective-permute-start | bytes 12296 | tf_op jit(solution)/shard_map/ppermute | solution.py:50
  104.0 5.1 %collective-permute-start.9 = (f32[8,128]{1,0:T(8,128)S(1)}, f32[8,128]{1,0:T(8,128)S(1)}, u32[]{:S(2)}, u32[]{:S(2)}) collective-permute-start(f32[8,128]{1,0:T(8,128)S(1)} %add.34), channel_id=1, source_target_pairs={{0,4},{1,5},{2,6},{3,7},{4,0},{5,1},{6,2},{7,3},{8,12},{9,13},{10,... | collective-permute-start | bytes 12296 | tf_op jit(solution)/shard_map/ppermute | solution.py:50
  109.1 5.1 %copy-start.14 = (f32[8,128]{1,0:T(8,128)}, f32[8,128]{1,0:T(8,128)S(1)}, u32[]{:S(2)}) copy-start(f32[8,128]{1,0:T(8,128)S(1)} %add_add_fusion.one_ref) | copy-start | bytes 12292
  109.1 5.1 %collective-permute-start.11 = (f32[8,128]{1,0:T(8,128)S(1)}, f32[8,128]{1,0:T(8,128)S(1)}, u32[]{:S(2)}, u32[]{:S(2)}) collective-permute-start(f32[8,128]{1,0:T(8,128)S(1)} %add_add_fusion.one_ref), channel_id=1, source_target_pairs={{0,8},{8,0},{1,9},{9,1},{2,10},{10,2},{3,11},{11,3},{4,12},{12,4},... | collective-permute-start | bytes 12296 | tf_op jit(solution)/shard_map/ppermute | solution.py:24
  114.2 0.6 copy-start.15
  123.3 0.8 copy-start.11
  124.8 28.2 %collective-permute-start.15 = (bf16[2,1040,256]{2,1,0:T(8,128)(2,1)}, bf16[2,1040,256]{2,1,0:T(8,128)(2,1)S(1)}, u32[]{:S(2)}, u32[]{:S(2)}) collective-permute-start(bf16[2,1040,256]{2,1,0:T(8,128)(2,1)} %shard_map.89.pair_ref), channel_id=1, source_target_pairs={{0,64},{16,80},{32,96},{48,112},{64,0},{80,16},{96,32},{112,48},{1... | collective-permute-start | bytes 3194888 | tf_op jit(solution)/shard_map/ppermute | solution.py:20
  132.2 43.4 %collective-permute-start.13 = (bf16[2,1024,256]{2,1,0:T(8,128)(2,1)}, bf16[2,1024,256]{2,1,0:T(8,128)(2,1)}, u32[]{:S(2)}, u32[]{:S(2)}) collective-permute-start(bf16[2,1024,256]{2,1,0:T(8,128)(2,1)} %get-tuple-element.53.pair_ref), channel_id=1, source_target_pairs={{0,64},{16,80},{32,96},{48,112},{64,0},{80,16},{96,32},{112,48},{1... | collective-permute-start | bytes 3145736 | tf_op jit(solution)/shard_map/ppermute | solution.py:20
  153.0 1.0 copy-start.8
  155.2 54.0 %collective-permute-start.17 = (bf16[2,1024,384]{2,1,0:T(8,128)(2,1)}, bf16[2,1024,384]{2,1,0:T(8,128)(2,1)S(1)}, u32[]{:S(2)}, u32[]{:S(2)}) collective-permute-start(bf16[2,1024,384]{2,1,0:T(8,128)(2,1)} %shard_map.93.pair_ref), channel_id=1, source_target_pairs={{0,64},{16,80},{32,96},{48,112},{64,0},{80,16},{96,32},{112,48},{1... | collective-permute-start | bytes 4718600 | tf_op jit(solution)/shard_map/ppermute | solution.py:20
  176.8 66.1 %collective-permute-start.16 = (bf16[2,1024,384]{2,1,0:T(8,128)(2,1)}, bf16[2,1024,384]{2,1,0:T(8,128)(2,1)S(1)}, u32[]{:S(2)}, u32[]{:S(2)}) collective-permute-start(bf16[2,1024,384]{2,1,0:T(8,128)(2,1)} %shard_map.91.pair_ref), channel_id=1, source_target_pairs={{0,64},{16,80},{32,96},{48,112},{64,0},{80,16},{96,32},{112,48},{1... | collective-permute-start | bytes 4718600 | tf_op jit(solution)/shard_map/ppermute | solution.py:20
  209.1 1.2 copy-start.10
  211.7 42.3 %collective-permute-start.19 = (bf16[2,1024,128]{2,1,0:T(8,128)(2,1)}, bf16[2,1024,128]{2,1,0:T(8,128)(2,1)S(1)}, u32[]{:S(2)}, u32[]{:S(2)}) collective-permute-start(bf16[2,1024,128]{2,1,0:T(8,128)(2,1)} %shard_map.99.pair_ref), channel_id=1, source_target_pairs={{0,64},{16,80},{32,96},{48,112},{64,0},{80,16},{96,32},{112,48},{1... | collective-permute-start | bytes 1572872 | tf_op jit(solution)/shard_map/ppermute | solution.py:20
  242.8 1.2 copy-start.9
  245.4 17.8 %collective-permute-start.18 = (bf16[2,1024,128]{2,1,0:T(8,128)(2,1)}, bf16[2,1024,128]{2,1,0:T(8,128)(2,1)S(1)}, u32[]{:S(2)}, u32[]{:S(2)}) collective-permute-start(bf16[2,1024,128]{2,1,0:T(8,128)(2,1)} %shard_map.97.pair_ref), channel_id=1, source_target_pairs={{0,64},{16,80},{32,96},{48,112},{64,0},{80,16},{96,32},{112,48},{1... | collective-permute-start | bytes 1572872 | tf_op jit(solution)/shard_map/ppermute | solution.py:20
  254.1 0.8 copy-start.12
  263.2 0.8 copy-start.13

commit v4 on v3

--- a/solution.py
+++ b/solution.py
@@ -1,3 +1,5 @@
+import functools
+
 import jax
 import jax.numpy as jnp
 from jax import lax
@@ -43,6 +45,7 @@
         out_specs=[ANYWHERE] * len(values),
         input_output_aliases={i: i for i in range(len(values))},
         cost_estimate=pl.CostEstimate(flops=0, bytes_accessed=size, transcendentals=0),
+        compiler_params=pltpu.CompilerParams(vmem_limit_bytes=4 * 2**20),
     )(*values, *earlier)
 
 
@@ -102,6 +105,7 @@
         in_specs=[corner(value)] * 2 + [corner(item) for item in earlier],
         out_specs=corner(value),
         cost_estimate=SLIGHT,
+        compiler_params=pltpu.CompilerParams(vmem_limit_bytes=4 * 2**20),
     )(value, swap_dp(value), *earlier)
 
 
@@ -133,40 +137,40 @@
     step_ref[...] = stepped(old_ref[...], one, two)
 
 
-def make_first_kernel(total_ref, grad_ref, first_ref, second_ref, old_ref, pair_ref, step_ref):
+def make_first_kernel(total_ref, grad_ref, first_ref, second_ref, pair_ref):
     rows = grad_ref.shape[0]
     clip = clip_of(total_ref)
     one, two = moments(clip * grad_ref[...], first_ref[...], second_ref[...])
     pair_ref[0, :rows] = one
     pair_ref[1, :rows] = two
-    step_ref[...] = stepped(old_ref[...], one, two)
     clip = jnp.broadcast_to(clip, (16, grad_ref.shape[1]))
     high = clip.astype(BF16)
     pair_ref[0, rows:] = high
     pair_ref[1, rows:] = (clip - high.astype(F32)).astype(BF16)
 
 
-def make_first(total, grad, within, first, second, old, at, width):
-    rows = grad.shape[0]
+def make_first(total, grad, within, first, second):
+    rows, width = first.shape
     chosen = lambda start: pl.BlockSpec((rows, width), lambda i: (0, start // width))
     return pl.pallas_call(
         make_first_kernel,
         grid=(1,),
-        out_shape=(jax.ShapeDtypeStruct((2, rows + 16, width), BF16), jax.ShapeDtypeStruct((rows, width), BF16)),
-        in_specs=[TOTAL, chosen(within), chosen(at), chosen(at), chosen(at)],
-        out_specs=(pl.BlockSpec((2, rows + 16, width), lambda i: (0, 0, 0)), chosen(0)),
+        out_shape=jax.ShapeDtypeStruct((2, rows + 16, width), BF16),
+        in_specs=[TOTAL, chosen(within), chosen(0), chosen(0)],
+        out_specs=pl.BlockSpec((2, rows + 16, width), lambda i: (0, 0, 0)),
         cost_estimate=cost(rows, width, 30, 16),
-        compiler_params=pltpu.CompilerParams(vmem_limit_bytes=56 * 2**20),
-    )(total, grad, first, second, old)
-
-
-def mix_kernel(pair_ref, step_ref, pair_other_ref, old_other_ref, *rest):
+        compiler_params=pltpu.CompilerParams(vmem_limit_bytes=24 * 2**20),
+    )(total, grad, first, second)
+
+
+def mix_kernel(ready, pair_ref, step_ref, pair_other_ref, old_other_ref, *rest):
     w_ref, one_ref, two_ref, flag_ref = rest[-4:]
     flag_ref[...] = jnp.zeros_like(flag_ref)
     depth = step_ref.shape[0]
     here = pl.ds(pl.multiple_of(pl.program_id(0) * depth, depth), depth)
     one_other, two_other = pair_other_ref[0, here], pair_other_ref[1, here]
-    w_ref[...] = mean(step_ref[...], stepped(old_other_ref[...], one_other, two_other))
+    step = step_ref[...] if ready else stepped(step_ref[...], pair_ref[0], pair_ref[1])
+    w_ref[...] = mean(step, stepped(old_other_ref[...], one_other, two_other))
     one_ref[...] = mean(pair_ref[0], one_other)
     two_ref[...] = mean(pair_ref[1], two_other)
 
@@ -223,13 +227,13 @@
     )(total, grad, first, second, old)
 
 
-def mix(pair, step, pair_other, old_other, at, width, shape, outs):
+def mix(pair, step, ready, pair_other, old_other, at, width, shape, outs):
     rows = shape[0]
     depth = rows if width == 128 else STEP_ROWS
     wide = pl.BlockSpec((depth, width), lambda i: (i, at // width))
     whole = jax.ShapeDtypeStruct(shape, BF16)
     return pl.pallas_call(
-        mix_kernel,
+        functools.partial(mix_kernel, ready),
         grid=(rows // depth,),
         out_shape=(whole, whole, whole, jax.ShapeDtypeStruct((8, 128), F32)),
         in_specs=[
@@ -242,6 +246,7 @@
         out_specs=(wide, wide, wide, TOTAL),
         input_output_aliases={4 + i: i for i in range(len(outs))},
         cost_estimate=cost(rows, width, 30, 18),
+        compiler_params=pltpu.CompilerParams(vmem_limit_bytes=16 * 2**20),
     )(pair, step, pair_other, old_other, *outs)
 
 
@@ -335,7 +340,7 @@
     old_other = across(old)
     state_other = across(jnp.concatenate([first[:, :EARLY], second[:, :EARLY]], axis=1))
 
-    (near,) = gate((along_y(settled),), (up_other[0],))
+    near, *leading = gate((along_y(settled), *(part(value, LATE[0]) for value in (first, second))), (up_other[0],))
     features = assemble(near, turned(near[:2], 1), turned(near[2:], 1))
     grads, squares = [], jnp.zeros((8, 128), F32)
     for i, (piece, other) in enumerate(zip(up, up_other)):
@@ -351,8 +356,10 @@
         if i < len(LATE):
             at, width = LATE[i]
             chunk, within = holder(UP, at)
-            build = make if i else make_first
-            pair, step = build(total, grads[chunk], within, first, second, old, at, width)
+            if i:
+                pair, step = make(total, grads[chunk], within, first, second, old, at, width)
+            else:
+                pair, step = make_first(total, grads[chunk], within, *leading), part(old, LATE[0])
             if i == 0:
                 (pair,) = gate((pair,), (grad_other,))
             elif i > 1:
@@ -363,7 +370,7 @@
         if i >= 2:
             j = i - 2
             at, width = LATE[j]
-            *outs, flag = mix(pairs[j], steps[j], received[j], old_other, at, width, old.shape, outs)
+            *outs, flag = mix(pairs[j], steps[j], j > 0, received[j], old_other, at, width, old.shape, outs)
             flags.append(flag)
         if i == 3:
             outs = early(total, received[0], grads[0], grad_other, first, second, state_other, old, old_other, EARLY, outs)

time: 268 us -> 266 us (level)
  Pallas kernels: 80.8 us -> 72 us
  waiting for transfers between devices: 114 us -> 122 us
    ppermute x9, waiting for transfers between devices: 71.5 us -> 79.9 us  [across(): return lax.ppermute(value, 'replica', [(s, s ^ 4) for s in range(8)])]
    pallas_call x7, Pallas kernels: 25.9 us -> 20.9 us  [the longest x6 19.1 us: mix(): pl.pallas_call(functools.partial(mix_kernel, ready), grid=(rows // depth,...]
    pallas_call x6, Pallas kernels: 6.63 us -> 2 us  [gate(): pl.pallas_call(nothing_kernel, grid=(1,), out_shape=[jax.ShapeDtypeStruct...]
    unnamed x32 -> x38, local copies, waits for them, and re-layouts: 12.5 us -> 9.11 us
    slice x2 -> x3, local copies, waits for them, and re-layouts: 4.83 us -> 7.49 us  [part(): return value[:, piece[0]:piece[0] + piece[1]]]
  transfers between devices with their start and end apart: 21 -> 21, of which waited for: 17 -> 17; matrix products, arithmetic and copies ran while one was open for 5% -> 5% of each run, Pallas kernels for 29% -> 26%
where the time goes in v4:
time: 266 us; the launch traced here: 265 us
  waiting for transfers between devices  122 us (46%)
  Pallas kernels  72 us (27%)
  starting transfers between devices  47.3 us (18%)
  local copies, waits for them, and re-layouts  21.9 us (8%)
    ppermute x9, waiting for transfers between devices, across(): return lax.ppermute(value, 'replica', [(s, s ^ 4) for s in range(8)])  79.9 us
    ppermute x4, waiting for transfers between devices, swap_dp(): return lax.ppermute(value, 'dp', [(0, 1), (1, 0)])  29.9 us
    ppermute x9, starting transfers between devices, across(): return lax.ppermute(value, 'replica', [(s, s ^ 4) for s in range(8)])  24.6 us
    pallas_call x5, Pallas kernels, make(): pl.pallas_call(make_kernel, grid=(rows // STEP_ROWS,), out_shape=(jax.Sha...  21 us
    pallas_call x6, Pallas kernels, mix(): pl.pallas_call(functools.partial(mix_kernel, ready), grid=(rows // depth,...  19.1 us
    pallas_call x3, Pallas kernels, finish(): pl.pallas_call(finish_kernel, grid=(blocks // 2,), out_shape=(jax.ShapeDt...  10.8 us
    unnamed x38, local copies, waits for them, and re-layouts  9.11 us
    pallas_call x3, Pallas kernels, local_product(): pl.pallas_call(local_kernel, grid=(blocks // 2,), out_shape=jax.ShapeDtyp...  8.94 us
  transfers between devices with their start and end apart: 21, of which 17 were waited for; matrix products, arithmetic and copies ran while one was open for 5% of the time, Pallas kernels for 26%

profile of v4, /device:TPU:6, one launch (start us, length us, event | category | flops | bytes accessed | tf_op | source)
XLA Modules:
  0.0 264.8 jit_solution(5734628823235048626)
XLA Ops:
  0.6 5.8 %collective-permute-start = (bf16[1024,256]{1,0:T(8,128)(2,1)}, bf16[1024,256]{1,0:T(8,128)(2,1)S(1)}, u32[]{:S(2)}, u32[]{:S(2)}) collective-permute-start(bf16[1024,256]{1,0:T(8,128)(2,1)} %bitcast.43), channel_id=1, source_target_pairs={{0,0},{1,1},{2,2},{3,3},{4,10},{5,11},{6,8},{7,9},{8,6},{9,7},{10,... | collective-permute-start | bytes 1572872 | tf_op jit(solution)/shard_map/ppermute | solution.py:62
  6.4 4.0 %collective-permute-start.6 = (bf16[1024,1792]{1,0:T(8,128)(2,1)}, bf16[1024,1792]{1,0:T(8,128)(2,1)}, u32[]{:S(2)}, u32[]{:S(2)}) collective-permute-start(bf16[1024,1792]{1,0:T(8,128)(2,1)} %bitcast.30), channel_id=1, source_target_pairs={{0,64},{16,80},{32,96},{48,112},{64,0},{80,16},{96,32},{112,48},{1... | collective-permute-start | bytes 11010056 | tf_op jit(solution)/shard_map/ppermute | solution.py:22
  10.4 3.8 %fusion.2 = (bf16[1024,768]{1,0:T(8,128)(2,1)}, bf16[1024,768]{1,0:T(8,128)(2,1)}) fusion(bf16[1024,1792]{1,0:T(8,128)(2,1)} %bitcast.41), kind=kLoop, calls=%fused_computation.11 | loop fusion | bytes 6291456 | tf_op jit(solution)/shard_map/slice | solution.py:325
  14.1 7.0 %collective-permute-done = bf16[1024,256]{1,0:T(8,128)(2,1)S(1)} collective-permute-done((bf16[1024,256]{1,0:T(8,128)(2,1)}, bf16[1024,256]{1,0:T(8,128)(2,1)S(1)}, u32[]{:S(2)}, u32[]{:S(2)}) %collective-permute-start) | collective-permute-done | bytes 524320 | tf_op jit(solution)/shard_map/ppermute | solution.py:62
  22.6 3.6 %all-to-all-start = ((bf16[4,1024,256]{2,1,0:T(8,128)(2,1)}), bf16[4,1024,256]{2,1,0:T(8,128)(2,1)S(1)}, u32[]{:S(2)}, u32[]{:S(2)}) async-start(bf16[4,1024,256]{2,1,0:T(8,128)(2,1)} %broadcast_in_dim.12), calls=%async_computation | async-start | bytes 4194304 | tf_op jit(solution)/shard_map/all_to_all | solution.py:67
  26.2 2.1 collective-permute-start.4
  28.3 2.6 fusion
  30.9 22.3 %collective-permute-done.1.refs_3_.u_ref = bf16[1024,768]{1,0:T(8,128)(2,1)} collective-permute-done((bf16[1024,768]{1,0:T(8,128)(2,1)}, bf16[1024,768]{1,0:T(8,128)(2,1)}, u32[]{:S(2)}, u32[]{:S(2)}) %collective-permute-start.1) | collective-permute-done | bytes 1572896 | tf_op jit(solution)/shard_map/ppermute | solution.py:26
  56.7 3.3 %collective-permute-start.12 = (bf16[1024,512]{1,0:T(8,128)(2,1)}, bf16[1024,512]{1,0:T(8,128)(2,1)}, u32[]{:S(2)}, u32[]{:S(2)}) collective-permute-start(bf16[1024,512]{1,0:T(8,128)(2,1)} %pad_maximum_fusion), channel_id=1, source_target_pairs={{0,64},{16,80},{32,96},{48,112},{64,0},{80,16},{96,32},{112,48},{1... | collective-permute-start | bytes 3145736 | tf_op jit(solution)/shard_map/ppermute | solution.py:22
  60.1 1.9 slice.49.u_ref
  62.9 4.0 %collective-permute-start.5 = (bf16[1024,256]{1,0:T(8,128)(2,1)}, bf16[1024,256]{1,0:T(8,128)(2,1)}, u32[]{:S(2)}, u32[]{:S(2)}) collective-permute-start(bf16[1024,256]{1,0:T(8,128)(2,1)} %slice.49.u_ref), channel_id=1, source_target_pairs={{0,8},{8,0},{1,9},{9,1},{2,10},{10,2},{3,11},{11,3},{4,12},{12,4},... | collective-permute-start | bytes 1572872 | tf_op jit(solution)/shard_map/ppermute | solution.py:26
  69.7 3.9 %shard_map.78.local_ref = f32[1024,768]{1,0:T(8,128)S(1)} custom-call(bf16[8,1024,256]{2,1,0:T(8,128)(2,1)S(1)} %shard_map.77.x_ref, bf16[1024,768]{1,0:T(8,128)(2,1)} %get-tuple-element.94.u_ref), custom_call_target="tpu_custom_call" | custom-call | bytes 4096 | tf_op jit(solution)/shard_map/pallas_call | solution.py:279
  73.7 4.1 %shard_map.79 = (f32[1024,768]{1,0:T(8,128)S(1)}, f32[8,128]{1,0:T(8,128)S(1)}) custom-call(bf16[8,1024,256]{2,1,0:T(8,128)(2,1)S(1)} %shard_map.77.x_ref, bf16[1024,768]{1,0:T(8,128)(2,1)} %collective-permute-done.1.refs_3_.u_ref, f32[1024,768]{1,0:T(8,128)S(1)} %shard_map.78.local_ref), custom_call_target="tpu_custom_call" | custom-call | bytes 4096 | tf_op jit(solution)/shard_map/pallas_call | solution.py:308
  78.7 2.5 shard_map.80.local_ref
  81.2 2.5 shard_map.82.local_ref
  83.7 3.3 %collective-permute-done.4.u_ref = bf16[1024,768]{1,0:T(8,128)(2,1)} collective-permute-done((bf16[1024,768]{1,0:T(8,128)(2,1)}, bf16[1024,768]{1,0:T(8,128)(2,1)}, u32[]{:S(2)}, u32[]{:S(2)}) %collective-permute-start.4) | collective-permute-done | bytes 1572896 | tf_op jit(solution)/shard_map/ppermute | solution.py:26
  87.0 4.0 %shard_map.81 = (f32[1024,768]{1,0:T(8,128)S(1)}, f32[8,128]{1,0:T(8,128)S(1)}) custom-call(bf16[8,1024,256]{2,1,0:T(8,128)(2,1)S(1)} %shard_map.77.x_ref, bf16[1024,768]{1,0:T(8,128)(2,1)} %collective-permute-done.4.u_ref, f32[1024,768]{1,0:T(8,128)S(1)} %shard_map.80.local_ref), custom_call_target="tpu_custom_call" | custom-call | bytes 4096 | tf_op jit(solution)/shard_map/pallas_call | solution.py:308
  92.7 3.9 %collective-permute-done.5.u_ref = bf16[1024,256]{1,0:T(8,128)(2,1)} collective-permute-done((bf16[1024,256]{1,0:T(8,128)(2,1)}, bf16[1024,256]{1,0:T(8,128)(2,1)}, u32[]{:S(2)}, u32[]{:S(2)}) %collective-permute-start.5) | collective-permute-done | bytes 524320 | tf_op jit(solution)/shard_map/ppermute | solution.py:26
  96.5 2.6 shard_map.83
  100.4 2.8 %collective-permute-start.10 = (f32[8,128]{1,0:T(8,128)S(1)}, f32[8,128]{1,0:T(8,128)S(1)}, u32[]{:S(2)}, u32[]{:S(2)}) collective-permute-start(f32[8,128]{1,0:T(8,128)S(1)} %add.34), channel_id=1, source_target_pairs={{0,6},{1,7},{2,4},{3,5},{4,2},{5,3},{6,0},{7,1},{8,14},{9,15},{10,... | collective-permute-start | bytes 12296 | tf_op jit(solution)/shard_map/ppermute | solution.py:53
  106.8 1.9 collective-permute-done.9
  108.7 2.0 collective-permute-start.11
  110.7 2.6 collective-permute-done.12.rest_0_.first_other_ref.second_other_ref
  116.3 7.0 %collective-permute-done.14.refs_1_.grad_other_ref = bf16[1024,256]{1,0:T(8,128)(2,1)S(1)} collective-permute-done((bf16[1024,256]{1,0:T(8,128)(2,1)S(1)}, bf16[1024,256]{1,0:T(8,128)(2,1)S(1)}, u32[]{:S(2)}, u32[]{:S(2)}) %collective-permute-start.14) | collective-permute-done | bytes 524320 | tf_op jit(solution)/shard_map/ppermute | solution.py:22
  124.1 3.2 %collective-permute-start.15 = (bf16[2,1040,256]{2,1,0:T(8,128)(2,1)}, bf16[2,1040,256]{2,1,0:T(8,128)(2,1)S(1)}, u32[]{:S(2)}, u32[]{:S(2)}) collective-permute-start(bf16[2,1040,256]{2,1,0:T(8,128)(2,1)} %shard_map.89.pair_ref), channel_id=1, source_target_pairs={{0,64},{16,80},{32,96},{48,112},{64,0},{80,16},{96,32},{112,48},{1... | collective-permute-start | bytes 3194888 | tf_op jit(solution)/shard_map/ppermute | solution.py:22
  127.4 4.1 %shard_map.87 = (bf16[2,1024,256]{2,1,0:T(8,128)(2,1)}, bf16[1024,256]{1,0:T(8,128)(2,1)}) custom-call(f32[8,128]{1,0:T(8,128)} %copy-done.16, f32[1024,768]{1,0:T(8,128)} %copy-done, bf16[1024,1792]{1,0:T(8,128)(2,1)} %bitcast.17, bf16[1024,1792]{1,0:T(8,128)(2,1)} %bitcast.24, bf16[1024,1792]{1,0:T(8,128)(2,1)} %bitcast.31), custom_call_target="tpu_custom_call" | custom-call | flops 7864320 | bytes 4194304 | tf_op jit(solution)/shard_map/pallas_call | solution.py:220
  131.7 1.9 slice.53.step_ref
  133.6 5.8 %shard_map.92 = (bf16[2,1024,384]{2,1,0:T(8,128)(2,1)}, bf16[1024,384]{1,0:T(8,128)(2,1)}) custom-call(f32[8,128]{1,0:T(8,128)} %copy-done.16, f32[1024,768]{1,0:T(8,128)} %copy-done.1, bf16[1024,1792]{1,0:T(8,128)(2,1)} %bitcast.18, bf16[1024,1792]{1,0:T(8,128)(2,1)} %bitcast.25, bf16[1024,1792]{1,0:T(8,128)(2,1)} %bitcast.33), custom_call_target="tpu_custom_call" | custom-call | flops 11796480 | bytes 6291456 | tf_op jit(solution)/shard_map/pallas_call | solution.py:220
  139.4 12.9 %collective-permute-done.15.pair_other_ref.refs_1_.clip_other_ref = bf16[2,1040,256]{2,1,0:T(8,128)(2,1)S(1)} collective-permute-done((bf16[2,1040,256]{2,1,0:T(8,128)(2,1)}, bf16[2,1040,256]{2,1,0:T(8,128)(2,1)S(1)}, u32[]{:S(2)}, u32[]{:S(2)}) %collective-permute-start.15) | collective-permute-done | bytes 1064992 | tf_op jit(solution)/shard_map/ppermute | solution.py:22
  152.3 3.2 %collective-permute-start.17 = (bf16[2,1024,384]{2,1,0:T(8,128)(2,1)}, bf16[2,1024,384]{2,1,0:T(8,128)(2,1)S(1)}, u32[]{:S(2)}, u32[]{:S(2)}) collective-permute-start(bf16[2,1024,384]{2,1,0:T(8,128)(2,1)} %shard_map.93.pair_ref), channel_id=1, source_target_pairs={{0,64},{16,80},{32,96},{48,112},{64,0},{80,16},{96,32},{112,48},{1... | collective-permute-start | bytes 4718600 | tf_op jit(solution)/shard_map/ppermute | solution.py:22
  155.5 5.5 %shard_map.86 = (bf16[2,1024,384]{2,1,0:T(8,128)(2,1)}, bf16[1024,384]{1,0:T(8,128)(2,1)}) custom-call(f32[8,128]{1,0:T(8,128)} %copy-done.16, f32[1024,768]{1,0:T(8,128)} %copy-done.1, bf16[1024,1792]{1,0:T(8,128)(2,1)} %bitcast.19, bf16[1024,1792]{1,0:T(8,128)(2,1)} %bitcast.26, bf16[1024,1792]{1,0:T(8,128)(2,1)} %bitcast.34), custom_call_target="tpu_custom_call" | custom-call | flops 11796480 | bytes 6291456 | tf_op jit(solution)/shard_map/pallas_call | solution.py:220
  162.1 3.6 %shard_map.90 = (bf16[1024,1792]{1,0:T(8,128)(2,1)}, bf16[1024,1792]{1,0:T(8,128)(2,1)}, bf16[1024,1792]{1,0:T(8,128)(2,1)}, f32[8,128]{1,0:T(8,128)S(1)}) custom-call(bf16[2,1040,256]{2,1,0:T(8,128)(2,1)} %shard_map.89.pair_ref, bf16[1024,256]{1,0:T(8,128)(2,1)S(1)} %copy-done.7, ...), custom_call_target="tpu_custom_call" | custom-call | flops 7864320 | bytes 4718592 | tf_op jit(solution)/shard_map/pallas_call | solution.py:235
  165.7 9.2 %collective-permute-done.13.refs_1_.pair_other_ref = bf16[2,1024,256]{2,1,0:T(8,128)(2,1)} collective-permute-done((bf16[2,1024,256]{2,1,0:T(8,128)(2,1)}, bf16[2,1024,256]{2,1,0:T(8,128)(2,1)}, u32[]{:S(2)}, u32[]{:S(2)}) %collective-permute-start.13) | collective-permute-done | bytes 1048608 | tf_op jit(solution)/shard_map/ppermute | solution.py:22
  176.1 3.2 %collective-permute-start.16 = (bf16[2,1024,384]{2,1,0:T(8,128)(2,1)}, bf16[2,1024,384]{2,1,0:T(8,128)(2,1)S(1)}, u32[]{:S(2)}, u32[]{:S(2)}) collective-permute-start(bf16[2,1024,384]{2,1,0:T(8,128)(2,1)} %shard_map.91.pair_ref), channel_id=1, source_target_pairs={{0,64},{16,80},{32,96},{48,112},{64,0},{80,16},{96,32},{112,48},{1... | collective-permute-start | bytes 4718600 | tf_op jit(solution)/shard_map/ppermute | solution.py:22
  179.3 2.8 %shard_map.98 = (bf16[2,1024,128]{2,1,0:T(8,128)(2,1)}, bf16[1024,128]{1,0:T(8,128)(2,1)}) custom-call(f32[8,128]{1,0:T(8,128)} %copy-done.16, f32[1024,256]{1,0:T(8,128)} %copy-done.4, bf16[1024,1792]{1,0:T(8,128)(2,1)} %bitcast.20, bf16[1024,1792]{1,0:T(8,128)(2,1)} %bitcast.27, bf16[1024,1792]{1,0:T(8,128)(2,1)} %bitcast.35), custom_call_target="tpu_custom_call" | custom-call | flops 3932160 | bytes 2097152 | tf_op jit(solution)/shard_map/pallas_call | solution.py:220
  182.2 2.8 %shard_map.85 = (bf16[2,1024,128]{2,1,0:T(8,128)(2,1)}, bf16[1024,128]{1,0:T(8,128)(2,1)}) custom-call(f32[8,128]{1,0:T(8,128)} %copy-done.16, f32[1024,256]{1,0:T(8,128)} %copy-done.4, bf16[1024,1792]{1,0:T(8,128)(2,1)} %bitcast.21, bf16[1024,1792]{1,0:T(8,128)(2,1)} %bitcast.28, bf16[1024,1792]{1,0:T(8,128)(2,1)} %bitcast.36), custom_call_target="tpu_custom_call" | custom-call | flops 3932160 | bytes 2097152 | tf_op jit(solution)/shard_map/pallas_call | solution.py:220
  187.3 3.2 %shard_map.94 = (bf16[1024,1792]{1,0:T(8,128)(2,1)}, bf16[1024,1792]{1,0:T(8,128)(2,1)}, bf16[1024,1792]{1,0:T(8,128)(2,1)}, f32[8,128]{1,0:T(8,128)S(1)}) custom-call(bf16[2,1024,256]{2,1,0:T(8,128)(2,1)S(1)} %copy-done.10, bf16[1024,256]{1,0:T(8,128)(2,1)S(1)} %copy-done.13, ...), custom_call_target="tpu_custom_call", output_to_operand_aliasing={{0}: (4, {}), {1}: (5, {}), {2}: (6, {})} | custom-call | flops 7864320 | bytes 4718592 | tf_op jit(solution)/shard_map/pallas_call | solution.py:235
  190.5 6.2 %shard_map.95 = (bf16[1024,1792]{1,0:T(8,128)(2,1)}, bf16[1024,1792]{1,0:T(8,128)(2,1)}, bf16[1024,1792]{1,0:T(8,128)(2,1)}) custom-call(f32[8,128]{1,0:T(8,128)} %copy-done.16, bf16[2,1040,256]{2,1,0:T(8,128)(2,1)} %copy-done.2, f32[1024,768]{1,0:T(8,128)} %copy-done, ...), custom_call_target="tpu_custom_call", output_to_operand_aliasing={{0}: (10, {}), {1}: (11, {}), {2}: (12, {})} | custom-call | flops 15728640 | bytes 5767168 | tf_op jit(solution)/shard_map/pallas_call | solution.py:257
  196.7 11.8 %collective-permute-done.17.pair_other_ref.refs_1_ = bf16[2,1024,384]{2,1,0:T(8,128)(2,1)S(1)} collective-permute-done((bf16[2,1024,384]{2,1,0:T(8,128)(2,1)}, bf16[2,1024,384]{2,1,0:T(8,128)(2,1)S(1)}, u32[]{:S(2)}, u32[]{:S(2)}) %collective-permute-start.17) | collective-permute-done | bytes 1572896 | tf_op jit(solution)/shard_map/ppermute | solution.py:22
  208.5 3.2 %collective-permute-start.19 = (bf16[2,1024,128]{2,1,0:T(8,128)(2,1)}, bf16[2,1024,128]{2,1,0:T(8,128)(2,1)S(1)}, u32[]{:S(2)}, u32[]{:S(2)}) collective-permute-start(bf16[2,1024,128]{2,1,0:T(8,128)(2,1)} %shard_map.99.pair_ref), channel_id=1, source_target_pairs={{0,64},{16,80},{32,96},{48,112},{64,0},{80,16},{96,32},{112,48},{1... | collective-permute-start | bytes 1572872 | tf_op jit(solution)/shard_map/ppermute | solution.py:22
  212.8 3.8 %shard_map.96 = (bf16[1024,1792]{1,0:T(8,128)(2,1)}, bf16[1024,1792]{1,0:T(8,128)(2,1)}, bf16[1024,1792]{1,0:T(8,128)(2,1)}, f32[8,128]{1,0:T(8,128)S(1)}) custom-call(bf16[2,1024,384]{2,1,0:T(8,128)(2,1)} %shard_map.93.pair_ref, bf16[1024,384]{1,0:T(8,128)(2,1)S(1)} %copy-done.12, ...), custom_call_target="tpu_custom_call", output_to_operand_aliasing={{0}: (4, {}), {1}: (5, {}), {2}: (6, {})} | custom-call | flops 11796480 | bytes 7077888 | tf_op jit(solution)/shard_map/pallas_call | solution.py:235
  216.7 25.5 %collective-permute-done.16.refs_1_.pair_other_ref = bf16[2,1024,384]{2,1,0:T(8,128)(2,1)S(1)} collective-permute-done((bf16[2,1024,384]{2,1,0:T(8,128)(2,1)}, bf16[2,1024,384]{2,1,0:T(8,128)(2,1)S(1)}, u32[]{:S(2)}, u32[]{:S(2)}) %collective-permute-start.16) | collective-permute-done | bytes 1572896 | tf_op jit(solution)/shard_map/ppermute | solution.py:22
  242.2 3.2 %collective-permute-start.18 = (bf16[2,1024,128]{2,1,0:T(8,128)(2,1)S(1)}, bf16[2,1024,128]{2,1,0:T(8,128)(2,1)S(1)}, u32[]{:S(2)}, u32[]{:S(2)}) collective-permute-start(bf16[2,1024,128]{2,1,0:T(8,128)(2,1)S(1)} %shard_map.97.pair_ref), channel_id=1, source_target_pairs={{0,64},{16,80},{32,96},{48,112},{64,0},{80,16},{96,32},{112,48},{1... | collective-permute-start | bytes 1572872 | tf_op jit(solution)/shard_map/ppermute | solution.py:22
  245.4 3.8 %shard_map.100 = (bf16[1024,1792]{1,0:T(8,128)(2,1)}, bf16[1024,1792]{1,0:T(8,128)(2,1)}, bf16[1024,1792]{1,0:T(8,128)(2,1)}, f32[8,128]{1,0:T(8,128)}) custom-call(bf16[2,1024,384]{2,1,0:T(8,128)(2,1)} %shard_map.91.pair_ref, bf16[1024,384]{1,0:T(8,128)(2,1)S(1)} %copy-done.11, ...), custom_call_target="tpu_custom_call", output_to_operand_aliasing={{0}: (4, {}), {1}: (5, {}), {2}: (6, {})} | custom-call | flops 11796480 | bytes 7077888 | tf_op jit(solution)/shard_map/pallas_call | solution.py:235
  249.2 4.2 %collective-permute-done.19.pair_other_ref = bf16[2,1024,128]{2,1,0:T(8,128)(2,1)S(1)} collective-permute-done((bf16[2,1024,128]{2,1,0:T(8,128)(2,1)}, bf16[2,1024,128]{2,1,0:T(8,128)(2,1)S(1)}, u32[]{:S(2)}, u32[]{:S(2)}) %collective-permute-start.19) | collective-permute-done | bytes 524320 | tf_op jit(solution)/shard_map/ppermute | solution.py:22
  253.4 2.4 shard_map.101
  255.8 6.7 %collective-permute-done.18.pair_other_ref = bf16[2,1024,128]{2,1,0:T(8,128)(2,1)S(1)} collective-permute-done((bf16[2,1024,128]{2,1,0:T(8,128)(2,1)S(1)}, bf16[2,1024,128]{2,1,0:T(8,128)(2,1)S(1)}, u32[]{:S(2)}, u32[]{:S(2)}) %collective-permute-start.18) | collective-permute-done | bytes 524320 | tf_op jit(solution)/shard_map/ppermute | solution.py:22
  262.6 2.2 shard_map.102
  (72 shorter events, 25.7 us)
Async XLA Ops:
  0.6 20.5 %collective-permute-start = (bf16[1024,256]{1,0:T(8,128)(2,1)}, bf16[1024,256]{1,0:T(8,128)(2,1)S(1)}, u32[]{:S(2)}, u32[]{:S(2)}) collective-permute-start(bf16[1024,256]{1,0:T(8,128)(2,1)} %bitcast.43), channel_id=1, source_target_pairs={{0,0},{1,1},{2,2},{3,3},{4,10},{5,11},{6,8},{7,9},{8,6},{9,7},{10,... | collective-permute-start | bytes 1572872 | tf_op jit(solution)/shard_map/ppermute | solution.py:62
  6.4 90.1 %collective-permute-start.6 = (bf16[1024,1792]{1,0:T(8,128)(2,1)}, bf16[1024,1792]{1,0:T(8,128)(2,1)}, u32[]{:S(2)}, u32[]{:S(2)}) collective-permute-start(bf16[1024,1792]{1,0:T(8,128)(2,1)} %bitcast.30), channel_id=1, source_target_pairs={{0,64},{16,80},{32,96},{48,112},{64,0},{80,16},{96,32},{112,48},{1... | collective-permute-start | bytes 11010056 | tf_op jit(solution)/shard_map/ppermute | solution.py:22
  14.1 39.2 %collective-permute-start.1 = (bf16[1024,768]{1,0:T(8,128)(2,1)}, bf16[1024,768]{1,0:T(8,128)(2,1)}, u32[]{:S(2)}, u32[]{:S(2)}) collective-permute-start(bf16[1024,768]{1,0:T(8,128)(2,1)} %get-tuple-element.94.u_ref), channel_id=1, source_target_pairs={{0,8},{8,0},{1,9},{9,1},{2,10},{10,2},{3,11},{11,3},{4,12},{12,4},... | collective-permute-start | bytes 4718600 | tf_op jit(solution)/shard_map/ppermute | solution.py:26
  22.6 30.7 %all-to-all-start = ((bf16[4,1024,256]{2,1,0:T(8,128)(2,1)}), bf16[4,1024,256]{2,1,0:T(8,128)(2,1)S(1)}, u32[]{:S(2)}, u32[]{:S(2)}) async-start(bf16[4,1024,256]{2,1,0:T(8,128)(2,1)} %broadcast_in_dim.12), calls=%async_computation | async-start | bytes 4194304 | tf_op jit(solution)/shard_map/all_to_all | solution.py:67
  26.2 60.7 %collective-permute-start.4 = (bf16[1024,768]{1,0:T(8,128)(2,1)}, bf16[1024,768]{1,0:T(8,128)(2,1)}, u32[]{:S(2)}, u32[]{:S(2)}) collective-permute-start(bf16[1024,768]{1,0:T(8,128)(2,1)} %get-tuple-element.93.u_ref), channel_id=1, source_target_pairs={{0,8},{8,0},{1,9},{9,1},{2,10},{10,2},{3,11},{11,3},{4,12},{12,4},... | collective-permute-start | bytes 4718600 | tf_op jit(solution)/shard_map/ppermute | solution.py:26
  53.3 2.4 copy-start.17
  53.3 2.4 copy-start.18
  55.1 6.8 %collective-permute-start.2 = (bf16[2,1024,256]{2,1,0:T(8,128)(2,1)S(1)}, bf16[2,1024,256]{2,1,0:T(8,128)(2,1)S(1)}, u32[]{:S(2)}, u32[]{:S(2)}) collective-permute-start(bf16[2,1024,256]{2,1,0:T(8,128)(2,1)S(1)} %get-tuple-element.96), channel_id=1, source_target_pairs={{0,1},{1,0},{2,3},{3,2},{4,5},{5,4},{6,7},{7,6},{8,9},{9,8},{10,11... | collective-permute-start | bytes 3145736 | tf_op jit(solution)/shard_map/ppermute | solution.py:53
  55.2 11.8 %collective-permute-start.3 = (bf16[2,1024,256]{2,1,0:T(8,128)(2,1)}, bf16[2,1024,256]{2,1,0:T(8,128)(2,1)}, u32[]{:S(2)}, u32[]{:S(2)}) collective-permute-start(bf16[2,1024,256]{2,1,0:T(8,128)(2,1)} %get-tuple-element.95), channel_id=1, source_target_pairs={{0,1},{1,0},{2,3},{3,2},{4,5},{5,4},{6,7},{7,6},{8,9},{9,8},{10,11... | collective-permute-start | bytes 3145736 | tf_op jit(solution)/shard_map/ppermute | solution.py:53
  56.7 56.6 %collective-permute-start.12 = (bf16[1024,512]{1,0:T(8,128)(2,1)}, bf16[1024,512]{1,0:T(8,128)(2,1)}, u32[]{:S(2)}, u32[]{:S(2)}) collective-permute-start(bf16[1024,512]{1,0:T(8,128)(2,1)} %pad_maximum_fusion), channel_id=1, source_target_pairs={{0,64},{16,80},{32,96},{48,112},{64,0},{80,16},{96,32},{112,48},{1... | collective-permute-start | bytes 3145736 | tf_op jit(solution)/shard_map/ppermute | solution.py:22
  61.9 1.0 copy-start.8
  62.9 33.6 %collective-permute-start.5 = (bf16[1024,256]{1,0:T(8,128)(2,1)}, bf16[1024,256]{1,0:T(8,128)(2,1)}, u32[]{:S(2)}, u32[]{:S(2)}) collective-permute-start(bf16[1024,256]{1,0:T(8,128)(2,1)} %slice.49.u_ref), channel_id=1, source_target_pairs={{0,8},{8,0},{1,9},{9,1},{2,10},{10,2},{3,11},{11,3},{4,12},{12,4},... | collective-permute-start | bytes 1572872 | tf_op jit(solution)/shard_map/ppermute | solution.py:26
  67.0 1.2 copy-start.9
  73.7 5.0 %copy-start.3 = (bf16[1024,768]{1,0:T(8,128)(2,1)S(1)}, bf16[1024,768]{1,0:T(8,128)(2,1)}, u32[]{:S(2)}) copy-start(bf16[1024,768]{1,0:T(8,128)(2,1)} %get-tuple-element.93.u_ref) | copy-start | bytes 4718596
  77.8 36.6 %copy-start = (f32[1024,768]{1,0:T(8,128)}, f32[1024,768]{1,0:T(8,128)S(1)}, u32[]{:S(2)}) copy-start(f32[1024,768]{1,0:T(8,128)S(1)} %get-tuple-element.54.grad_ref) | copy-start | bytes 9437188
  77.9 45.4 %collective-permute-start.14 = (bf16[1024,256]{1,0:T(8,128)(2,1)S(1)}, bf16[1024,256]{1,0:T(8,128)(2,1)S(1)}, u32[]{:S(2)}, u32[]{:S(2)}) collective-permute-start(bf16[1024,256]{1,0:T(8,128)(2,1)S(1)} %slice.55), channel_id=1, source_target_pairs={{0,64},{16,80},{32,96},{48,112},{64,0},{80,16},{96,32},{112,48},{1... | collective-permute-start | bytes 1572872 | tf_op jit(solution)/shard_map/ppermute | solution.py:22
  91.0 1.7 copy-start.1
  99.1 24.2 %copy-start.4 = (f32[1024,256]{1,0:T(8,128)}, f32[1024,256]{1,0:T(8,128)S(1)}, u32[]{:S(2)}) copy-start(f32[1024,256]{1,0:T(8,128)S(1)} %get-tuple-element.50.grad_ref) | copy-start | bytes 3145732
  99.2 1.2 collective-permute-start.7
  100.4 4.8 %collective-permute-start.10 = (f32[8,128]{1,0:T(8,128)S(1)}, f32[8,128]{1,0:T(8,128)S(1)}, u32[]{:S(2)}, u32[]{:S(2)}) collective-permute-start(f32[8,128]{1,0:T(8,128)S(1)} %add.34), channel_id=1, source_target_pairs={{0,6},{1,7},{2,4},{3,5},{4,2},{5,3},{6,0},{7,1},{8,14},{9,15},{10,... | collective-permute-start | bytes 12296 | tf_op jit(solution)/shard_map/ppermute | solution.py:53
  103.2 3.6 %collective-permute-start.8 = (f32[8,128]{1,0:T(8,128)S(1)}, f32[8,128]{1,0:T(8,128)S(1)}, u32[]{:S(2)}, u32[]{:S(2)}) collective-permute-start(f32[8,128]{1,0:T(8,128)S(1)} %add.34), channel_id=1, source_target_pairs={{0,2},{1,3},{2,0},{3,1},{4,6},{5,7},{6,4},{7,5},{8,10},{9,11},{10,... | collective-permute-start | bytes 12296 | tf_op jit(solution)/shard_map/ppermute | solution.py:53
  103.6 5.1 %collective-permute-start.9 = (f32[8,128]{1,0:T(8,128)S(1)}, f32[8,128]{1,0:T(8,128)S(1)}, u32[]{:S(2)}, u32[]{:S(2)}) collective-permute-start(f32[8,128]{1,0:T(8,128)S(1)} %add.34), channel_id=1, source_target_pairs={{0,4},{1,5},{2,6},{3,7},{4,0},{5,1},{6,2},{7,3},{8,12},{9,13},{10,... | collective-permute-start | bytes 12296 | tf_op jit(solution)/shard_map/ppermute | solution.py:53
  108.7 5.1 %collective-permute-start.11 = (f32[8,128]{1,0:T(8,128)S(1)}, f32[8,128]{1,0:T(8,128)S(1)}, u32[]{:S(2)}, u32[]{:S(2)}) collective-permute-start(f32[8,128]{1,0:T(8,128)S(1)} %add_add_fusion.one_ref), channel_id=1, source_target_pairs={{0,8},{8,0},{1,9},{9,1},{2,10},{10,2},{3,11},{11,3},{4,12},{12,4},... | collective-permute-start | bytes 12296 | tf_op jit(solution)/shard_map/ppermute | solution.py:26
  114.5 8.9 %copy-start.16 = (f32[8,128]{1,0:T(8,128)}, f32[8,128]{1,0:T(8,128)S(1)}, u32[]{:S(2)}) copy-start(f32[8,128]{1,0:T(8,128)S(1)} %shard_map.84.total_ref) | copy-start | bytes 12292
  123.3 0.8 copy-start.5
  124.1 28.2 %collective-permute-start.15 = (bf16[2,1040,256]{2,1,0:T(8,128)(2,1)}, bf16[2,1040,256]{2,1,0:T(8,128)(2,1)S(1)}, u32[]{:S(2)}, u32[]{:S(2)}) collective-permute-start(bf16[2,1040,256]{2,1,0:T(8,128)(2,1)} %shard_map.89.pair_ref), channel_id=1, source_target_pairs={{0,64},{16,80},{32,96},{48,112},{64,0},{80,16},{96,32},{112,48},{1... | collective-permute-start | bytes 3194888 | tf_op jit(solution)/shard_map/ppermute | solution.py:22
  131.5 43.4 %collective-permute-start.13 = (bf16[2,1024,256]{2,1,0:T(8,128)(2,1)}, bf16[2,1024,256]{2,1,0:T(8,128)(2,1)}, u32[]{:S(2)}, u32[]{:S(2)}) collective-permute-start(bf16[2,1024,256]{2,1,0:T(8,128)(2,1)} %get-tuple-element.55.pair_ref), channel_id=1, source_target_pairs={{0,64},{16,80},{32,96},{48,112},{64,0},{80,16},{96,32},{112,48},{1... | collective-permute-start | bytes 3145736 | tf_op jit(solution)/shard_map/ppermute | solution.py:22
  152.3 8.7 %copy-start.2 = (bf16[2,1040,256]{2,1,0:T(8,128)(2,1)}, bf16[2,1040,256]{2,1,0:T(8,128)(2,1)S(1)}, u32[]{:S(2)}) copy-start(bf16[2,1040,256]{2,1,0:T(8,128)(2,1)S(1)} %collective-permute-done.15.pair_other_ref.refs_1_.clip_other_ref) | copy-start | bytes 3194884
  152.3 56.2 %collective-permute-start.17 = (bf16[2,1024,384]{2,1,0:T(8,128)(2,1)}, bf16[2,1024,384]{2,1,0:T(8,128)(2,1)S(1)}, u32[]{:S(2)}, u32[]{:S(2)}) collective-permute-start(bf16[2,1024,384]{2,1,0:T(8,128)(2,1)} %shard_map.93.pair_ref), channel_id=1, source_target_pairs={{0,64},{16,80},{32,96},{48,112},{64,0},{80,16},{96,32},{112,48},{1... | collective-permute-start | bytes 4718600 | tf_op jit(solution)/shard_map/ppermute | solution.py:22
  161.0 1.0 copy-start.7
  176.1 66.1 %collective-permute-start.16 = (bf16[2,1024,384]{2,1,0:T(8,128)(2,1)}, bf16[2,1024,384]{2,1,0:T(8,128)(2,1)S(1)}, u32[]{:S(2)}, u32[]{:S(2)}) collective-permute-start(bf16[2,1024,384]{2,1,0:T(8,128)(2,1)} %shard_map.91.pair_ref), channel_id=1, source_target_pairs={{0,64},{16,80},{32,96},{48,112},{64,0},{80,16},{96,32},{112,48},{1... | collective-permute-start | bytes 4718600 | tf_op jit(solution)/shard_map/ppermute | solution.py:22
  185.0 1.2 copy-start.10
  186.2 1.0 copy-start.13
  208.5 44.9 %collective-permute-start.19 = (bf16[2,1024,128]{2,1,0:T(8,128)(2,1)}, bf16[2,1024,128]{2,1,0:T(8,128)(2,1)S(1)}, u32[]{:S(2)}, u32[]{:S(2)}) collective-permute-start(bf16[2,1024,128]{2,1,0:T(8,128)(2,1)} %shard_map.99.pair_ref), channel_id=1, source_target_pairs={{0,64},{16,80},{32,96},{48,112},{64,0},{80,16},{96,32},{112,48},{1... | collective-permute-start | bytes 1572872 | tf_op jit(solution)/shard_map/ppermute | solution.py:22
  211.7 1.1 copy-start.12
  212.8 29.3 %copy-start.6 = (bf16[2,1024,128]{2,1,0:T(8,128)(2,1)S(1)}, bf16[2,1024,128]{2,1,0:T(8,128)(2,1)}, u32[]{:S(2)}) copy-start(bf16[2,1024,128]{2,1,0:T(8,128)(2,1)} %get-tuple-element.51.refs_0_) | copy-start | bytes 1572868
  212.8 32.6 %copy-start.11 = (bf16[1024,384]{1,0:T(8,128)(2,1)S(1)}, bf16[1024,384]{1,0:T(8,128)(2,1)}, u32[]{:S(2)}) copy-start(bf16[1024,384]{1,0:T(8,128)(2,1)} %get-tuple-element.76.step_ref) | copy-start | bytes 2359300
  242.2 20.4 %collective-permute-start.18 = (bf16[2,1024,128]{2,1,0:T(8,128)(2,1)S(1)}, bf16[2,1024,128]{2,1,0:T(8,128)(2,1)S(1)}, u32[]{:S(2)}, u32[]{:S(2)}) collective-permute-start(bf16[2,1024,128]{2,1,0:T(8,128)(2,1)S(1)} %shard_map.97.pair_ref), channel_id=1, source_target_pairs={{0,64},{16,80},{32,96},{48,112},{64,0},{80,16},{96,32},{112,48},{1... | collective-permute-start | bytes 1572872 | tf_op jit(solution)/shard_map/ppermute | solution.py:22
  245.4 8.0 %copy-start.15 = (bf16[1024,128]{1,0:T(8,128)(2,1)S(1)}, bf16[1024,128]{1,0:T(8,128)(2,1)}, u32[]{:S(2)}) copy-start(bf16[1024,128]{1,0:T(8,128)(2,1)} %get-tuple-element.75.step_ref) | copy-start | bytes 786436
  253.4 9.2 %copy-start.14 = (bf16[1024,128]{1,0:T(8,128)(2,1)S(1)}, bf16[1024,128]{1,0:T(8,128)(2,1)}, u32[]{:S(2)}) copy-start(bf16[1024,128]{1,0:T(8,128)(2,1)} %get-tuple-element.72.step_ref) | copy-start | bytes 786436

commit v5 on v4

--- a/solution.py
+++ b/solution.py
@@ -184,15 +184,17 @@
     second_ref,
     first_other_ref,
     second_other_ref,
+    second_rest_ref,
     old_ref,
     old_other_ref,
     *rest,
 ):
     w_ref, one_ref, two_ref = rest[-3:]
     one, two = moments(clip_of(total_ref) * grad_ref[...], first_ref[...], second_ref[...])
+    second_other = jnp.concatenate([second_other_ref[...], second_rest_ref[...]], axis=1)
     clip_other = clip_other_ref[0, :1, :1].astype(F32) + clip_other_ref[1, :1, :1].astype(F32)
     scaled_other = clip_other * grad_other_ref[...].astype(F32)
-    one_other, two_other = moments(scaled_other, first_other_ref[...], second_other_ref[...])
+    one_other, two_other = moments(scaled_other, first_other_ref[...], second_other)
     w_ref[...] = mean(stepped(old_ref[...], one, two), stepped(old_other_ref[...], one_other, two_other))
     one_ref[...] = mean(one, one_other)
     two_ref[...] = mean(two, two_other)
@@ -258,11 +260,11 @@
         early_kernel,
         grid=(rows // STEP_ROWS,),
         out_shape=(shape, shape, shape),
-        in_specs=[TOTAL, pl.BlockSpec((2, 16, 128), lambda i: (0, rows // 16, 0))] + [wide] * 5 + [columns(width, width), wide, wide] + [ANYWHERE] * 3,
+        in_specs=[TOTAL, pl.BlockSpec((2, 16, 128), lambda i: (0, rows // 16, 0))] + [wide] * 5 + [columns(width // 2, width)] * 2 + [wide, wide] + [ANYWHERE] * 3,
         out_specs=(wide, wide, wide),
-        input_output_aliases={10 + i: i for i in range(3)},
+        input_output_aliases={11 + i: i for i in range(3)},
         cost_estimate=cost(rows, width, 60, 22),
-    )(total, pair_other, grad, grad_other, first, second, other, other, old, old_other, *outs)
+    )(total, pair_other, grad, grad_other, first, second, other, other, grad_other, old, old_other, *outs)
 
 
 def times(x, u):
@@ -318,7 +320,8 @@
 
 EARLY = 256
 UP = ((0, 768), (768, 768), (1536, 256))
-LATE = ((256, 256), (512, 256), (768, 384), (1152, 384), (1536, 128), (1664, 128))
+FIRST = 2
+LATE = ((256, 128), (384, 128), (512, 256), (1536, 128), (768, 384), (1152, 384), (1664, 128))
 
 
 def part(value, piece):
@@ -338,16 +341,18 @@
     up = [part(upstream, piece) for piece in UP]
     up_other = [swap_dp(piece) for piece in up]
     old_other = across(old)
-    state_other = across(jnp.concatenate([first[:, :EARLY], second[:, :EARLY]], axis=1))
-
-    near, *leading = gate((along_y(settled), *(part(value, LATE[0]) for value in (first, second))), (up_other[0],))
+    state_other = across(jnp.concatenate([first[:, :EARLY], second[:, : EARLY // 2]], axis=1))
+
+    near, *leading = gate(
+        (along_y(settled), part(first, LATE[FIRST]), part(second, LATE[FIRST])), (up_other[0],)
+    )
     features = assemble(near, turned(near[:2], 1), turned(near[2:], 1))
     grads, squares = [], jnp.zeros((8, 128), F32)
     for i, (piece, other) in enumerate(zip(up, up_other)):
         grad, square = finish(features, other, local_product(features, piece), (old_other,) if i == 2 else ())
         grads.append(grad)
         squares = squares + square
-    grad_other = across(grads[0][:, :EARLY].astype(BF16))
+    grad_other = across(jnp.concatenate([grads[0][:, :EARLY].astype(BF16), second[:, EARLY // 2 : EARLY]], axis=1))
     total = group_sum(squares, (state_other,))
 
     pairs, steps, received, flags = [], [], [], []
@@ -356,24 +361,25 @@
         if i < len(LATE):
             at, width = LATE[i]
             chunk, within = holder(UP, at)
-            if i:
+            if i == FIRST:
+                pair, step = make_first(total, grads[chunk], within, *leading), part(old, LATE[i])
+            else:
                 pair, step = make(total, grads[chunk], within, first, second, old, at, width)
-            else:
-                pair, step = make_first(total, grads[chunk], within, *leading), part(old, LATE[0])
-            if i == 0:
+            if i == 1:
                 (pair,) = gate((pair,), (grad_other,))
-            elif i > 1:
-                (pair,) = gate((pair,), (received[i - 2],) + ((flags[i - 3],) if i > 2 else ()))
+            elif i > 3:
+                earlier = [(received[0], received[1], flags[0]), (*received[2:4], *flags[1:2]), (*received[4:5], *flags[3:4])][i - 4]
+                (pair,) = gate((pair,), earlier)
             pairs.append(pair)
             steps.append(step)
             received.append(across(pair))
         if i >= 2:
             j = i - 2
             at, width = LATE[j]
-            *outs, flag = mix(pairs[j], steps[j], j > 0, received[j], old_other, at, width, old.shape, outs)
+            *outs, flag = mix(pairs[j], steps[j], j != FIRST, received[j], old_other, at, width, old.shape, outs)
             flags.append(flag)
-        if i == 3:
-            outs = early(total, received[0], grads[0], grad_other, first, second, state_other, old, old_other, EARLY, outs)
+        if i == FIRST + 2:
+            outs = early(total, received[FIRST], grads[0], grad_other, first, second, state_other, old, old_other, EARLY, outs)
     return tuple(out[None] for out in outs)
 
 

time: 266 us -> 262 us (0.985)
  local copies, waits for them, and re-layouts: 21.9 us -> 15.8 us
  Pallas kernels: 72 us -> 76.2 us
  waiting for transfers between devices: 122 us -> 118 us
    unnamed x38 -> x32, local copies, waits for them, and re-layouts: 9.11 us -> 1.8 us
    ppermute x9 -> x10, waiting for transfers between devices: 79.9 us -> 73.8 us  [across(): return lax.ppermute(value, 'replica', [(s, s ^ 4) for s in range(8)])]
    ppermute x4, waiting for transfers between devices: 29.9 us -> 32.8 us  [swap_dp(): return lax.ppermute(value, 'dp', [(0, 1), (1, 0)])]
    pallas_call x6 -> x7, Pallas kernels: 19.1 us -> 21.1 us  [mix(): pl.pallas_call(functools.partial(mix_kernel, ready), grid=(rows // depth,...]
    pallas_call x5 -> x6, Pallas kernels: 21 us -> 22.6 us  [make(): pl.pallas_call(make_kernel, grid=(rows // STEP_ROWS,), out_shape=(jax.Sha...]
    ppermute x9 -> x10, starting transfers between devices: 24.6 us -> 26.1 us  [across(): return lax.ppermute(value, 'replica', [(s, s ^ 4) for s in range(8)])]
    slice x3 -> x4, local copies, waits for them, and re-layouts: 7.49 us -> 7.77 us  [part(): return value[:, piece[0]:piece[0] + piece[1]]]
  transfers between devices with their start and end apart: 21 -> 22, of which waited for: 17 -> 14; matrix products, arithmetic and copies ran while one was open for 5% -> 6% of each run, Pallas kernels for 26% -> 28%
where the time goes in v5:
time: 262 us; the launch traced here: 261 us
  waiting for transfers between devices  118 us (45%)
  Pallas kernels  76.2 us (29%)
  starting transfers between devices  48.3 us (18%)
  local copies, waits for them, and re-layouts  15.8 us (6%)
    ppermute x10, waiting for transfers between devices, across(): return lax.ppermute(value, 'replica', [(s, s ^ 4) for s in range(8)])  73.8 us
    ppermute x4, waiting for transfers between devices, swap_dp(): return lax.ppermute(value, 'dp', [(0, 1), (1, 0)])  32.8 us
    ppermute x10, starting transfers between devices, across(): return lax.ppermute(value, 'replica', [(s, s ^ 4) for s in range(8)])  26.1 us
    pallas_call x6, Pallas kernels, make(): pl.pallas_call(make_kernel, grid=(rows // STEP_ROWS,), out_shape=(jax.Sha...  22.6 us
    pallas_call x7, Pallas kernels, mix(): pl.pallas_call(functools.partial(mix_kernel, ready), grid=(rows // depth,...  21.1 us
    pallas_call x3, Pallas kernels, finish(): pl.pallas_call(finish_kernel, grid=(blocks // 2,), out_shape=(jax.ShapeDt...  10.8 us
    pallas_call x3, Pallas kernels, local_product(): pl.pallas_call(local_kernel, grid=(blocks // 2,), out_shape=jax.ShapeDtyp...  9 us
    slice x4, local copies, waits for them, and re-layouts, part(): return value[:, piece[0]:piece[0] + piece[1]]  7.77 us
  transfers between devices with their start and end apart: 22, of which 14 were waited for; matrix products, arithmetic and copies ran while one was open for 6% of the time, Pallas kernels for 28%

profile of v5, /device:TPU:6, one launch (start us, length us, event | category | flops | bytes accessed | tf_op | source)
XLA Modules:
  0.0 260.7 jit_solution(12891933439444772610)
XLA Ops:
  0.6 5.8 %collective-permute-start = (bf16[1024,256]{1,0:T(8,128)(2,1)}, bf16[1024,256]{1,0:T(8,128)(2,1)S(1)}, u32[]{:S(2)}, u32[]{:S(2)}) collective-permute-start(bf16[1024,256]{1,0:T(8,128)(2,1)} %bitcast.47), channel_id=1, source_target_pairs={{0,0},{1,1},{2,2},{3,3},{4,10},{5,11},{6,8},{7,9},{8,6},{9,7},{10,... | collective-permute-start | bytes 1572872 | tf_op jit(solution)/shard_map/ppermute | solution.py:62
  6.4 4.0 %collective-permute-start.6 = (bf16[1024,1792]{1,0:T(8,128)(2,1)}, bf16[1024,1792]{1,0:T(8,128)(2,1)}, u32[]{:S(2)}, u32[]{:S(2)}) collective-permute-start(bf16[1024,1792]{1,0:T(8,128)(2,1)} %bitcast.33), channel_id=1, source_target_pairs={{0,64},{16,80},{32,96},{48,112},{64,0},{80,16},{96,32},{112,48},{1... | collective-permute-start | bytes 11010056 | tf_op jit(solution)/shard_map/ppermute | solution.py:22
  10.4 3.8 %fusion.2 = (bf16[1024,768]{1,0:T(8,128)(2,1)}, bf16[1024,768]{1,0:T(8,128)(2,1)}) fusion(bf16[1024,1792]{1,0:T(8,128)(2,1)} %bitcast.45), kind=kLoop, calls=%fused_computation.12 | loop fusion | bytes 6291456 | tf_op jit(solution)/shard_map/slice | solution.py:328
  14.1 7.0 %collective-permute-done = bf16[1024,256]{1,0:T(8,128)(2,1)S(1)} collective-permute-done((bf16[1024,256]{1,0:T(8,128)(2,1)}, bf16[1024,256]{1,0:T(8,128)(2,1)S(1)}, u32[]{:S(2)}, u32[]{:S(2)}) %collective-permute-start) | collective-permute-done | bytes 524320 | tf_op jit(solution)/shard_map/ppermute | solution.py:62
  22.6 3.6 %all-to-all-start = ((bf16[4,1024,256]{2,1,0:T(8,128)(2,1)}), bf16[4,1024,256]{2,1,0:T(8,128)(2,1)S(1)}, u32[]{:S(2)}, u32[]{:S(2)}) async-start(bf16[4,1024,256]{2,1,0:T(8,128)(2,1)} %broadcast_in_dim.12), calls=%async_computation | async-start | bytes 4194304 | tf_op jit(solution)/shard_map/all_to_all | solution.py:67
  26.2 2.1 collective-permute-start.4
  29.4 2.1 fusion.1
  31.5 21.8 %collective-permute-done.1.refs_3_.u_ref = bf16[1024,768]{1,0:T(8,128)(2,1)} collective-permute-done((bf16[1024,768]{1,0:T(8,128)(2,1)}, bf16[1024,768]{1,0:T(8,128)(2,1)}, u32[]{:S(2)}, u32[]{:S(2)}) %collective-permute-start.1) | collective-permute-done | bytes 1572896 | tf_op jit(solution)/shard_map/ppermute | solution.py:26
  55.9 1.9 slice.53.u_ref
  57.8 3.5 %collective-permute-start.5 = (bf16[1024,256]{1,0:T(8,128)(2,1)}, bf16[1024,256]{1,0:T(8,128)(2,1)}, u32[]{:S(2)}, u32[]{:S(2)}) collective-permute-start(bf16[1024,256]{1,0:T(8,128)(2,1)} %slice.53.u_ref), channel_id=1, source_target_pairs={{0,8},{8,0},{1,9},{9,1},{2,10},{10,2},{3,11},{11,3},{4,12},{12,4},... | collective-permute-start | bytes 1572872 | tf_op jit(solution)/shard_map/ppermute | solution.py:26
  63.6 4.0 %collective-permute-start.12 = (bf16[1024,384]{1,0:T(8,128)(2,1)S(1)}, bf16[1024,384]{1,0:T(8,128)(2,1)S(1)}, u32[]{:S(2)}, u32[]{:S(2)}) collective-permute-start(bf16[1024,384]{1,0:T(8,128)(2,1)S(1)} %pad_maximum_fusion), channel_id=1, source_target_pairs={{0,64},{16,80},{32,96},{48,112},{64,0},{80,16},{96,32},{112,48},{1... | collective-permute-start | bytes 2359304 | tf_op jit(solution)/shard_map/ppermute | solution.py:22
  67.5 1.8 shard_map.77.x_ref
  69.4 3.9 %shard_map.78.local_ref = f32[1024,768]{1,0:T(8,128)S(1)} custom-call(bf16[8,1024,256]{2,1,0:T(8,128)(2,1)S(1)} %shard_map.77.x_ref, bf16[1024,768]{1,0:T(8,128)(2,1)} %get-tuple-element.104.u_ref), custom_call_target="tpu_custom_call" | custom-call | bytes 4096 | tf_op jit(solution)/shard_map/pallas_call | solution.py:281
  73.3 4.2 %shard_map.79 = (f32[1024,768]{1,0:T(8,128)S(1)}, f32[8,128]{1,0:T(8,128)S(1)}) custom-call(bf16[8,1024,256]{2,1,0:T(8,128)(2,1)S(1)} %shard_map.77.x_ref, bf16[1024,768]{1,0:T(8,128)(2,1)} %collective-permute-done.1.refs_3_.u_ref, f32[1024,768]{1,0:T(8,128)S(1)} %shard_map.78.local_ref), custom_call_target="tpu_custom_call" | custom-call | bytes 4096 | tf_op jit(solution)/shard_map/pallas_call | solution.py:310
  77.8 2.5 shard_map.80.local_ref
  80.3 2.5 shard_map.82.local_ref
  82.8 4.1 %collective-permute-done.4.u_ref = bf16[1024,768]{1,0:T(8,128)(2,1)} collective-permute-done((bf16[1024,768]{1,0:T(8,128)(2,1)}, bf16[1024,768]{1,0:T(8,128)(2,1)}, u32[]{:S(2)}, u32[]{:S(2)}) %collective-permute-start.4) | collective-permute-done | bytes 1572896 | tf_op jit(solution)/shard_map/ppermute | solution.py:26
  87.0 4.0 %shard_map.81 = (f32[1024,768]{1,0:T(8,128)S(1)}, f32[8,128]{1,0:T(8,128)S(1)}) custom-call(bf16[8,1024,256]{2,1,0:T(8,128)(2,1)S(1)} %shard_map.77.x_ref, bf16[1024,768]{1,0:T(8,128)(2,1)} %collective-permute-done.4.u_ref, f32[1024,768]{1,0:T(8,128)S(1)} %shard_map.80.local_ref), custom_call_target="tpu_custom_call" | custom-call | bytes 4096 | tf_op jit(solution)/shard_map/pallas_call | solution.py:310
  92.8 3.8 %collective-permute-done.5.u_ref = bf16[1024,256]{1,0:T(8,128)(2,1)} collective-permute-done((bf16[1024,256]{1,0:T(8,128)(2,1)}, bf16[1024,256]{1,0:T(8,128)(2,1)}, u32[]{:S(2)}, u32[]{:S(2)}) %collective-permute-start.5) | collective-permute-done | bytes 524320 | tf_op jit(solution)/shard_map/ppermute | solution.py:26
  96.5 2.6 %shard_map.83 = (f32[1024,256]{1,0:T(8,128)S(1)}, f32[8,128]{1,0:T(8,128)S(1)}) custom-call(bf16[8,1024,256]{2,1,0:T(8,128)(2,1)S(1)} %shard_map.77.x_ref, bf16[1024,256]{1,0:T(8,128)(2,1)} %collective-permute-done.5.u_ref, f32[1024,256]{1,0:T(8,128)S(1)} %shard_map.82.local_ref, bf16[1024,1792]{1,0:T(8,128)(2,1)} %collective-permute-done.6.rest_0_.old_other_ref), custom_call_target="tpu_custom_call" | custom-call | bytes 4096 | tf_op jit(solution)/shard_map/pallas_call | solution.py:310
  100.4 2.8 %collective-permute-start.10 = (f32[8,128]{1,0:T(8,128)S(1)}, f32[8,128]{1,0:T(8,128)S(1)}, u32[]{:S(2)}, u32[]{:S(2)}) collective-permute-start(f32[8,128]{1,0:T(8,128)S(1)} %add.34), channel_id=1, source_target_pairs={{0,6},{1,7},{2,4},{3,5},{4,2},{5,3},{6,0},{7,1},{8,14},{9,15},{10,... | collective-permute-start | bytes 12296 | tf_op jit(solution)/shard_map/ppermute | solution.py:53
  106.9 1.9 collective-permute-done.9
  108.7 2.0 collective-permute-start.11
  110.8 3.1 %collective-permute-done.11.two_ref = f32[8,128]{1,0:T(8,128)S(1)} collective-permute-done((f32[8,128]{1,0:T(8,128)S(1)}, f32[8,128]{1,0:T(8,128)S(1)}, u32[]{:S(2)}, u32[]{:S(2)}) %collective-permute-start.11) | collective-permute-done | bytes 4128 | tf_op jit(solution)/shard_map/ppermute | solution.py:26
  115.6 3.9 %collective-permute-start.18 = (bf16[2,1040,256]{2,1,0:T(8,128)(2,1)}, bf16[2,1040,256]{2,1,0:T(8,128)(2,1)S(1)}, u32[]{:S(2)}, u32[]{:S(2)}) collective-permute-start(bf16[2,1040,256]{2,1,0:T(8,128)(2,1)} %shard_map.93.pair_ref), channel_id=1, source_target_pairs={{0,64},{16,80},{32,96},{48,112},{64,0},{80,16},{96,32},{112,48},{1... | collective-permute-start | bytes 3194888 | tf_op jit(solution)/shard_map/ppermute | solution.py:22
  119.5 2.8 %shard_map.87 = (bf16[2,1024,128]{2,1,0:T(8,128)(2,1)}, bf16[1024,128]{1,0:T(8,128)(2,1)}) custom-call(f32[8,128]{1,0:T(8,128)} %copy-done.11, f32[1024,768]{1,0:T(8,128)} %copy-done, bf16[1024,1792]{1,0:T(8,128)(2,1)} %bitcast.17, bf16[1024,1792]{1,0:T(8,128)(2,1)} %bitcast.26, bf16[1024,1792]{1,0:T(8,128)(2,1)} %bitcast.34), custom_call_target="tpu_custom_call" | custom-call | flops 3932160 | bytes 2097152 | tf_op jit(solution)/shard_map/pallas_call | solution.py:222
  122.4 2.9 %shard_map.88 = (bf16[2,1024,128]{2,1,0:T(8,128)(2,1)}, bf16[1024,128]{1,0:T(8,128)(2,1)}) custom-call(f32[8,128]{1,0:T(8,128)} %copy-done.11, f32[1024,768]{1,0:T(8,128)} %copy-done, bf16[1024,1792]{1,0:T(8,128)(2,1)} %bitcast.18, bf16[1024,1792]{1,0:T(8,128)(2,1)} %bitcast.27, bf16[1024,1792]{1,0:T(8,128)(2,1)} %bitcast.35), custom_call_target="tpu_custom_call" | custom-call | flops 3932160 | bytes 2097152 | tf_op jit(solution)/shard_map/pallas_call | solution.py:222
  125.9 3.5 %collective-permute-start.15 = (bf16[2,1024,128]{2,1,0:T(8,128)(2,1)}, bf16[2,1024,128]{2,1,0:T(8,128)(2,1)S(1)}, u32[]{:S(2)}, u32[]{:S(2)}) collective-permute-start(bf16[2,1024,128]{2,1,0:T(8,128)(2,1)} %shard_map.89.pair_ref), channel_id=1, source_target_pairs={{0,64},{16,80},{32,96},{48,112},{64,0},{80,16},{96,32},{112,48},{1... | collective-permute-start | bytes 1572872 | tf_op jit(solution)/shard_map/ppermute | solution.py:22
  129.4 2.8 %shard_map.92 = (bf16[2,1024,128]{2,1,0:T(8,128)(2,1)}, bf16[1024,128]{1,0:T(8,128)(2,1)}) custom-call(f32[8,128]{1,0:T(8,128)} %copy-done.11, f32[1024,256]{1,0:T(8,128)} %copy-done.5, bf16[1024,1792]{1,0:T(8,128)(2,1)} %bitcast.19, bf16[1024,1792]{1,0:T(8,128)(2,1)} %bitcast.28, bf16[1024,1792]{1,0:T(8,128)(2,1)} %bitcast.36), custom_call_target="tpu_custom_call" | custom-call | flops 3932160 | bytes 2097152 | tf_op jit(solution)/shard_map/pallas_call | solution.py:222
  132.3 5.7 %shard_map.86 = (bf16[2,1024,384]{2,1,0:T(8,128)(2,1)}, bf16[1024,384]{1,0:T(8,128)(2,1)}) custom-call(f32[8,128]{1,0:T(8,128)} %copy-done.11, f32[1024,768]{1,0:T(8,128)} %copy-done.1, bf16[1024,1792]{1,0:T(8,128)(2,1)} %bitcast.20, bf16[1024,1792]{1,0:T(8,128)(2,1)} %bitcast.29, bf16[1024,1792]{1,0:T(8,128)(2,1)} %bitcast.37), custom_call_target="tpu_custom_call" | custom-call | flops 11796480 | bytes 6291456 | tf_op jit(solution)/shard_map/pallas_call | solution.py:222
  138.0 20.5 %collective-permute-done.13.pair_other_ref.refs_1_ = bf16[2,1024,128]{2,1,0:T(8,128)(2,1)S(1)} collective-permute-done((bf16[2,1024,128]{2,1,0:T(8,128)(2,1)}, bf16[2,1024,128]{2,1,0:T(8,128)(2,1)S(1)}, u32[]{:S(2)}, u32[]{:S(2)}) %collective-permute-start.13) | collective-permute-done | bytes 524320 | tf_op jit(solution)/shard_map/ppermute | solution.py:22
  158.5 2.2 shard_map.90
  160.8 9.0 %collective-permute-done.15.refs_2_.pair_other_ref = bf16[2,1024,128]{2,1,0:T(8,128)(2,1)S(1)} collective-permute-done((bf16[2,1024,128]{2,1,0:T(8,128)(2,1)}, bf16[2,1024,128]{2,1,0:T(8,128)(2,1)S(1)}, u32[]{:S(2)}, u32[]{:S(2)}) %collective-permute-start.15) | collective-permute-done | bytes 524320 | tf_op jit(solution)/shard_map/ppermute | solution.py:22
  169.8 3.6 %collective-permute-start.16 = (bf16[2,1024,384]{2,1,0:T(8,128)(2,1)}, bf16[2,1024,384]{2,1,0:T(8,128)(2,1)S(1)}, u32[]{:S(2)}, u32[]{:S(2)}) collective-permute-start(bf16[2,1024,384]{2,1,0:T(8,128)(2,1)} %shard_map.91.pair_ref), channel_id=1, source_target_pairs={{0,64},{16,80},{32,96},{48,112},{64,0},{80,16},{96,32},{112,48},{1... | collective-permute-start | bytes 4718600 | tf_op jit(solution)/shard_map/ppermute | solution.py:22
  173.3 5.5 %shard_map.99 = (bf16[2,1024,384]{2,1,0:T(8,128)(2,1)}, bf16[1024,384]{1,0:T(8,128)(2,1)}) custom-call(f32[8,128]{1,0:T(8,128)} %copy-done.11, f32[1024,768]{1,0:T(8,128)} %copy-done.1, bf16[1024,1792]{1,0:T(8,128)(2,1)} %bitcast.21, bf16[1024,1792]{1,0:T(8,128)(2,1)} %bitcast.30, bf16[1024,1792]{1,0:T(8,128)(2,1)} %bitcast.38), custom_call_target="tpu_custom_call" | custom-call | flops 11796480 | bytes 6291456 | tf_op jit(solution)/shard_map/pallas_call | solution.py:222
  178.8 2.4 shard_map.94
  182.6 3.5 %collective-permute-start.20 = (bf16[2,1024,384]{2,1,0:T(8,128)(2,1)}, bf16[2,1024,384]{2,1,0:T(8,128)(2,1)}, u32[]{:S(2)}, u32[]{:S(2)}) collective-permute-start(bf16[2,1024,384]{2,1,0:T(8,128)(2,1)} %shard_map.100.pair_ref), channel_id=1, source_target_pairs={{0,64},{16,80},{32,96},{48,112},{64,0},{80,16},{96,32},{112,48},{1... | collective-permute-start | bytes 4718600 | tf_op jit(solution)/shard_map/ppermute | solution.py:22
  187.2 2.9 %shard_map.85 = (bf16[2,1024,128]{2,1,0:T(8,128)(2,1)}, bf16[1024,128]{1,0:T(8,128)(2,1)}) custom-call(f32[8,128]{1,0:T(8,128)} %copy-done.11, f32[1024,256]{1,0:T(8,128)} %copy-done.5, bf16[1024,1792]{1,0:T(8,128)(2,1)} %bitcast.22, bf16[1024,1792]{1,0:T(8,128)(2,1)} %bitcast.31, bf16[1024,1792]{1,0:T(8,128)(2,1)} %bitcast.40), custom_call_target="tpu_custom_call" | custom-call | flops 3932160 | bytes 2097152 | tf_op jit(solution)/shard_map/pallas_call | solution.py:222
  190.0 3.7 %shard_map.95 = (bf16[1024,1792]{1,0:T(8,128)(2,1)}, bf16[1024,1792]{1,0:T(8,128)(2,1)}, bf16[1024,1792]{1,0:T(8,128)(2,1)}, f32[8,128]{1,0:T(8,128)}) custom-call(bf16[2,1040,256]{2,1,0:T(8,128)(2,1)} %shard_map.93.pair_ref, bf16[1024,256]{1,0:T(8,128)(2,1)S(1)} %slice.58.step_ref, ...), custom_call_target="tpu_custom_call", output_to_operand_aliasing={{0}: (4, {}), {1}: (5, {}), {2}: (6, {})} | custom-call | flops 7864320 | bytes 4718592 | tf_op jit(solution)/shard_map/pallas_call | solution.py:237
  193.7 6.3 %shard_map.96 = (bf16[1024,1792]{1,0:T(8,128)(2,1)}, bf16[1024,1792]{1,0:T(8,128)(2,1)}, bf16[1024,1792]{1,0:T(8,128)(2,1)}) custom-call(f32[8,128]{1,0:T(8,128)} %copy-done.11, bf16[2,1040,256]{2,1,0:T(8,128)(2,1)} %copy-done.2, f32[1024,768]{1,0:T(8,128)} %copy-done, ...), custom_call_target="tpu_custom_call", output_to_operand_aliasing={{0}: (11, {}), {1}: (12, {}), {2}: (13, {})} | custom-call | flops 15728640 | bytes 5767168 | tf_op jit(solution)/shard_map/pallas_call | solution.py:259
  200.0 2.5 shard_map.97
  202.5 12.2 %collective-permute-done.16.refs_1_.pair_other_ref = bf16[2,1024,384]{2,1,0:T(8,128)(2,1)S(1)} collective-permute-done((bf16[2,1024,384]{2,1,0:T(8,128)(2,1)}, bf16[2,1024,384]{2,1,0:T(8,128)(2,1)S(1)}, u32[]{:S(2)}, u32[]{:S(2)}) %collective-permute-start.16) | collective-permute-done | bytes 1572896 | tf_op jit(solution)/shard_map/ppermute | solution.py:22
  214.7 3.6 %collective-permute-start.19 = (bf16[2,1024,128]{2,1,0:T(8,128)(2,1)S(1)}, bf16[2,1024,128]{2,1,0:T(8,128)(2,1)S(1)}, u32[]{:S(2)}, u32[]{:S(2)}) collective-permute-start(bf16[2,1024,128]{2,1,0:T(8,128)(2,1)S(1)} %shard_map.98.pair_ref), channel_id=1, source_target_pairs={{0,64},{16,80},{32,96},{48,112},{64,0},{80,16},{96,32},{112,48},{1... | collective-permute-start | bytes 1572872 | tf_op jit(solution)/shard_map/ppermute | solution.py:22
  218.3 3.8 %shard_map.101 = (bf16[1024,1792]{1,0:T(8,128)(2,1)}, bf16[1024,1792]{1,0:T(8,128)(2,1)}, bf16[1024,1792]{1,0:T(8,128)(2,1)}, f32[8,128]{1,0:T(8,128)}) custom-call(bf16[2,1024,384]{2,1,0:T(8,128)(2,1)} %shard_map.91.pair_ref, bf16[1024,384]{1,0:T(8,128)(2,1)S(1)} %copy-done.7, ...), custom_call_target="tpu_custom_call", output_to_operand_aliasing={{0}: (4, {}), {1}: (5, {}), {2}: (6, {})} | custom-call | flops 11796480 | bytes 7077888 | tf_op jit(solution)/shard_map/pallas_call | solution.py:237
  222.1 26.4 %collective-permute-done.20.pair_other_ref = bf16[2,1024,384]{2,1,0:T(8,128)(2,1)} collective-permute-done((bf16[2,1024,384]{2,1,0:T(8,128)(2,1)}, bf16[2,1024,384]{2,1,0:T(8,128)(2,1)}, u32[]{:S(2)}, u32[]{:S(2)}) %collective-permute-start.20) | collective-permute-done | bytes 1572896 | tf_op jit(solution)/shard_map/ppermute | solution.py:22
  248.5 4.3 %shard_map.102 = (bf16[1024,1792]{1,0:T(8,128)(2,1)}, bf16[1024,1792]{1,0:T(8,128)(2,1)}, bf16[1024,1792]{1,0:T(8,128)(2,1)}, f32[8,128]{1,0:T(8,128)}) custom-call(bf16[2,1024,384]{2,1,0:T(8,128)(2,1)} %shard_map.100.pair_ref, bf16[1024,384]{1,0:T(8,128)(2,1)S(1)} %copy-done.8, ...), custom_call_target="tpu_custom_call", output_to_operand_aliasing={{0}: (4, {}), {1}: (5, {}), {2}: (6, {})} | custom-call | flops 11796480 | bytes 7077888 | tf_op jit(solution)/shard_map/pallas_call | solution.py:237
  252.9 5.6 %collective-permute-done.19.pair_other_ref = bf16[2,1024,128]{2,1,0:T(8,128)(2,1)S(1)} collective-permute-done((bf16[2,1024,128]{2,1,0:T(8,128)(2,1)S(1)}, bf16[2,1024,128]{2,1,0:T(8,128)(2,1)S(1)}, u32[]{:S(2)}, u32[]{:S(2)}) %collective-permute-start.19) | collective-permute-done | bytes 524320 | tf_op jit(solution)/shard_map/ppermute | solution.py:22
  258.5 2.2 shard_map.103
  (72 shorter events, 19.4 us)
Async XLA Ops:
  0.6 20.5 %collective-permute-start = (bf16[1024,256]{1,0:T(8,128)(2,1)}, bf16[1024,256]{1,0:T(8,128)(2,1)S(1)}, u32[]{:S(2)}, u32[]{:S(2)}) collective-permute-start(bf16[1024,256]{1,0:T(8,128)(2,1)} %bitcast.47), channel_id=1, source_target_pairs={{0,0},{1,1},{2,2},{3,3},{4,10},{5,11},{6,8},{7,9},{8,6},{9,7},{10,... | collective-permute-start | bytes 1572872 | tf_op jit(solution)/shard_map/ppermute | solution.py:62
  6.4 90.1 %collective-permute-start.6 = (bf16[1024,1792]{1,0:T(8,128)(2,1)}, bf16[1024,1792]{1,0:T(8,128)(2,1)}, u32[]{:S(2)}, u32[]{:S(2)}) collective-permute-start(bf16[1024,1792]{1,0:T(8,128)(2,1)} %bitcast.33), channel_id=1, source_target_pairs={{0,64},{16,80},{32,96},{48,112},{64,0},{80,16},{96,32},{112,48},{1... | collective-permute-start | bytes 11010056 | tf_op jit(solution)/shard_map/ppermute | solution.py:22
  14.1 39.2 %collective-permute-start.1 = (bf16[1024,768]{1,0:T(8,128)(2,1)}, bf16[1024,768]{1,0:T(8,128)(2,1)}, u32[]{:S(2)}, u32[]{:S(2)}) collective-permute-start(bf16[1024,768]{1,0:T(8,128)(2,1)} %get-tuple-element.104.u_ref), channel_id=1, source_target_pairs={{0,8},{8,0},{1,9},{9,1},{2,10},{10,2},{3,11},{11,3},{4,12},{12,4},... | collective-permute-start | bytes 4718600 | tf_op jit(solution)/shard_map/ppermute | solution.py:26
  22.6 30.7 %all-to-all-start = ((bf16[4,1024,256]{2,1,0:T(8,128)(2,1)}), bf16[4,1024,256]{2,1,0:T(8,128)(2,1)S(1)}, u32[]{:S(2)}, u32[]{:S(2)}) async-start(bf16[4,1024,256]{2,1,0:T(8,128)(2,1)} %broadcast_in_dim.12), calls=%async_computation | async-start | bytes 4194304 | tf_op jit(solution)/shard_map/all_to_all | solution.py:67
  26.2 60.7 %collective-permute-start.4 = (bf16[1024,768]{1,0:T(8,128)(2,1)}, bf16[1024,768]{1,0:T(8,128)(2,1)}, u32[]{:S(2)}, u32[]{:S(2)}) collective-permute-start(bf16[1024,768]{1,0:T(8,128)(2,1)} %get-tuple-element.103.u_ref), channel_id=1, source_target_pairs={{0,8},{8,0},{1,9},{9,1},{2,10},{10,2},{3,11},{11,3},{4,12},{12,4},... | collective-permute-start | bytes 4718600 | tf_op jit(solution)/shard_map/ppermute | solution.py:26
  55.4 8.1 %collective-permute-start.2 = (bf16[2,1024,256]{2,1,0:T(8,128)(2,1)}, bf16[2,1024,256]{2,1,0:T(8,128)(2,1)}, u32[]{:S(2)}, u32[]{:S(2)}) collective-permute-start(bf16[2,1024,256]{2,1,0:T(8,128)(2,1)} %get-tuple-element.106), channel_id=1, source_target_pairs={{0,1},{1,0},{2,3},{3,2},{4,5},{5,4},{6,7},{7,6},{8,9},{9,8},{10,11... | collective-permute-start | bytes 3145736 | tf_op jit(solution)/shard_map/ppermute | solution.py:53
  55.4 12.1 %collective-permute-start.3 = (bf16[2,1024,256]{2,1,0:T(8,128)(2,1)}, bf16[2,1024,256]{2,1,0:T(8,128)(2,1)}, u32[]{:S(2)}, u32[]{:S(2)}) collective-permute-start(bf16[2,1024,256]{2,1,0:T(8,128)(2,1)} %get-tuple-element.105), channel_id=1, source_target_pairs={{0,1},{1,0},{2,3},{3,2},{4,5},{5,4},{6,7},{7,6},{8,9},{9,8},{10,11... | collective-permute-start | bytes 3145736 | tf_op jit(solution)/shard_map/ppermute | solution.py:53
  57.8 38.7 %collective-permute-start.5 = (bf16[1024,256]{1,0:T(8,128)(2,1)}, bf16[1024,256]{1,0:T(8,128)(2,1)}, u32[]{:S(2)}, u32[]{:S(2)}) collective-permute-start(bf16[1024,256]{1,0:T(8,128)(2,1)} %slice.53.u_ref), channel_id=1, source_target_pairs={{0,8},{8,0},{1,9},{9,1},{2,10},{10,2},{3,11},{11,3},{4,12},{12,4},... | collective-permute-start | bytes 1572872 | tf_op jit(solution)/shard_map/ppermute | solution.py:26
  63.6 47.2 %collective-permute-start.12 = (bf16[1024,384]{1,0:T(8,128)(2,1)S(1)}, bf16[1024,384]{1,0:T(8,128)(2,1)S(1)}, u32[]{:S(2)}, u32[]{:S(2)}) collective-permute-start(bf16[1024,384]{1,0:T(8,128)(2,1)S(1)} %pad_maximum_fusion), channel_id=1, source_target_pairs={{0,64},{16,80},{32,96},{48,112},{64,0},{80,16},{96,32},{112,48},{1... | collective-permute-start | bytes 2359304 | tf_op jit(solution)/shard_map/ppermute | solution.py:22
  73.3 4.5 %copy-start.4 = (bf16[1024,768]{1,0:T(8,128)(2,1)S(1)}, bf16[1024,768]{1,0:T(8,128)(2,1)}, u32[]{:S(2)}) copy-start(bf16[1024,768]{1,0:T(8,128)(2,1)} %get-tuple-element.103.u_ref) | copy-start | bytes 4718596
  77.5 36.4 %copy-start = (f32[1024,768]{1,0:T(8,128)}, f32[1024,768]{1,0:T(8,128)S(1)}, u32[]{:S(2)}) copy-start(f32[1024,768]{1,0:T(8,128)S(1)} %get-tuple-element.59.grad_ref) | copy-start | bytes 9437188
  77.7 47.6 %collective-permute-start.14 = (bf16[1024,384]{1,0:T(8,128)(2,1)S(1)}, bf16[1024,384]{1,0:T(8,128)(2,1)}, u32[]{:S(2)}, u32[]{:S(2)}) collective-permute-start(bf16[1024,384]{1,0:T(8,128)(2,1)S(1)} %pad_maximum_fusion.1), channel_id=1, source_target_pairs={{0,64},{16,80},{32,96},{48,112},{64,0},{80,16},{96,32},{112,48},{1... | collective-permute-start | bytes 2359304 | tf_op jit(solution)/shard_map/ppermute | solution.py:22
  91.0 1.7 copy-start.1
  99.2 16.5 %copy-start.5 = (f32[1024,256]{1,0:T(8,128)}, f32[1024,256]{1,0:T(8,128)S(1)}, u32[]{:S(2)}) copy-start(f32[1024,256]{1,0:T(8,128)S(1)} %get-tuple-element.55.grad_ref) | copy-start | bytes 3145732
  99.2 1.2 collective-permute-start.7
  100.4 4.8 %collective-permute-start.10 = (f32[8,128]{1,0:T(8,128)S(1)}, f32[8,128]{1,0:T(8,128)S(1)}, u32[]{:S(2)}, u32[]{:S(2)}) collective-permute-start(f32[8,128]{1,0:T(8,128)S(1)} %add.34), channel_id=1, source_target_pairs={{0,6},{1,7},{2,4},{3,5},{4,2},{5,3},{6,0},{7,1},{8,14},{9,15},{10,... | collective-permute-start | bytes 12296 | tf_op jit(solution)/shard_map/ppermute | solution.py:53
  103.2 3.6 %collective-permute-start.8 = (f32[8,128]{1,0:T(8,128)S(1)}, f32[8,128]{1,0:T(8,128)S(1)}, u32[]{:S(2)}, u32[]{:S(2)}) collective-permute-start(f32[8,128]{1,0:T(8,128)S(1)} %add.34), channel_id=1, source_target_pairs={{0,2},{1,3},{2,0},{3,1},{4,6},{5,7},{6,4},{7,5},{8,10},{9,11},{10,... | collective-permute-start | bytes 12296 | tf_op jit(solution)/shard_map/ppermute | solution.py:53
  103.6 5.1 %collective-permute-start.9 = (f32[8,128]{1,0:T(8,128)S(1)}, f32[8,128]{1,0:T(8,128)S(1)}, u32[]{:S(2)}, u32[]{:S(2)}) collective-permute-start(f32[8,128]{1,0:T(8,128)S(1)} %add.34), channel_id=1, source_target_pairs={{0,4},{1,5},{2,6},{3,7},{4,0},{5,1},{6,2},{7,3},{8,12},{9,13},{10,... | collective-permute-start | bytes 12296 | tf_op jit(solution)/shard_map/ppermute | solution.py:53
  108.7 5.1 %collective-permute-start.11 = (f32[8,128]{1,0:T(8,128)S(1)}, f32[8,128]{1,0:T(8,128)S(1)}, u32[]{:S(2)}, u32[]{:S(2)}) collective-permute-start(f32[8,128]{1,0:T(8,128)S(1)} %add_add_fusion.one_ref), channel_id=1, source_target_pairs={{0,8},{8,0},{1,9},{9,1},{2,10},{10,2},{3,11},{11,3},{4,12},{12,4},... | collective-permute-start | bytes 12296 | tf_op jit(solution)/shard_map/ppermute | solution.py:26
  110.8 4.9 %copy-start.3 = (bf16[1024,384]{1,0:T(8,128)(2,1)}, bf16[1024,384]{1,0:T(8,128)(2,1)S(1)}, u32[]{:S(2)}) copy-start(bf16[1024,384]{1,0:T(8,128)(2,1)S(1)} %collective-permute-done.12.rest_0_.first_other_ref.second_other_ref) | copy-start | bytes 2359300
  113.8 5.7 %copy-start.11 = (f32[8,128]{1,0:T(8,128)}, f32[8,128]{1,0:T(8,128)S(1)}, u32[]{:S(2)}) copy-start(f32[8,128]{1,0:T(8,128)S(1)} %shard_map.84.total_ref) | copy-start | bytes 12292
  115.6 65.6 %collective-permute-start.18 = (bf16[2,1040,256]{2,1,0:T(8,128)(2,1)}, bf16[2,1040,256]{2,1,0:T(8,128)(2,1)S(1)}, u32[]{:S(2)}, u32[]{:S(2)}) collective-permute-start(bf16[2,1040,256]{2,1,0:T(8,128)(2,1)} %shard_map.93.pair_ref), channel_id=1, source_target_pairs={{0,64},{16,80},{32,96},{48,112},{64,0},{80,16},{96,32},{112,48},{1... | collective-permute-start | bytes 3194888 | tf_op jit(solution)/shard_map/ppermute | solution.py:22
  122.4 36.2 %collective-permute-start.13 = (bf16[2,1024,128]{2,1,0:T(8,128)(2,1)}, bf16[2,1024,128]{2,1,0:T(8,128)(2,1)S(1)}, u32[]{:S(2)}, u32[]{:S(2)}) collective-permute-start(bf16[2,1024,128]{2,1,0:T(8,128)(2,1)} %get-tuple-element.60.pair_ref), channel_id=1, source_target_pairs={{0,64},{16,80},{32,96},{48,112},{64,0},{80,16},{96,32},{112,48},{1... | collective-permute-start | bytes 1572872 | tf_op jit(solution)/shard_map/ppermute | solution.py:22
  125.9 43.8 %collective-permute-start.15 = (bf16[2,1024,128]{2,1,0:T(8,128)(2,1)}, bf16[2,1024,128]{2,1,0:T(8,128)(2,1)S(1)}, u32[]{:S(2)}, u32[]{:S(2)}) collective-permute-start(bf16[2,1024,128]{2,1,0:T(8,128)(2,1)} %shard_map.89.pair_ref), channel_id=1, source_target_pairs={{0,64},{16,80},{32,96},{48,112},{64,0},{80,16},{96,32},{112,48},{1... | collective-permute-start | bytes 1572872 | tf_op jit(solution)/shard_map/ppermute | solution.py:22
  132.3 48.9 %collective-permute-start.17 = (bf16[2,1024,128]{2,1,0:T(8,128)(2,1)}, bf16[2,1024,128]{2,1,0:T(8,128)(2,1)}, u32[]{:S(2)}, u32[]{:S(2)}) collective-permute-start(bf16[2,1024,128]{2,1,0:T(8,128)(2,1)} %get-tuple-element.64.pair_ref), channel_id=1, source_target_pairs={{0,64},{16,80},{32,96},{48,112},{64,0},{80,16},{96,32},{112,48},{1... | collective-permute-start | bytes 1572872 | tf_op jit(solution)/shard_map/ppermute | solution.py:22
  132.3 26.2 %copy-start.10 = (bf16[2,1024,128]{2,1,0:T(8,128)(2,1)S(1)}, bf16[2,1024,128]{2,1,0:T(8,128)(2,1)}, u32[]{:S(2)}) copy-start(bf16[2,1024,128]{2,1,0:T(8,128)(2,1)} %get-tuple-element.60.pair_ref) | copy-start | bytes 1572868
  132.3 26.2 %copy-start.15 = (bf16[1024,128]{1,0:T(8,128)(2,1)S(1)}, bf16[1024,128]{1,0:T(8,128)(2,1)}, u32[]{:S(2)}) copy-start(bf16[1024,128]{1,0:T(8,128)(2,1)} %get-tuple-element.62.step_ref) | copy-start | bytes 786436
  169.8 9.0 %copy-start.14 = (bf16[1024,128]{1,0:T(8,128)(2,1)S(1)}, bf16[1024,128]{1,0:T(8,128)(2,1)}, u32[]{:S(2)}) copy-start(bf16[1024,128]{1,0:T(8,128)(2,1)} %get-tuple-element.68.step_ref) | copy-start | bytes 786436
  169.8 44.9 %collective-permute-start.16 = (bf16[2,1024,384]{2,1,0:T(8,128)(2,1)}, bf16[2,1024,384]{2,1,0:T(8,128)(2,1)S(1)}, u32[]{:S(2)}, u32[]{:S(2)}) collective-permute-start(bf16[2,1024,384]{2,1,0:T(8,128)(2,1)} %shard_map.91.pair_ref), channel_id=1, source_target_pairs={{0,64},{16,80},{32,96},{48,112},{64,0},{80,16},{96,32},{112,48},{1... | collective-permute-start | bytes 4718600 | tf_op jit(solution)/shard_map/ppermute | solution.py:22
  181.2 8.9 %copy-start.2 = (bf16[2,1040,256]{2,1,0:T(8,128)(2,1)}, bf16[2,1040,256]{2,1,0:T(8,128)(2,1)S(1)}, u32[]{:S(2)}) copy-start(bf16[2,1040,256]{2,1,0:T(8,128)(2,1)S(1)} %collective-permute-done.18.pair_other_ref.clip_other_ref.refs_1_) | copy-start | bytes 3194884
  182.6 65.9 %collective-permute-start.20 = (bf16[2,1024,384]{2,1,0:T(8,128)(2,1)}, bf16[2,1024,384]{2,1,0:T(8,128)(2,1)}, u32[]{:S(2)}, u32[]{:S(2)}) collective-permute-start(bf16[2,1024,384]{2,1,0:T(8,128)(2,1)} %shard_map.100.pair_ref), channel_id=1, source_target_pairs={{0,64},{16,80},{32,96},{48,112},{64,0},{80,16},{96,32},{112,48},{1... | collective-permute-start | bytes 4718600 | tf_op jit(solution)/shard_map/ppermute | solution.py:22
  193.7 6.3 %copy-start.9 = (bf16[2,1024,128]{2,1,0:T(8,128)(2,1)S(1)}, bf16[2,1024,128]{2,1,0:T(8,128)(2,1)}, u32[]{:S(2)}) copy-start(bf16[2,1024,128]{2,1,0:T(8,128)(2,1)} %get-tuple-element.64.pair_ref) | copy-start | bytes 1572868
  193.7 6.3 %copy-start.12 = (bf16[1024,128]{1,0:T(8,128)(2,1)S(1)}, bf16[1024,128]{1,0:T(8,128)(2,1)}, u32[]{:S(2)}) copy-start(bf16[1024,128]{1,0:T(8,128)(2,1)} %get-tuple-element.65.step_ref) | copy-start | bytes 786436
  200.0 14.7 %copy-start.6 = (bf16[2,1024,128]{2,1,0:T(8,128)(2,1)S(1)}, bf16[2,1024,128]{2,1,0:T(8,128)(2,1)}, u32[]{:S(2)}) copy-start(bf16[2,1024,128]{2,1,0:T(8,128)(2,1)} %get-tuple-element.56.refs_0_) | copy-start | bytes 1572868
  200.0 18.3 %copy-start.7 = (bf16[1024,384]{1,0:T(8,128)(2,1)S(1)}, bf16[1024,384]{1,0:T(8,128)(2,1)}, u32[]{:S(2)}) copy-start(bf16[1024,384]{1,0:T(8,128)(2,1)} %get-tuple-element.86.step_ref) | copy-start | bytes 2359300
  214.7 43.8 %collective-permute-start.19 = (bf16[2,1024,128]{2,1,0:T(8,128)(2,1)S(1)}, bf16[2,1024,128]{2,1,0:T(8,128)(2,1)S(1)}, u32[]{:S(2)}, u32[]{:S(2)}) collective-permute-start(bf16[2,1024,128]{2,1,0:T(8,128)(2,1)S(1)} %shard_map.98.pair_ref), channel_id=1, source_target_pairs={{0,64},{16,80},{32,96},{48,112},{64,0},{80,16},{96,32},{112,48},{1... | collective-permute-start | bytes 1572872 | tf_op jit(solution)/shard_map/ppermute | solution.py:22
  218.3 30.2 %copy-start.8 = (bf16[1024,384]{1,0:T(8,128)(2,1)S(1)}, bf16[1024,384]{1,0:T(8,128)(2,1)}, u32[]{:S(2)}) copy-start(bf16[1024,384]{1,0:T(8,128)(2,1)} %get-tuple-element.85.step_ref) | copy-start | bytes 2359300
  248.5 10.0 %copy-start.13 = (bf16[1024,128]{1,0:T(8,128)(2,1)S(1)}, bf16[1024,128]{1,0:T(8,128)(2,1)}, u32[]{:S(2)}) copy-start(bf16[1024,128]{1,0:T(8,128)(2,1)} %get-tuple-element.82.step_ref) | copy-start | bytes 786436

commit v6 on v5

--- a/solution.py
+++ b/solution.py
@@ -231,7 +231,9 @@
 
 def mix(pair, step, ready, pair_other, old_other, at, width, shape, outs):
     rows = shape[0]
-    depth = rows if width == 128 else STEP_ROWS
+    narrow = width == 128
+    depth = rows if narrow else STEP_ROWS
+    inside = pl.BlockSpec(memory_space=pltpu.VMEM)
     wide = pl.BlockSpec((depth, width), lambda i: (i, at // width))
     whole = jax.ShapeDtypeStruct(shape, BF16)
     return pl.pallas_call(
@@ -239,17 +241,17 @@
         grid=(rows // depth,),
         out_shape=(whole, whole, whole, jax.ShapeDtypeStruct((8, 128), F32)),
         in_specs=[
-            pl.BlockSpec((2, depth, width), lambda i: (0, i, 0)),
-            pl.BlockSpec((depth, width), lambda i: (i, 0)),
-            pl.BlockSpec(memory_space=pltpu.VMEM),
-            wide,
+            inside if narrow else pl.BlockSpec((2, depth, width), lambda i: (0, i, 0)),
+            inside if narrow else pl.BlockSpec((depth, width), lambda i: (i, 0)),
+            inside,
+            inside if narrow else wide,
         ]
         + [ANYWHERE] * len(outs),
         out_specs=(wide, wide, wide, TOTAL),
         input_output_aliases={4 + i: i for i in range(len(outs))},
         cost_estimate=cost(rows, width, 30, 18),
         compiler_params=pltpu.CompilerParams(vmem_limit_bytes=16 * 2**20),
-    )(pair, step, pair_other, old_other, *outs)
+    )(pair, step, pair_other, part(old_other, (at, width)) if narrow else old_other, *outs)
 
 
 def early(total, pair_other, grad, grad_other, first, second, other, old, old_other, width, outs):
@@ -338,7 +340,8 @@
     first, second = first_moment[0], second_moment[0]
 
     settled = settle(tokens[0])
-    up = [part(upstream, piece) for piece in UP]
+    later = lax.optimization_barrier((upstream, settled))[0]
+    up = [part(later if i else upstream, piece) for i, piece in enumerate(UP)]
     up_other = [swap_dp(piece) for piece in up]
     old_other = across(old)
     state_other = across(jnp.concatenate([first[:, :EARLY], second[:, : EARLY // 2]], axis=1))

time: 262 us -> 261 us (level)
  local copies, waits for them, and re-layouts: 15.8 us -> 20.6 us
  waiting for transfers between devices: 118 us -> 115 us
    ppermute x4, waiting for transfers between devices: 32.8 us -> 29 us  [swap_dp(): return lax.ppermute(value, 'dp', [(0, 1), (1, 0)])]
    slice x4 -> x6, local copies, waits for them, and re-layouts: 7.77 us -> 10.6 us  [part(): return value[:, piece[0]:piece[0] + piece[1]]]
  transfers between devices with their start and end apart: 22 -> 22, of which waited for: 14 -> 14; matrix products, arithmetic and copies ran while one was open for 6% -> 7% of each run, Pallas kernels for 28% -> 28%
where the time goes in v6:
time: 261 us; the launch traced here: 260 us
  waiting for transfers between devices  115 us (44%)
  Pallas kernels  75.1 us (29%)
  starting transfers between devices  47 us (18%)
  local copies, waits for them, and re-layouts  20.6 us (8%)
    ppermute x10, waiting for transfers between devices, across(): return lax.ppermute(value, 'replica', [(s, s ^ 4) for s in range(8)])  73 us
    ppermute x4, waiting for transfers between devices, swap_dp(): return lax.ppermute(value, 'dp', [(0, 1), (1, 0)])  29 us
    ppermute x10, starting transfers between devices, across(): return lax.ppermute(value, 'replica', [(s, s ^ 4) for s in range(8)])  24.2 us
    pallas_call x6, Pallas kernels, make(): pl.pallas_call(make_kernel, grid=(rows // STEP_ROWS,), out_shape=(jax.Sha...  22.6 us
    pallas_call x7, Pallas kernels, mix(): pl.pallas_call(functools.partial(mix_kernel, ready), grid=(rows // depth,...  19.4 us
    slice x6, local copies, waits for them, and re-layouts, part(): return value[:, piece[0]:piece[0] + piece[1]]  10.6 us
    pallas_call x3, Pallas kernels, finish(): pl.pallas_call(finish_kernel, grid=(blocks // 2,), out_shape=(jax.ShapeDt...  10.4 us
    pallas_call x3, Pallas kernels, local_product(): pl.pallas_call(local_kernel, grid=(blocks // 2,), out_shape=jax.ShapeDtyp...  10.2 us
  transfers between devices with their start and end apart: 22, of which 14 were waited for; matrix products, arithmetic and copies ran while one was open for 7% of the time, Pallas kernels for 28%

profile of v6, /device:TPU:6, one launch (start us, length us, event | category | flops | bytes accessed | tf_op | source)
XLA Modules:
  0.0 259.9 jit_solution(3347011333840348636)
XLA Ops:
  0.6 5.8 %collective-permute-start = (bf16[1024,256]{1,0:T(8,128)(2,1)}, bf16[1024,256]{1,0:T(8,128)(2,1)S(1)}, u32[]{:S(2)}, u32[]{:S(2)}) collective-permute-start(bf16[1024,256]{1,0:T(8,128)(2,1)} %bitcast.48), channel_id=1, source_target_pairs={{0,0},{1,1},{2,2},{3,3},{4,10},{5,11},{6,8},{7,9},{8,6},{9,7},{10,... | collective-permute-start | bytes 1572872 | tf_op jit(solution)/shard_map/ppermute | solution.py:62
  6.4 4.0 %collective-permute-start.6 = (bf16[1024,1792]{1,0:T(8,128)(2,1)}, bf16[1024,1792]{1,0:T(8,128)(2,1)}, u32[]{:S(2)}, u32[]{:S(2)}) collective-permute-start(bf16[1024,1792]{1,0:T(8,128)(2,1)} %bitcast.33), channel_id=1, source_target_pairs={{0,64},{16,80},{32,96},{48,112},{64,0},{80,16},{96,32},{112,48},{1... | collective-permute-start | bytes 11010056 | tf_op jit(solution)/shard_map/ppermute | solution.py:22
  10.4 2.7 %slice.67.u_ref = bf16[1024,768]{1,0:T(8,128)(2,1)} slice(bf16[1024,1792]{1,0:T(8,128)(2,1)} %bitcast.45), slice={[0:1024], [0:768]} | slice | bytes 3145728 | tf_op jit(solution)/shard_map/slice | solution.py:330
  13.0 8.1 %collective-permute-done = bf16[1024,256]{1,0:T(8,128)(2,1)S(1)} collective-permute-done((bf16[1024,256]{1,0:T(8,128)(2,1)}, bf16[1024,256]{1,0:T(8,128)(2,1)S(1)}, u32[]{:S(2)}, u32[]{:S(2)}) %collective-permute-start) | collective-permute-done | bytes 524320 | tf_op jit(solution)/shard_map/ppermute | solution.py:62
  22.6 3.6 %all-to-all-start = ((bf16[4,1024,256]{2,1,0:T(8,128)(2,1)}), bf16[4,1024,256]{2,1,0:T(8,128)(2,1)S(1)}, u32[]{:S(2)}, u32[]{:S(2)}) async-start(bf16[4,1024,256]{2,1,0:T(8,128)(2,1)} %broadcast_in_dim.12), calls=%async_computation | async-start | bytes 4194304 | tf_op jit(solution)/shard_map/all_to_all | solution.py:67
  27.3 2.1 fusion.2
  29.4 2.7 %slice.54.u_ref = bf16[1024,768]{1,0:T(8,128)(2,1)} slice(bf16[1024,1792]{1,0:T(8,128)(2,1)} %bitcast.46), slice={[0:1024], [768:1536]} | slice | bytes 3145728 | tf_op jit(solution)/shard_map/slice | solution.py:330
  32.0 2.1 collective-permute-start.4
  34.1 18.6 %collective-permute-done.1.refs_3_.u_ref = bf16[1024,768]{1,0:T(8,128)(2,1)} collective-permute-done((bf16[1024,768]{1,0:T(8,128)(2,1)}, bf16[1024,768]{1,0:T(8,128)(2,1)}, u32[]{:S(2)}, u32[]{:S(2)}) %collective-permute-start.1) | collective-permute-done | bytes 1572896 | tf_op jit(solution)/shard_map/ppermute | solution.py:26
  57.8 4.1 %collective-permute-start.5 = (bf16[1024,256]{1,0:T(8,128)(2,1)S(1)}, bf16[1024,256]{1,0:T(8,128)(2,1)S(1)}, u32[]{:S(2)}, u32[]{:S(2)}) collective-permute-start(bf16[1024,256]{1,0:T(8,128)(2,1)S(1)} %slice.55.u_ref), channel_id=1, source_target_pairs={{0,8},{8,0},{1,9},{9,1},{2,10},{10,2},{3,11},{11,3},{4,12},{12,4},... | collective-permute-start | bytes 1572872 | tf_op jit(solution)/shard_map/ppermute | solution.py:26
  63.0 4.0 %collective-permute-start.12 = (bf16[1024,384]{1,0:T(8,128)(2,1)S(1)}, bf16[1024,384]{1,0:T(8,128)(2,1)S(1)}, u32[]{:S(2)}, u32[]{:S(2)}) collective-permute-start(bf16[1024,384]{1,0:T(8,128)(2,1)S(1)} %pad_maximum_fusion), channel_id=1, source_target_pairs={{0,64},{16,80},{32,96},{48,112},{64,0},{80,16},{96,32},{112,48},{1... | collective-permute-start | bytes 2359304 | tf_op jit(solution)/shard_map/ppermute | solution.py:22
  66.9 1.8 shard_map.77.x_ref
  68.8 3.9 %shard_map.78.local_ref = f32[1024,768]{1,0:T(8,128)S(1)} custom-call(bf16[8,1024,256]{2,1,0:T(8,128)(2,1)S(1)} %shard_map.77.x_ref, bf16[1024,768]{1,0:T(8,128)(2,1)} %slice.67.u_ref), custom_call_target="tpu_custom_call" | custom-call | bytes 4096 | tf_op jit(solution)/shard_map/pallas_call | solution.py:283
  72.7 4.1 %shard_map.79 = (f32[1024,768]{1,0:T(8,128)S(1)}, f32[8,128]{1,0:T(8,128)S(1)}) custom-call(bf16[8,1024,256]{2,1,0:T(8,128)(2,1)S(1)} %shard_map.77.x_ref, bf16[1024,768]{1,0:T(8,128)(2,1)} %collective-permute-done.1.refs_3_.u_ref, f32[1024,768]{1,0:T(8,128)S(1)} %shard_map.78.local_ref), custom_call_target="tpu_custom_call" | custom-call | bytes 4096 | tf_op jit(solution)/shard_map/pallas_call | solution.py:312
  77.0 4.8 %shard_map.80.local_ref = f32[1024,768]{1,0:T(8,128)S(1)} custom-call(bf16[8,1024,256]{2,1,0:T(8,128)(2,1)S(1)} %shard_map.77.x_ref, bf16[1024,768]{1,0:T(8,128)(2,1)} %slice.54.u_ref), custom_call_target="tpu_custom_call" | custom-call | bytes 4096 | tf_op jit(solution)/shard_map/pallas_call | solution.py:283
  83.3 3.1 %collective-permute-done.4.u_ref = bf16[1024,768]{1,0:T(8,128)(2,1)} collective-permute-done((bf16[1024,768]{1,0:T(8,128)(2,1)}, bf16[1024,768]{1,0:T(8,128)(2,1)}, u32[]{:S(2)}, u32[]{:S(2)}) %collective-permute-start.4) | collective-permute-done | bytes 1572896 | tf_op jit(solution)/shard_map/ppermute | solution.py:26
  86.4 4.1 %shard_map.81 = (f32[1024,768]{1,0:T(8,128)S(1)}, f32[8,128]{1,0:T(8,128)S(1)}) custom-call(bf16[8,1024,256]{2,1,0:T(8,128)(2,1)S(1)} %shard_map.77.x_ref, bf16[1024,768]{1,0:T(8,128)(2,1)} %collective-permute-done.4.u_ref, f32[1024,768]{1,0:T(8,128)S(1)} %shard_map.80.local_ref), custom_call_target="tpu_custom_call" | custom-call | bytes 4096 | tf_op jit(solution)/shard_map/pallas_call | solution.py:312
  90.5 1.7 copy-done.1
  92.2 4.2 %collective-permute-done.5.u_ref = bf16[1024,256]{1,0:T(8,128)(2,1)S(1)} collective-permute-done((bf16[1024,256]{1,0:T(8,128)(2,1)S(1)}, bf16[1024,256]{1,0:T(8,128)(2,1)S(1)}, u32[]{:S(2)}, u32[]{:S(2)}) %collective-permute-start.5) | collective-permute-done | bytes 524320 | tf_op jit(solution)/shard_map/ppermute | solution.py:26
  96.4 2.3 shard_map.83
  100.0 2.8 %collective-permute-start.10 = (f32[8,128]{1,0:T(8,128)S(1)}, f32[8,128]{1,0:T(8,128)S(1)}, u32[]{:S(2)}, u32[]{:S(2)}) collective-permute-start(f32[8,128]{1,0:T(8,128)S(1)} %add.34), channel_id=1, source_target_pairs={{0,6},{1,7},{2,4},{3,5},{4,2},{5,3},{6,0},{7,1},{8,14},{9,15},{10,... | collective-permute-start | bytes 12296 | tf_op jit(solution)/shard_map/ppermute | solution.py:53
  106.4 1.9 collective-permute-done.9
  108.2 2.0 collective-permute-start.11
  110.3 3.1 %collective-permute-done.11.two_ref = f32[8,128]{1,0:T(8,128)S(1)} collective-permute-done((f32[8,128]{1,0:T(8,128)S(1)}, f32[8,128]{1,0:T(8,128)S(1)}, u32[]{:S(2)}, u32[]{:S(2)}) %collective-permute-start.11) | collective-permute-done | bytes 4128 | tf_op jit(solution)/shard_map/ppermute | solution.py:26
  113.4 1.8 shard_map.93.pair_ref
  115.2 3.9 %collective-permute-start.18 = (bf16[2,1040,256]{2,1,0:T(8,128)(2,1)}, bf16[2,1040,256]{2,1,0:T(8,128)(2,1)S(1)}, u32[]{:S(2)}, u32[]{:S(2)}) collective-permute-start(bf16[2,1040,256]{2,1,0:T(8,128)(2,1)} %shard_map.93.pair_ref), channel_id=1, source_target_pairs={{0,64},{16,80},{32,96},{48,112},{64,0},{80,16},{96,32},{112,48},{1... | collective-permute-start | bytes 3194888 | tf_op jit(solution)/shard_map/ppermute | solution.py:22
  119.1 2.8 %shard_map.87 = (bf16[2,1024,128]{2,1,0:T(8,128)(2,1)}, bf16[1024,128]{1,0:T(8,128)(2,1)}) custom-call(f32[8,128]{1,0:T(8,128)} %copy-done.16, f32[1024,768]{1,0:T(8,128)} %copy-done, bf16[1024,1792]{1,0:T(8,128)(2,1)} %bitcast.17, bf16[1024,1792]{1,0:T(8,128)(2,1)} %bitcast.26, bf16[1024,1792]{1,0:T(8,128)(2,1)} %bitcast.34), custom_call_target="tpu_custom_call" | custom-call | flops 3932160 | bytes 2097152 | tf_op jit(solution)/shard_map/pallas_call | solution.py:222
  121.9 2.9 %shard_map.88 = (bf16[2,1024,128]{2,1,0:T(8,128)(2,1)}, bf16[1024,128]{1,0:T(8,128)(2,1)}) custom-call(f32[8,128]{1,0:T(8,128)} %copy-done.16, f32[1024,768]{1,0:T(8,128)} %copy-done, bf16[1024,1792]{1,0:T(8,128)(2,1)} %bitcast.18, bf16[1024,1792]{1,0:T(8,128)(2,1)} %bitcast.27, bf16[1024,1792]{1,0:T(8,128)(2,1)} %bitcast.35), custom_call_target="tpu_custom_call" | custom-call | flops 3932160 | bytes 2097152 | tf_op jit(solution)/shard_map/pallas_call | solution.py:222
  125.5 3.5 %collective-permute-start.15 = (bf16[2,1024,128]{2,1,0:T(8,128)(2,1)}, bf16[2,1024,128]{2,1,0:T(8,128)(2,1)S(1)}, u32[]{:S(2)}, u32[]{:S(2)}) collective-permute-start(bf16[2,1024,128]{2,1,0:T(8,128)(2,1)} %shard_map.89.pair_ref), channel_id=1, source_target_pairs={{0,64},{16,80},{32,96},{48,112},{64,0},{80,16},{96,32},{112,48},{1... | collective-permute-start | bytes 1572872 | tf_op jit(solution)/shard_map/ppermute | solution.py:22
  129.0 2.1 fusion
  131.1 2.9 %shard_map.92 = (bf16[2,1024,128]{2,1,0:T(8,128)(2,1)}, bf16[1024,128]{1,0:T(8,128)(2,1)}) custom-call(f32[8,128]{1,0:T(8,128)} %copy-done.16, f32[1024,256]{1,0:T(8,128)} %copy-done.8, bf16[1024,1792]{1,0:T(8,128)(2,1)} %bitcast.19, bf16[1024,1792]{1,0:T(8,128)(2,1)} %bitcast.28, bf16[1024,1792]{1,0:T(8,128)(2,1)} %bitcast.36), custom_call_target="tpu_custom_call" | custom-call | flops 3932160 | bytes 2097152 | tf_op jit(solution)/shard_map/pallas_call | solution.py:222
  134.0 5.7 %shard_map.86 = (bf16[2,1024,384]{2,1,0:T(8,128)(2,1)}, bf16[1024,384]{1,0:T(8,128)(2,1)}) custom-call(f32[8,128]{1,0:T(8,128)} %copy-done.16, f32[1024,768]{1,0:T(8,128)} %copy-done.1, bf16[1024,1792]{1,0:T(8,128)(2,1)} %bitcast.20, bf16[1024,1792]{1,0:T(8,128)(2,1)} %bitcast.29, bf16[1024,1792]{1,0:T(8,128)(2,1)} %bitcast.37), custom_call_target="tpu_custom_call" | custom-call | flops 11796480 | bytes 6291456 | tf_op jit(solution)/shard_map/pallas_call | solution.py:222
  139.7 18.9 %collective-permute-done.13.pair_other_ref.refs_1_ = bf16[2,1024,128]{2,1,0:T(8,128)(2,1)S(1)} collective-permute-done((bf16[2,1024,128]{2,1,0:T(8,128)(2,1)}, bf16[2,1024,128]{2,1,0:T(8,128)(2,1)S(1)}, u32[]{:S(2)}, u32[]{:S(2)}) %collective-permute-start.13) | collective-permute-done | bytes 524320 | tf_op jit(solution)/shard_map/ppermute | solution.py:22
  159.9 9.9 %collective-permute-done.15.refs_2_.pair_other_ref = bf16[2,1024,128]{2,1,0:T(8,128)(2,1)S(1)} collective-permute-done((bf16[2,1024,128]{2,1,0:T(8,128)(2,1)}, bf16[2,1024,128]{2,1,0:T(8,128)(2,1)S(1)}, u32[]{:S(2)}, u32[]{:S(2)}) %collective-permute-start.15) | collective-permute-done | bytes 524320 | tf_op jit(solution)/shard_map/ppermute | solution.py:22
  169.8 3.6 %collective-permute-start.16 = (bf16[2,1024,384]{2,1,0:T(8,128)(2,1)}, bf16[2,1024,384]{2,1,0:T(8,128)(2,1)S(1)}, u32[]{:S(2)}, u32[]{:S(2)}) collective-permute-start(bf16[2,1024,384]{2,1,0:T(8,128)(2,1)} %shard_map.91.pair_ref), channel_id=1, source_target_pairs={{0,64},{16,80},{32,96},{48,112},{64,0},{80,16},{96,32},{112,48},{1... | collective-permute-start | bytes 4718600 | tf_op jit(solution)/shard_map/ppermute | solution.py:22
  173.3 5.4 %shard_map.99 = (bf16[2,1024,384]{2,1,0:T(8,128)(2,1)}, bf16[1024,384]{1,0:T(8,128)(2,1)}) custom-call(f32[8,128]{1,0:T(8,128)} %copy-done.16, f32[1024,768]{1,0:T(8,128)} %copy-done.1, bf16[1024,1792]{1,0:T(8,128)(2,1)} %bitcast.21, bf16[1024,1792]{1,0:T(8,128)(2,1)} %bitcast.30, bf16[1024,1792]{1,0:T(8,128)(2,1)} %bitcast.38), custom_call_target="tpu_custom_call" | custom-call | flops 11796480 | bytes 6291456 | tf_op jit(solution)/shard_map/pallas_call | solution.py:222
  180.6 2.4 shard_map.94
  184.4 1.6 collective-permute-start.20
  187.2 2.9 %shard_map.85 = (bf16[2,1024,128]{2,1,0:T(8,128)(2,1)}, bf16[1024,128]{1,0:T(8,128)(2,1)}) custom-call(f32[8,128]{1,0:T(8,128)} %copy-done.16, f32[1024,256]{1,0:T(8,128)} %copy-done.8, bf16[1024,1792]{1,0:T(8,128)(2,1)} %bitcast.22, bf16[1024,1792]{1,0:T(8,128)(2,1)} %bitcast.31, bf16[1024,1792]{1,0:T(8,128)(2,1)} %bitcast.40), custom_call_target="tpu_custom_call" | custom-call | flops 3932160 | bytes 2097152 | tf_op jit(solution)/shard_map/pallas_call | solution.py:222
  190.1 3.7 %shard_map.95 = (bf16[1024,1792]{1,0:T(8,128)(2,1)}, bf16[1024,1792]{1,0:T(8,128)(2,1)}, bf16[1024,1792]{1,0:T(8,128)(2,1)}, f32[8,128]{1,0:T(8,128)}) custom-call(bf16[2,1040,256]{2,1,0:T(8,128)(2,1)} %shard_map.93.pair_ref, bf16[1024,256]{1,0:T(8,128)(2,1)S(1)} %slice.74.step_ref, ...), custom_call_target="tpu_custom_call", output_to_operand_aliasing={{0}: (4, {}), {1}: (5, {}), {2}: (6, {})} | custom-call | flops 7864320 | bytes 4718592 | tf_op jit(solution)/shard_map/pallas_call | solution.py:239
  193.7 6.3 %shard_map.96 = (bf16[1024,1792]{1,0:T(8,128)(2,1)}, bf16[1024,1792]{1,0:T(8,128)(2,1)}, bf16[1024,1792]{1,0:T(8,128)(2,1)}) custom-call(f32[8,128]{1,0:T(8,128)} %copy-done.16, bf16[2,1040,256]{2,1,0:T(8,128)(2,1)} %copy-done.2, f32[1024,768]{1,0:T(8,128)} %copy-done, ...), custom_call_target="tpu_custom_call", output_to_operand_aliasing={{0}: (11, {}), {1}: (12, {}), {2}: (13, {})} | custom-call | flops 15728640 | bytes 5767168 | tf_op jit(solution)/shard_map/pallas_call | solution.py:261
  200.1 2.5 shard_map.97
  202.6 12.1 %collective-permute-done.16.refs_1_.pair_other_ref = bf16[2,1024,384]{2,1,0:T(8,128)(2,1)S(1)} collective-permute-done((bf16[2,1024,384]{2,1,0:T(8,128)(2,1)}, bf16[2,1024,384]{2,1,0:T(8,128)(2,1)S(1)}, u32[]{:S(2)}, u32[]{:S(2)}) %collective-permute-start.16) | collective-permute-done | bytes 1572896 | tf_op jit(solution)/shard_map/ppermute | solution.py:22
  214.7 3.6 %collective-permute-start.19 = (bf16[2,1024,128]{2,1,0:T(8,128)(2,1)S(1)}, bf16[2,1024,128]{2,1,0:T(8,128)(2,1)S(1)}, u32[]{:S(2)}, u32[]{:S(2)}) collective-permute-start(bf16[2,1024,128]{2,1,0:T(8,128)(2,1)S(1)} %shard_map.98.pair_ref), channel_id=1, source_target_pairs={{0,64},{16,80},{32,96},{48,112},{64,0},{80,16},{96,32},{112,48},{1... | collective-permute-start | bytes 1572872 | tf_op jit(solution)/shard_map/ppermute | solution.py:22
  218.3 3.8 %shard_map.101 = (bf16[1024,1792]{1,0:T(8,128)(2,1)}, bf16[1024,1792]{1,0:T(8,128)(2,1)}, bf16[1024,1792]{1,0:T(8,128)(2,1)}, f32[8,128]{1,0:T(8,128)}) custom-call(bf16[2,1024,384]{2,1,0:T(8,128)(2,1)} %shard_map.91.pair_ref, bf16[1024,384]{1,0:T(8,128)(2,1)S(1)} %copy-done.12, ...), custom_call_target="tpu_custom_call", output_to_operand_aliasing={{0}: (4, {}), {1}: (5, {}), {2}: (6, {})} | custom-call | flops 11796480 | bytes 7077888 | tf_op jit(solution)/shard_map/pallas_call | solution.py:239
  222.1 26.4 %collective-permute-done.20.pair_other_ref = bf16[2,1024,384]{2,1,0:T(8,128)(2,1)} collective-permute-done((bf16[2,1024,384]{2,1,0:T(8,128)(2,1)}, bf16[2,1024,384]{2,1,0:T(8,128)(2,1)}, u32[]{:S(2)}, u32[]{:S(2)}) %collective-permute-start.20) | collective-permute-done | bytes 1572896 | tf_op jit(solution)/shard_map/ppermute | solution.py:22
  248.5 4.3 %shard_map.102 = (bf16[1024,1792]{1,0:T(8,128)(2,1)}, bf16[1024,1792]{1,0:T(8,128)(2,1)}, bf16[1024,1792]{1,0:T(8,128)(2,1)}, f32[8,128]{1,0:T(8,128)}) custom-call(bf16[2,1024,384]{2,1,0:T(8,128)(2,1)} %shard_map.100.pair_ref, bf16[1024,384]{1,0:T(8,128)(2,1)S(1)} %copy-done.13, ...), custom_call_target="tpu_custom_call", output_to_operand_aliasing={{0}: (4, {}), {1}: (5, {}), {2}: (6, {})} | custom-call | flops 11796480 | bytes 7077888 | tf_op jit(solution)/shard_map/pallas_call | solution.py:239
  252.9 5.6 %collective-permute-done.19.pair_other_ref = bf16[2,1024,128]{2,1,0:T(8,128)(2,1)S(1)} collective-permute-done((bf16[2,1024,128]{2,1,0:T(8,128)(2,1)S(1)}, bf16[2,1024,128]{2,1,0:T(8,128)(2,1)S(1)}, u32[]{:S(2)}, u32[]{:S(2)}) %collective-permute-start.19) | collective-permute-done | bytes 524320 | tf_op jit(solution)/shard_map/ppermute | solution.py:22
  (84 shorter events, 23.1 us)
Async XLA Ops:
  0.6 20.5 %collective-permute-start = (bf16[1024,256]{1,0:T(8,128)(2,1)}, bf16[1024,256]{1,0:T(8,128)(2,1)S(1)}, u32[]{:S(2)}, u32[]{:S(2)}) collective-permute-start(bf16[1024,256]{1,0:T(8,128)(2,1)} %bitcast.48), channel_id=1, source_target_pairs={{0,0},{1,1},{2,2},{3,3},{4,10},{5,11},{6,8},{7,9},{8,6},{9,7},{10,... | collective-permute-start | bytes 1572872 | tf_op jit(solution)/shard_map/ppermute | solution.py:62
  6.4 90.0 %collective-permute-start.6 = (bf16[1024,1792]{1,0:T(8,128)(2,1)}, bf16[1024,1792]{1,0:T(8,128)(2,1)}, u32[]{:S(2)}, u32[]{:S(2)}) collective-permute-start(bf16[1024,1792]{1,0:T(8,128)(2,1)} %bitcast.33), channel_id=1, source_target_pairs={{0,64},{16,80},{32,96},{48,112},{64,0},{80,16},{96,32},{112,48},{1... | collective-permute-start | bytes 11010056 | tf_op jit(solution)/shard_map/ppermute | solution.py:22
  13.0 39.7 %collective-permute-start.1 = (bf16[1024,768]{1,0:T(8,128)(2,1)}, bf16[1024,768]{1,0:T(8,128)(2,1)}, u32[]{:S(2)}, u32[]{:S(2)}) collective-permute-start(bf16[1024,768]{1,0:T(8,128)(2,1)} %slice.67.u_ref), channel_id=1, source_target_pairs={{0,8},{8,0},{1,9},{9,1},{2,10},{10,2},{3,11},{11,3},{4,12},{12,4},... | collective-permute-start | bytes 4718600 | tf_op jit(solution)/shard_map/ppermute | solution.py:26
  22.6 30.1 %all-to-all-start = ((bf16[4,1024,256]{2,1,0:T(8,128)(2,1)}), bf16[4,1024,256]{2,1,0:T(8,128)(2,1)S(1)}, u32[]{:S(2)}, u32[]{:S(2)}) async-start(bf16[4,1024,256]{2,1,0:T(8,128)(2,1)} %broadcast_in_dim.12), calls=%async_computation | async-start | bytes 4194304 | tf_op jit(solution)/shard_map/all_to_all | solution.py:67
  32.0 54.4 %collective-permute-start.4 = (bf16[1024,768]{1,0:T(8,128)(2,1)}, bf16[1024,768]{1,0:T(8,128)(2,1)}, u32[]{:S(2)}, u32[]{:S(2)}) collective-permute-start(bf16[1024,768]{1,0:T(8,128)(2,1)} %slice.54.u_ref), channel_id=1, source_target_pairs={{0,8},{8,0},{1,9},{9,1},{2,10},{10,2},{3,11},{11,3},{4,12},{12,4},... | collective-permute-start | bytes 4718600 | tf_op jit(solution)/shard_map/ppermute | solution.py:26
  53.4 9.5 %copy-start.4 = (bf16[1024,256]{1,0:T(8,128)(2,1)}, bf16[1024,256]{1,0:T(8,128)(2,1)S(1)}, u32[]{:S(2)}) copy-start(bf16[1024,256]{1,0:T(8,128)(2,1)S(1)} %get-tuple-element.69.second_ref) | copy-start | bytes 1572868
  53.4 9.6 %copy-start.6 = (bf16[1024,256]{1,0:T(8,128)(2,1)}, bf16[1024,256]{1,0:T(8,128)(2,1)S(1)}, u32[]{:S(2)}) copy-start(bf16[1024,256]{1,0:T(8,128)(2,1)S(1)} %get-tuple-element.68.first_ref) | copy-start | bytes 1572868
  55.0 8.0 %collective-permute-start.2 = (bf16[2,1024,256]{2,1,0:T(8,128)(2,1)}, bf16[2,1024,256]{2,1,0:T(8,128)(2,1)}, u32[]{:S(2)}, u32[]{:S(2)}) collective-permute-start(bf16[2,1024,256]{2,1,0:T(8,128)(2,1)} %get-tuple-element.110), channel_id=1, source_target_pairs={{0,1},{1,0},{2,3},{3,2},{4,5},{5,4},{6,7},{7,6},{8,9},{9,8},{10,11... | collective-permute-start | bytes 3145736 | tf_op jit(solution)/shard_map/ppermute | solution.py:53
  55.0 11.9 %collective-permute-start.3 = (bf16[2,1024,256]{2,1,0:T(8,128)(2,1)}, bf16[2,1024,256]{2,1,0:T(8,128)(2,1)}, u32[]{:S(2)}, u32[]{:S(2)}) collective-permute-start(bf16[2,1024,256]{2,1,0:T(8,128)(2,1)} %get-tuple-element.109), channel_id=1, source_target_pairs={{0,1},{1,0},{2,3},{3,2},{4,5},{5,4},{6,7},{7,6},{8,9},{9,8},{10,11... | collective-permute-start | bytes 3145736 | tf_op jit(solution)/shard_map/ppermute | solution.py:53
  57.8 38.7 %collective-permute-start.5 = (bf16[1024,256]{1,0:T(8,128)(2,1)S(1)}, bf16[1024,256]{1,0:T(8,128)(2,1)S(1)}, u32[]{:S(2)}, u32[]{:S(2)}) collective-permute-start(bf16[1024,256]{1,0:T(8,128)(2,1)S(1)} %slice.55.u_ref), channel_id=1, source_target_pairs={{0,8},{8,0},{1,9},{9,1},{2,10},{10,2},{3,11},{11,3},{4,12},{12,4},... | collective-permute-start | bytes 1572872 | tf_op jit(solution)/shard_map/ppermute | solution.py:26
  63.0 47.3 %collective-permute-start.12 = (bf16[1024,384]{1,0:T(8,128)(2,1)S(1)}, bf16[1024,384]{1,0:T(8,128)(2,1)S(1)}, u32[]{:S(2)}, u32[]{:S(2)}) collective-permute-start(bf16[1024,384]{1,0:T(8,128)(2,1)S(1)} %pad_maximum_fusion), channel_id=1, source_target_pairs={{0,64},{16,80},{32,96},{48,112},{64,0},{80,16},{96,32},{112,48},{1... | collective-permute-start | bytes 2359304 | tf_op jit(solution)/shard_map/ppermute | solution.py:22
  76.8 36.6 %copy-start = (f32[1024,768]{1,0:T(8,128)}, f32[1024,768]{1,0:T(8,128)S(1)}, u32[]{:S(2)}) copy-start(f32[1024,768]{1,0:T(8,128)S(1)} %get-tuple-element.61.grad_ref) | copy-start | bytes 9437188
  76.9 47.9 %collective-permute-start.14 = (bf16[1024,384]{1,0:T(8,128)(2,1)S(1)}, bf16[1024,384]{1,0:T(8,128)(2,1)}, u32[]{:S(2)}, u32[]{:S(2)}) collective-permute-start(bf16[1024,384]{1,0:T(8,128)(2,1)S(1)} %pad_maximum_fusion.1), channel_id=1, source_target_pairs={{0,64},{16,80},{32,96},{48,112},{64,0},{80,16},{96,32},{112,48},{1... | collective-permute-start | bytes 2359304 | tf_op jit(solution)/shard_map/ppermute | solution.py:22
  90.5 1.7 copy-start.1
  92.2 21.1 %copy-start.5 = (bf16[1024,256]{1,0:T(8,128)(2,1)S(1)}, bf16[1024,256]{1,0:T(8,128)(2,1)}, u32[]{:S(2)}) copy-start(bf16[1024,256]{1,0:T(8,128)(2,1)} %copy-done.4) | copy-start | bytes 1572868
  92.2 21.1 %copy-start.7 = (bf16[1024,256]{1,0:T(8,128)(2,1)S(1)}, bf16[1024,256]{1,0:T(8,128)(2,1)}, u32[]{:S(2)}) copy-start(bf16[1024,256]{1,0:T(8,128)(2,1)} %copy-done.6) | copy-start | bytes 1572868
  98.7 16.5 %copy-start.8 = (f32[1024,256]{1,0:T(8,128)}, f32[1024,256]{1,0:T(8,128)S(1)}, u32[]{:S(2)}) copy-start(f32[1024,256]{1,0:T(8,128)S(1)} %get-tuple-element.57.grad_ref) | copy-start | bytes 3145732
  98.7 1.2 collective-permute-start.7
  100.0 4.8 %collective-permute-start.10 = (f32[8,128]{1,0:T(8,128)S(1)}, f32[8,128]{1,0:T(8,128)S(1)}, u32[]{:S(2)}, u32[]{:S(2)}) collective-permute-start(f32[8,128]{1,0:T(8,128)S(1)} %add.34), channel_id=1, source_target_pairs={{0,6},{1,7},{2,4},{3,5},{4,2},{5,3},{6,0},{7,1},{8,14},{9,15},{10,... | collective-permute-start | bytes 12296 | tf_op jit(solution)/shard_map/ppermute | solution.py:53
  102.8 3.6 %collective-permute-start.8 = (f32[8,128]{1,0:T(8,128)S(1)}, f32[8,128]{1,0:T(8,128)S(1)}, u32[]{:S(2)}, u32[]{:S(2)}) collective-permute-start(f32[8,128]{1,0:T(8,128)S(1)} %add.34), channel_id=1, source_target_pairs={{0,2},{1,3},{2,0},{3,1},{4,6},{5,7},{6,4},{7,5},{8,10},{9,11},{10,... | collective-permute-start | bytes 12296 | tf_op jit(solution)/shard_map/ppermute | solution.py:53
  103.1 5.1 %collective-permute-start.9 = (f32[8,128]{1,0:T(8,128)S(1)}, f32[8,128]{1,0:T(8,128)S(1)}, u32[]{:S(2)}, u32[]{:S(2)}) collective-permute-start(f32[8,128]{1,0:T(8,128)S(1)} %add.34), channel_id=1, source_target_pairs={{0,4},{1,5},{2,6},{3,7},{4,0},{5,1},{6,2},{7,3},{8,12},{9,13},{10,... | collective-permute-start | bytes 12296 | tf_op jit(solution)/shard_map/ppermute | solution.py:53
  108.2 5.1 %collective-permute-start.11 = (f32[8,128]{1,0:T(8,128)S(1)}, f32[8,128]{1,0:T(8,128)S(1)}, u32[]{:S(2)}, u32[]{:S(2)}) collective-permute-start(f32[8,128]{1,0:T(8,128)S(1)} %add_add_fusion.one_ref), channel_id=1, source_target_pairs={{0,8},{8,0},{1,9},{9,1},{2,10},{10,2},{3,11},{11,3},{4,12},{12,4},... | collective-permute-start | bytes 12296 | tf_op jit(solution)/shard_map/ppermute | solution.py:26
  110.3 4.9 %copy-start.3 = (bf16[1024,384]{1,0:T(8,128)(2,1)}, bf16[1024,384]{1,0:T(8,128)(2,1)S(1)}, u32[]{:S(2)}) copy-start(bf16[1024,384]{1,0:T(8,128)(2,1)S(1)} %collective-permute-done.12.rest_0_.first_other_ref.second_other_ref) | copy-start | bytes 2359300
  113.4 5.7 %copy-start.16 = (f32[8,128]{1,0:T(8,128)}, f32[8,128]{1,0:T(8,128)S(1)}, u32[]{:S(2)}) copy-start(f32[8,128]{1,0:T(8,128)S(1)} %shard_map.84.total_ref) | copy-start | bytes 12292
  115.2 67.8 %collective-permute-start.18 = (bf16[2,1040,256]{2,1,0:T(8,128)(2,1)}, bf16[2,1040,256]{2,1,0:T(8,128)(2,1)S(1)}, u32[]{:S(2)}, u32[]{:S(2)}) collective-permute-start(bf16[2,1040,256]{2,1,0:T(8,128)(2,1)} %shard_map.93.pair_ref), channel_id=1, source_target_pairs={{0,64},{16,80},{32,96},{48,112},{64,0},{80,16},{96,32},{112,48},{1... | collective-permute-start | bytes 3194888 | tf_op jit(solution)/shard_map/ppermute | solution.py:22
  121.9 36.6 %collective-permute-start.13 = (bf16[2,1024,128]{2,1,0:T(8,128)(2,1)}, bf16[2,1024,128]{2,1,0:T(8,128)(2,1)S(1)}, u32[]{:S(2)}, u32[]{:S(2)}) collective-permute-start(bf16[2,1024,128]{2,1,0:T(8,128)(2,1)} %get-tuple-element.62.pair_ref), channel_id=1, source_target_pairs={{0,64},{16,80},{32,96},{48,112},{64,0},{80,16},{96,32},{112,48},{1... | collective-permute-start | bytes 1572872 | tf_op jit(solution)/shard_map/ppermute | solution.py:22
  125.5 44.3 %collective-permute-start.15 = (bf16[2,1024,128]{2,1,0:T(8,128)(2,1)}, bf16[2,1024,128]{2,1,0:T(8,128)(2,1)S(1)}, u32[]{:S(2)}, u32[]{:S(2)}) collective-permute-start(bf16[2,1024,128]{2,1,0:T(8,128)(2,1)} %shard_map.89.pair_ref), channel_id=1, source_target_pairs={{0,64},{16,80},{32,96},{48,112},{64,0},{80,16},{96,32},{112,48},{1... | collective-permute-start | bytes 1572872 | tf_op jit(solution)/shard_map/ppermute | solution.py:22
  134.0 49.1 %collective-permute-start.17 = (bf16[2,1024,128]{2,1,0:T(8,128)(2,1)}, bf16[2,1024,128]{2,1,0:T(8,128)(2,1)}, u32[]{:S(2)}, u32[]{:S(2)}) collective-permute-start(bf16[2,1024,128]{2,1,0:T(8,128)(2,1)} %get-tuple-element.66.pair_ref), channel_id=1, source_target_pairs={{0,64},{16,80},{32,96},{48,112},{64,0},{80,16},{96,32},{112,48},{1... | collective-permute-start | bytes 1572872 | tf_op jit(solution)/shard_map/ppermute | solution.py:22
  134.0 24.5 %copy-start.15 = (bf16[2,1024,128]{2,1,0:T(8,128)(2,1)S(1)}, bf16[2,1024,128]{2,1,0:T(8,128)(2,1)}, u32[]{:S(2)}) copy-start(bf16[2,1024,128]{2,1,0:T(8,128)(2,1)} %get-tuple-element.62.pair_ref) | copy-start | bytes 1572868
  134.0 24.6 %copy-start.20 = (bf16[1024,128]{1,0:T(8,128)(2,1)S(1)}, bf16[1024,128]{1,0:T(8,128)(2,1)}, u32[]{:S(2)}) copy-start(bf16[1024,128]{1,0:T(8,128)(2,1)} %get-tuple-element.64.step_ref) | copy-start | bytes 786436
  169.8 44.9 %collective-permute-start.16 = (bf16[2,1024,384]{2,1,0:T(8,128)(2,1)}, bf16[2,1024,384]{2,1,0:T(8,128)(2,1)S(1)}, u32[]{:S(2)}, u32[]{:S(2)}) collective-permute-start(bf16[2,1024,384]{2,1,0:T(8,128)(2,1)} %shard_map.91.pair_ref), channel_id=1, source_target_pairs={{0,64},{16,80},{32,96},{48,112},{64,0},{80,16},{96,32},{112,48},{1... | collective-permute-start | bytes 4718600 | tf_op jit(solution)/shard_map/ppermute | solution.py:22
  178.7 0.9 copy-start.11
  179.7 0.9 copy-start.19
  183.0 7.0 %copy-start.2 = (bf16[2,1040,256]{2,1,0:T(8,128)(2,1)}, bf16[2,1040,256]{2,1,0:T(8,128)(2,1)S(1)}, u32[]{:S(2)}) copy-start(bf16[2,1040,256]{2,1,0:T(8,128)(2,1)S(1)} %collective-permute-done.18.pair_other_ref.clip_other_ref.refs_1_) | copy-start | bytes 3194884
  184.4 64.1 %collective-permute-start.20 = (bf16[2,1024,384]{2,1,0:T(8,128)(2,1)}, bf16[2,1024,384]{2,1,0:T(8,128)(2,1)}, u32[]{:S(2)}, u32[]{:S(2)}) collective-permute-start(bf16[2,1024,384]{2,1,0:T(8,128)(2,1)} %shard_map.100.pair_ref), channel_id=1, source_target_pairs={{0,64},{16,80},{32,96},{48,112},{64,0},{80,16},{96,32},{112,48},{1... | collective-permute-start | bytes 4718600 | tf_op jit(solution)/shard_map/ppermute | solution.py:22
  193.7 6.3 %copy-start.10 = (bf16[1024,128]{1,0:T(8,128)(2,1)S(1)}, bf16[1024,128]{1,0:T(8,128)(2,1)}, u32[]{:S(2)}) copy-start(bf16[1024,128]{1,0:T(8,128)(2,1)} %get-tuple-element.103.old_other_ref) | copy-start | bytes 786436
  193.7 6.3 %copy-start.14 = (bf16[2,1024,128]{2,1,0:T(8,128)(2,1)S(1)}, bf16[2,1024,128]{2,1,0:T(8,128)(2,1)}, u32[]{:S(2)}) copy-start(bf16[2,1024,128]{2,1,0:T(8,128)(2,1)} %get-tuple-element.66.pair_ref) | copy-start | bytes 1572868
  193.7 6.3 %copy-start.17 = (bf16[1024,128]{1,0:T(8,128)(2,1)S(1)}, bf16[1024,128]{1,0:T(8,128)(2,1)}, u32[]{:S(2)}) copy-start(bf16[1024,128]{1,0:T(8,128)(2,1)} %get-tuple-element.67.step_ref) | copy-start | bytes 786436
  200.1 14.7 %copy-start.9 = (bf16[2,1024,128]{2,1,0:T(8,128)(2,1)S(1)}, bf16[2,1024,128]{2,1,0:T(8,128)(2,1)}, u32[]{:S(2)}) copy-start(bf16[2,1024,128]{2,1,0:T(8,128)(2,1)} %get-tuple-element.58.refs_0_) | copy-start | bytes 1572868
  200.1 18.2 %copy-start.12 = (bf16[1024,384]{1,0:T(8,128)(2,1)S(1)}, bf16[1024,384]{1,0:T(8,128)(2,1)}, u32[]{:S(2)}) copy-start(bf16[1024,384]{1,0:T(8,128)(2,1)} %get-tuple-element.88.step_ref) | copy-start | bytes 2359300
  214.7 43.8 %collective-permute-start.19 = (bf16[2,1024,128]{2,1,0:T(8,128)(2,1)S(1)}, bf16[2,1024,128]{2,1,0:T(8,128)(2,1)S(1)}, u32[]{:S(2)}, u32[]{:S(2)}) collective-permute-start(bf16[2,1024,128]{2,1,0:T(8,128)(2,1)S(1)} %shard_map.98.pair_ref), channel_id=1, source_target_pairs={{0,64},{16,80},{32,96},{48,112},{64,0},{80,16},{96,32},{112,48},{1... | collective-permute-start | bytes 1572872 | tf_op jit(solution)/shard_map/ppermute | solution.py:22
  218.3 30.2 %copy-start.13 = (bf16[1024,384]{1,0:T(8,128)(2,1)S(1)}, bf16[1024,384]{1,0:T(8,128)(2,1)}, u32[]{:S(2)}) copy-start(bf16[1024,384]{1,0:T(8,128)(2,1)} %get-tuple-element.87.step_ref) | copy-start | bytes 2359300
  248.5 10.0 %copy-start.18 = (bf16[1024,128]{1,0:T(8,128)(2,1)S(1)}, bf16[1024,128]{1,0:T(8,128)(2,1)}, u32[]{:S(2)}) copy-start(bf16[1024,128]{1,0:T(8,128)(2,1)} %get-tuple-element.84.step_ref) | copy-start | bytes 786436

commit v7 on v6

--- a/solution.py
+++ b/solution.py
@@ -305,6 +305,33 @@
     squares_ref[...] += jnp.sum(lanes.reshape(-1, 8, 128), axis=0)
 
 
+def finish_inside_kernel(x_ref, u_ref, local_ref, *rest):
+    grad_ref, squares_ref = rest[-2:]
+    blocks, _, step = x_ref.shape
+    total = jnp.zeros(squares_ref.shape, F32)
+    for k in range(blocks // 2):
+        here = slice(k * step, (k + 1) * step)
+        grad = local_ref[here] + times(x_ref[blocks // 2 + k], u_ref[...])
+        grad_ref[here] = grad
+        square = grad * grad
+        lanes = sum(square[:, j : j + 128] for j in range(0, grad.shape[1], 128))
+        total = total + jnp.sum(lanes.reshape(-1, 8, 128), axis=0)
+    squares_ref[...] = total
+
+
+def finish_inside(x, u, local, earlier):
+    inside = pl.BlockSpec(memory_space=pltpu.VMEM)
+    return pl.pallas_call(
+        finish_inside_kernel,
+        grid=(1,),
+        out_shape=(jax.ShapeDtypeStruct(local.shape, F32), jax.ShapeDtypeStruct((8, 128), F32)),
+        in_specs=[inside] * 3 + [corner(value) for value in earlier],
+        out_specs=(inside, inside),
+        cost_estimate=SLIGHT,
+        compiler_params=pltpu.CompilerParams(vmem_limit_bytes=32 * 2**20),
+    )(x, u, local, *earlier)
+
+
 def finish(x, u, local, earlier):
     blocks, depth, step = x.shape
     width = u.shape[1]
@@ -352,7 +379,7 @@
     features = assemble(near, turned(near[:2], 1), turned(near[2:], 1))
     grads, squares = [], jnp.zeros((8, 128), F32)
     for i, (piece, other) in enumerate(zip(up, up_other)):
-        grad, square = finish(features, other, local_product(features, piece), (old_other,) if i == 2 else ())
+        grad, square = (finish_inside if i == 2 else finish)(features, other, local_product(features, piece), (old_other,) if i == 2 else ())
         grads.append(grad)
         squares = squares + square
     grad_other = across(jnp.concatenate([grads[0][:, :EARLY].astype(BF16), second[:, EARLY // 2 : EARLY]], axis=1))

time: 261 us -> 261 us (level)
    pallas_call x3 -> x2, Pallas kernels: 10.4 us -> 8.11 us  [finish(): pl.pallas_call(finish_kernel, grid=(blocks // 2,), out_shape=(jax.ShapeDt...]
  transfers between devices with their start and end apart: 22 -> 22, of which waited for: 14 -> 15; matrix products, arithmetic and copies ran while one was open for 7% -> 7% of each run, Pallas kernels for 28% -> 28%
where the time goes in v7:
time: 261 us; the launch traced here: 260 us
  waiting for transfers between devices  116 us (44%)
  Pallas kernels  74.3 us (28%)
  starting transfers between devices  47.1 us (18%)
  local copies, waits for them, and re-layouts  20.6 us (8%)
    ppermute x10, waiting for transfers between devices, across(): return lax.ppermute(value, 'replica', [(s, s ^ 4) for s in range(8)])  73.8 us
    ppermute x4, waiting for transfers between devices, swap_dp(): return lax.ppermute(value, 'dp', [(0, 1), (1, 0)])  29 us
    ppermute x10, starting transfers between devices, across(): return lax.ppermute(value, 'replica', [(s, s ^ 4) for s in range(8)])  24.2 us
    pallas_call x6, Pallas kernels, make(): pl.pallas_call(make_kernel, grid=(rows // STEP_ROWS,), out_shape=(jax.Sha...  22.5 us
    pallas_call x7, Pallas kernels, mix(): pl.pallas_call(functools.partial(mix_kernel, ready), grid=(rows // depth,...  19.4 us
    slice x6, local copies, waits for them, and re-layouts, part(): return value[:, piece[0]:piece[0] + piece[1]]  10.6 us
    pallas_call x3, Pallas kernels, local_product(): pl.pallas_call(local_kernel, grid=(blocks // 2,), out_shape=jax.ShapeDtyp...  10.2 us
    ppermute x4, starting transfers between devices, swap_dp(): return lax.ppermute(value, 'dp', [(0, 1), (1, 0)])  8.16 us
  transfers between devices with their start and end apart: 22, of which 15 were waited for; matrix products, arithmetic and copies ran while one was open for 7% of the time, Pallas kernels for 28%

profile of v7, /device:TPU:6, one launch (start us, length us, event | category | flops | bytes accessed | tf_op | source)
XLA Modules:
  0.0 259.9 jit_solution(131015992075778496)
XLA Ops:
  0.6 5.8 %collective-permute-start = (bf16[1024,256]{1,0:T(8,128)(2,1)}, bf16[1024,256]{1,0:T(8,128)(2,1)S(1)}, u32[]{:S(2)}, u32[]{:S(2)}) collective-permute-start(bf16[1024,256]{1,0:T(8,128)(2,1)} %bitcast.48), channel_id=1, source_target_pairs={{0,0},{1,1},{2,2},{3,3},{4,10},{5,11},{6,8},{7,9},{8,6},{9,7},{10,... | collective-permute-start | bytes 1572872 | tf_op jit(solution)/shard_map/ppermute | solution.py:62
  6.4 4.0 %collective-permute-start.6 = (bf16[1024,1792]{1,0:T(8,128)(2,1)}, bf16[1024,1792]{1,0:T(8,128)(2,1)}, u32[]{:S(2)}, u32[]{:S(2)}) collective-permute-start(bf16[1024,1792]{1,0:T(8,128)(2,1)} %bitcast.33), channel_id=1, source_target_pairs={{0,64},{16,80},{32,96},{48,112},{64,0},{80,16},{96,32},{112,48},{1... | collective-permute-start | bytes 11010056 | tf_op jit(solution)/shard_map/ppermute | solution.py:22
  10.4 2.7 %slice.67.u_ref = bf16[1024,768]{1,0:T(8,128)(2,1)} slice(bf16[1024,1792]{1,0:T(8,128)(2,1)} %bitcast.45), slice={[0:1024], [0:768]} | slice | bytes 3145728 | tf_op jit(solution)/shard_map/slice | solution.py:357
  13.0 8.1 %collective-permute-done = bf16[1024,256]{1,0:T(8,128)(2,1)S(1)} collective-permute-done((bf16[1024,256]{1,0:T(8,128)(2,1)}, bf16[1024,256]{1,0:T(8,128)(2,1)S(1)}, u32[]{:S(2)}, u32[]{:S(2)}) %collective-permute-start) | collective-permute-done | bytes 524320 | tf_op jit(solution)/shard_map/ppermute | solution.py:62
  22.6 3.6 %all-to-all-start = ((bf16[4,1024,256]{2,1,0:T(8,128)(2,1)}), bf16[4,1024,256]{2,1,0:T(8,128)(2,1)S(1)}, u32[]{:S(2)}, u32[]{:S(2)}) async-start(bf16[4,1024,256]{2,1,0:T(8,128)(2,1)} %broadcast_in_dim.12), calls=%async_computation | async-start | bytes 4194304 | tf_op jit(solution)/shard_map/all_to_all | solution.py:67
  27.3 2.1 fusion.2
  29.4 2.7 %slice.54.u_ref = bf16[1024,768]{1,0:T(8,128)(2,1)} slice(bf16[1024,1792]{1,0:T(8,128)(2,1)} %bitcast.46), slice={[0:1024], [768:1536]} | slice | bytes 3145728 | tf_op jit(solution)/shard_map/slice | solution.py:357
  32.0 2.1 collective-permute-start.4
  34.1 18.6 %collective-permute-done.1.refs_3_.u_ref = bf16[1024,768]{1,0:T(8,128)(2,1)} collective-permute-done((bf16[1024,768]{1,0:T(8,128)(2,1)}, bf16[1024,768]{1,0:T(8,128)(2,1)}, u32[]{:S(2)}, u32[]{:S(2)}) %collective-permute-start.1) | collective-permute-done | bytes 1572896 | tf_op jit(solution)/shard_map/ppermute | solution.py:26
  57.8 4.1 %collective-permute-start.5 = (bf16[1024,256]{1,0:T(8,128)(2,1)S(1)}, bf16[1024,256]{1,0:T(8,128)(2,1)S(1)}, u32[]{:S(2)}, u32[]{:S(2)}) collective-permute-start(bf16[1024,256]{1,0:T(8,128)(2,1)S(1)} %slice.55.u_ref), channel_id=1, source_target_pairs={{0,8},{8,0},{1,9},{9,1},{2,10},{10,2},{3,11},{11,3},{4,12},{12,4},... | collective-permute-start | bytes 1572872 | tf_op jit(solution)/shard_map/ppermute | solution.py:26
  63.0 4.0 %collective-permute-start.12 = (bf16[1024,384]{1,0:T(8,128)(2,1)S(1)}, bf16[1024,384]{1,0:T(8,128)(2,1)S(1)}, u32[]{:S(2)}, u32[]{:S(2)}) collective-permute-start(bf16[1024,384]{1,0:T(8,128)(2,1)S(1)} %pad_maximum_fusion), channel_id=1, source_target_pairs={{0,64},{16,80},{32,96},{48,112},{64,0},{80,16},{96,32},{112,48},{1... | collective-permute-start | bytes 2359304 | tf_op jit(solution)/shard_map/ppermute | solution.py:22
  66.9 1.8 shard_map.77.x_ref
  68.8 3.9 %shard_map.78.local_ref = f32[1024,768]{1,0:T(8,128)S(1)} custom-call(bf16[8,1024,256]{2,1,0:T(8,128)(2,1)S(1)} %shard_map.77.x_ref, bf16[1024,768]{1,0:T(8,128)(2,1)} %slice.67.u_ref), custom_call_target="tpu_custom_call" | custom-call | bytes 4096 | tf_op jit(solution)/shard_map/pallas_call | solution.py:283
  72.7 4.1 %shard_map.79 = (f32[1024,768]{1,0:T(8,128)S(1)}, f32[8,128]{1,0:T(8,128)S(1)}) custom-call(bf16[8,1024,256]{2,1,0:T(8,128)(2,1)S(1)} %shard_map.77.x_ref, bf16[1024,768]{1,0:T(8,128)(2,1)} %collective-permute-done.1.refs_3_.u_ref, f32[1024,768]{1,0:T(8,128)S(1)} %shard_map.78.local_ref), custom_call_target="tpu_custom_call" | custom-call | bytes 4096 | tf_op jit(solution)/shard_map/pallas_call | solution.py:339
  77.0 4.8 %shard_map.80.local_ref = f32[1024,768]{1,0:T(8,128)S(1)} custom-call(bf16[8,1024,256]{2,1,0:T(8,128)(2,1)S(1)} %shard_map.77.x_ref, bf16[1024,768]{1,0:T(8,128)(2,1)} %slice.54.u_ref), custom_call_target="tpu_custom_call" | custom-call | bytes 4096 | tf_op jit(solution)/shard_map/pallas_call | solution.py:283
  83.3 3.1 %collective-permute-done.4.u_ref = bf16[1024,768]{1,0:T(8,128)(2,1)} collective-permute-done((bf16[1024,768]{1,0:T(8,128)(2,1)}, bf16[1024,768]{1,0:T(8,128)(2,1)}, u32[]{:S(2)}, u32[]{:S(2)}) %collective-permute-start.4) | collective-permute-done | bytes 1572896 | tf_op jit(solution)/shard_map/ppermute | solution.py:26
  86.4 4.1 %shard_map.81 = (f32[1024,768]{1,0:T(8,128)S(1)}, f32[8,128]{1,0:T(8,128)S(1)}) custom-call(bf16[8,1024,256]{2,1,0:T(8,128)(2,1)S(1)} %shard_map.77.x_ref, bf16[1024,768]{1,0:T(8,128)(2,1)} %collective-permute-done.4.u_ref, f32[1024,768]{1,0:T(8,128)S(1)} %shard_map.80.local_ref), custom_call_target="tpu_custom_call" | custom-call | bytes 4096 | tf_op jit(solution)/shard_map/pallas_call | solution.py:339
  90.5 1.7 copy-done.1
  92.2 4.2 %collective-permute-done.5.u_ref = bf16[1024,256]{1,0:T(8,128)(2,1)S(1)} collective-permute-done((bf16[1024,256]{1,0:T(8,128)(2,1)S(1)}, bf16[1024,256]{1,0:T(8,128)(2,1)S(1)}, u32[]{:S(2)}, u32[]{:S(2)}) %collective-permute-start.5) | collective-permute-done | bytes 524320 | tf_op jit(solution)/shard_map/ppermute | solution.py:26
  99.1 2.8 %collective-permute-start.10 = (f32[8,128]{1,0:T(8,128)S(1)}, f32[8,128]{1,0:T(8,128)S(1)}, u32[]{:S(2)}, u32[]{:S(2)}) collective-permute-start(f32[8,128]{1,0:T(8,128)S(1)} %add.34), channel_id=1, source_target_pairs={{0,6},{1,7},{2,4},{3,5},{4,2},{5,3},{6,0},{7,1},{8,14},{9,15},{10,... | collective-permute-start | bytes 12296 | tf_op jit(solution)/shard_map/ppermute | solution.py:53
  104.0 1.6 collective-permute-done.8
  105.6 1.9 collective-permute-done.9
  107.4 2.0 collective-permute-start.11
  109.5 3.1 %collective-permute-done.11.two_ref = f32[8,128]{1,0:T(8,128)S(1)} collective-permute-done((f32[8,128]{1,0:T(8,128)S(1)}, f32[8,128]{1,0:T(8,128)S(1)}, u32[]{:S(2)}, u32[]{:S(2)}) %collective-permute-start.11) | collective-permute-done | bytes 4128 | tf_op jit(solution)/shard_map/ppermute | solution.py:26
  112.6 1.8 shard_map.93.pair_ref
  114.4 3.9 %collective-permute-start.18 = (bf16[2,1040,256]{2,1,0:T(8,128)(2,1)}, bf16[2,1040,256]{2,1,0:T(8,128)(2,1)S(1)}, u32[]{:S(2)}, u32[]{:S(2)}) collective-permute-start(bf16[2,1040,256]{2,1,0:T(8,128)(2,1)} %shard_map.93.pair_ref), channel_id=1, source_target_pairs={{0,64},{16,80},{32,96},{48,112},{64,0},{80,16},{96,32},{112,48},{1... | collective-permute-start | bytes 3194888 | tf_op jit(solution)/shard_map/ppermute | solution.py:22
  118.2 2.8 %shard_map.87 = (bf16[2,1024,128]{2,1,0:T(8,128)(2,1)}, bf16[1024,128]{1,0:T(8,128)(2,1)}) custom-call(f32[8,128]{1,0:T(8,128)} %copy-done.16, f32[1024,768]{1,0:T(8,128)} %copy-done, bf16[1024,1792]{1,0:T(8,128)(2,1)} %bitcast.17, bf16[1024,1792]{1,0:T(8,128)(2,1)} %bitcast.26, bf16[1024,1792]{1,0:T(8,128)(2,1)} %bitcast.34), custom_call_target="tpu_custom_call" | custom-call | flops 3932160 | bytes 2097152 | tf_op jit(solution)/shard_map/pallas_call | solution.py:222
  121.1 2.9 %shard_map.88 = (bf16[2,1024,128]{2,1,0:T(8,128)(2,1)}, bf16[1024,128]{1,0:T(8,128)(2,1)}) custom-call(f32[8,128]{1,0:T(8,128)} %copy-done.16, f32[1024,768]{1,0:T(8,128)} %copy-done, bf16[1024,1792]{1,0:T(8,128)(2,1)} %bitcast.18, bf16[1024,1792]{1,0:T(8,128)(2,1)} %bitcast.27, bf16[1024,1792]{1,0:T(8,128)(2,1)} %bitcast.35), custom_call_target="tpu_custom_call" | custom-call | flops 3932160 | bytes 2097152 | tf_op jit(solution)/shard_map/pallas_call | solution.py:222
  125.3 3.6 %collective-permute-start.15 = (bf16[2,1024,128]{2,1,0:T(8,128)(2,1)}, bf16[2,1024,128]{2,1,0:T(8,128)(2,1)S(1)}, u32[]{:S(2)}, u32[]{:S(2)}) collective-permute-start(bf16[2,1024,128]{2,1,0:T(8,128)(2,1)} %shard_map.89.pair_ref), channel_id=1, source_target_pairs={{0,64},{16,80},{32,96},{48,112},{64,0},{80,16},{96,32},{112,48},{1... | collective-permute-start | bytes 1572872 | tf_op jit(solution)/shard_map/ppermute | solution.py:22
  128.8 2.1 fusion
  130.9 2.9 %shard_map.92 = (bf16[2,1024,128]{2,1,0:T(8,128)(2,1)}, bf16[1024,128]{1,0:T(8,128)(2,1)}) custom-call(f32[8,128]{1,0:T(8,128)} %copy-done.16, f32[1024,256]{1,0:T(8,128)} %copy-done.8, bf16[1024,1792]{1,0:T(8,128)(2,1)} %bitcast.19, bf16[1024,1792]{1,0:T(8,128)(2,1)} %bitcast.28, bf16[1024,1792]{1,0:T(8,128)(2,1)} %bitcast.36), custom_call_target="tpu_custom_call" | custom-call | flops 3932160 | bytes 2097152 | tf_op jit(solution)/shard_map/pallas_call | solution.py:222
  133.8 5.7 %shard_map.86 = (bf16[2,1024,384]{2,1,0:T(8,128)(2,1)}, bf16[1024,384]{1,0:T(8,128)(2,1)}) custom-call(f32[8,128]{1,0:T(8,128)} %copy-done.16, f32[1024,768]{1,0:T(8,128)} %copy-done.1, bf16[1024,1792]{1,0:T(8,128)(2,1)} %bitcast.20, bf16[1024,1792]{1,0:T(8,128)(2,1)} %bitcast.29, bf16[1024,1792]{1,0:T(8,128)(2,1)} %bitcast.37), custom_call_target="tpu_custom_call" | custom-call | flops 11796480 | bytes 6291456 | tf_op jit(solution)/shard_map/pallas_call | solution.py:222
  139.5 19.0 %collective-permute-done.13.pair_other_ref.refs_1_ = bf16[2,1024,128]{2,1,0:T(8,128)(2,1)S(1)} collective-permute-done((bf16[2,1024,128]{2,1,0:T(8,128)(2,1)}, bf16[2,1024,128]{2,1,0:T(8,128)(2,1)S(1)}, u32[]{:S(2)}, u32[]{:S(2)}) %collective-permute-start.13) | collective-permute-done | bytes 524320 | tf_op jit(solution)/shard_map/ppermute | solution.py:22
  159.9 9.9 %collective-permute-done.15.refs_2_.pair_other_ref = bf16[2,1024,128]{2,1,0:T(8,128)(2,1)S(1)} collective-permute-done((bf16[2,1024,128]{2,1,0:T(8,128)(2,1)}, bf16[2,1024,128]{2,1,0:T(8,128)(2,1)S(1)}, u32[]{:S(2)}, u32[]{:S(2)}) %collective-permute-start.15) | collective-permute-done | bytes 524320 | tf_op jit(solution)/shard_map/ppermute | solution.py:22
  169.8 3.6 %collective-permute-start.16 = (bf16[2,1024,384]{2,1,0:T(8,128)(2,1)}, bf16[2,1024,384]{2,1,0:T(8,128)(2,1)S(1)}, u32[]{:S(2)}, u32[]{:S(2)}) collective-permute-start(bf16[2,1024,384]{2,1,0:T(8,128)(2,1)} %shard_map.91.pair_ref), channel_id=1, source_target_pairs={{0,64},{16,80},{32,96},{48,112},{64,0},{80,16},{96,32},{112,48},{1... | collective-permute-start | bytes 4718600 | tf_op jit(solution)/shard_map/ppermute | solution.py:22
  173.3 5.4 %shard_map.99 = (bf16[2,1024,384]{2,1,0:T(8,128)(2,1)}, bf16[1024,384]{1,0:T(8,128)(2,1)}) custom-call(f32[8,128]{1,0:T(8,128)} %copy-done.16, f32[1024,768]{1,0:T(8,128)} %copy-done.1, bf16[1024,1792]{1,0:T(8,128)(2,1)} %bitcast.21, bf16[1024,1792]{1,0:T(8,128)(2,1)} %bitcast.30, bf16[1024,1792]{1,0:T(8,128)(2,1)} %bitcast.38), custom_call_target="tpu_custom_call" | custom-call | flops 11796480 | bytes 6291456 | tf_op jit(solution)/shard_map/pallas_call | solution.py:222
  180.6 2.4 shard_map.94
  184.4 1.6 collective-permute-start.20
  187.2 2.9 %shard_map.85 = (bf16[2,1024,128]{2,1,0:T(8,128)(2,1)}, bf16[1024,128]{1,0:T(8,128)(2,1)}) custom-call(f32[8,128]{1,0:T(8,128)} %copy-done.16, f32[1024,256]{1,0:T(8,128)} %copy-done.8, bf16[1024,1792]{1,0:T(8,128)(2,1)} %bitcast.22, bf16[1024,1792]{1,0:T(8,128)(2,1)} %bitcast.31, bf16[1024,1792]{1,0:T(8,128)(2,1)} %bitcast.40), custom_call_target="tpu_custom_call" | custom-call | flops 3932160 | bytes 2097152 | tf_op jit(solution)/shard_map/pallas_call | solution.py:222
  190.1 3.7 %shard_map.95 = (bf16[1024,1792]{1,0:T(8,128)(2,1)}, bf16[1024,1792]{1,0:T(8,128)(2,1)}, bf16[1024,1792]{1,0:T(8,128)(2,1)}, f32[8,128]{1,0:T(8,128)}) custom-call(bf16[2,1040,256]{2,1,0:T(8,128)(2,1)} %shard_map.93.pair_ref, bf16[1024,256]{1,0:T(8,128)(2,1)S(1)} %slice.74.step_ref, ...), custom_call_target="tpu_custom_call", output_to_operand_aliasing={{0}: (4, {}), {1}: (5, {}), {2}: (6, {})} | custom-call | flops 7864320 | bytes 4718592 | tf_op jit(solution)/shard_map/pallas_call | solution.py:239
  193.7 6.3 %shard_map.96 = (bf16[1024,1792]{1,0:T(8,128)(2,1)}, bf16[1024,1792]{1,0:T(8,128)(2,1)}, bf16[1024,1792]{1,0:T(8,128)(2,1)}) custom-call(f32[8,128]{1,0:T(8,128)} %copy-done.16, bf16[2,1040,256]{2,1,0:T(8,128)(2,1)} %copy-done.2, f32[1024,768]{1,0:T(8,128)} %copy-done, ...), custom_call_target="tpu_custom_call", output_to_operand_aliasing={{0}: (11, {}), {1}: (12, {}), {2}: (13, {})} | custom-call | flops 15728640 | bytes 5767168 | tf_op jit(solution)/shard_map/pallas_call | solution.py:261
  200.1 2.5 shard_map.97
  202.6 12.1 %collective-permute-done.16.refs_1_.pair_other_ref = bf16[2,1024,384]{2,1,0:T(8,128)(2,1)S(1)} collective-permute-done((bf16[2,1024,384]{2,1,0:T(8,128)(2,1)}, bf16[2,1024,384]{2,1,0:T(8,128)(2,1)S(1)}, u32[]{:S(2)}, u32[]{:S(2)}) %collective-permute-start.16) | collective-permute-done | bytes 1572896 | tf_op jit(solution)/shard_map/ppermute | solution.py:22
  214.7 3.6 %collective-permute-start.19 = (bf16[2,1024,128]{2,1,0:T(8,128)(2,1)S(1)}, bf16[2,1024,128]{2,1,0:T(8,128)(2,1)S(1)}, u32[]{:S(2)}, u32[]{:S(2)}) collective-permute-start(bf16[2,1024,128]{2,1,0:T(8,128)(2,1)S(1)} %shard_map.98.pair_ref), channel_id=1, source_target_pairs={{0,64},{16,80},{32,96},{48,112},{64,0},{80,16},{96,32},{112,48},{1... | collective-permute-start | bytes 1572872 | tf_op jit(solution)/shard_map/ppermute | solution.py:22
  218.3 3.8 %shard_map.101 = (bf16[1024,1792]{1,0:T(8,128)(2,1)}, bf16[1024,1792]{1,0:T(8,128)(2,1)}, bf16[1024,1792]{1,0:T(8,128)(2,1)}, f32[8,128]{1,0:T(8,128)}) custom-call(bf16[2,1024,384]{2,1,0:T(8,128)(2,1)} %shard_map.91.pair_ref, bf16[1024,384]{1,0:T(8,128)(2,1)S(1)} %copy-done.12, ...), custom_call_target="tpu_custom_call", output_to_operand_aliasing={{0}: (4, {}), {1}: (5, {}), {2}: (6, {})} | custom-call | flops 11796480 | bytes 7077888 | tf_op jit(solution)/shard_map/pallas_call | solution.py:239
  222.1 26.4 %collective-permute-done.20.pair_other_ref = bf16[2,1024,384]{2,1,0:T(8,128)(2,1)} collective-permute-done((bf16[2,1024,384]{2,1,0:T(8,128)(2,1)}, bf16[2,1024,384]{2,1,0:T(8,128)(2,1)}, u32[]{:S(2)}, u32[]{:S(2)}) %collective-permute-start.20) | collective-permute-done | bytes 1572896 | tf_op jit(solution)/shard_map/ppermute | solution.py:22
  248.5 4.3 %shard_map.102 = (bf16[1024,1792]{1,0:T(8,128)(2,1)}, bf16[1024,1792]{1,0:T(8,128)(2,1)}, bf16[1024,1792]{1,0:T(8,128)(2,1)}, f32[8,128]{1,0:T(8,128)}) custom-call(bf16[2,1024,384]{2,1,0:T(8,128)(2,1)} %shard_map.100.pair_ref, bf16[1024,384]{1,0:T(8,128)(2,1)S(1)} %copy-done.13, ...), custom_call_target="tpu_custom_call", output_to_operand_aliasing={{0}: (4, {}), {1}: (5, {}), {2}: (6, {})} | custom-call | flops 11796480 | bytes 7077888 | tf_op jit(solution)/shard_map/pallas_call | solution.py:239
  252.9 5.6 %collective-permute-done.19.pair_other_ref = bf16[2,1024,128]{2,1,0:T(8,128)(2,1)S(1)} collective-permute-done((bf16[2,1024,128]{2,1,0:T(8,128)(2,1)S(1)}, bf16[2,1024,128]{2,1,0:T(8,128)(2,1)S(1)}, u32[]{:S(2)}, u32[]{:S(2)}) %collective-permute-start.19) | collective-permute-done | bytes 524320 | tf_op jit(solution)/shard_map/ppermute | solution.py:22
  (84 shorter events, 23.5 us)
Async XLA Ops:
  0.6 20.5 %collective-permute-start = (bf16[1024,256]{1,0:T(8,128)(2,1)}, bf16[1024,256]{1,0:T(8,128)(2,1)S(1)}, u32[]{:S(2)}, u32[]{:S(2)}) collective-permute-start(bf16[1024,256]{1,0:T(8,128)(2,1)} %bitcast.48), channel_id=1, source_target_pairs={{0,0},{1,1},{2,2},{3,3},{4,10},{5,11},{6,8},{7,9},{8,6},{9,7},{10,... | collective-permute-start | bytes 1572872 | tf_op jit(solution)/shard_map/ppermute | solution.py:62
  6.4 90.0 %collective-permute-start.6 = (bf16[1024,1792]{1,0:T(8,128)(2,1)}, bf16[1024,1792]{1,0:T(8,128)(2,1)}, u32[]{:S(2)}, u32[]{:S(2)}) collective-permute-start(bf16[1024,1792]{1,0:T(8,128)(2,1)} %bitcast.33), channel_id=1, source_target_pairs={{0,64},{16,80},{32,96},{48,112},{64,0},{80,16},{96,32},{112,48},{1... | collective-permute-start | bytes 11010056 | tf_op jit(solution)/shard_map/ppermute | solution.py:22
  13.0 39.7 %collective-permute-start.1 = (bf16[1024,768]{1,0:T(8,128)(2,1)}, bf16[1024,768]{1,0:T(8,128)(2,1)}, u32[]{:S(2)}, u32[]{:S(2)}) collective-permute-start(bf16[1024,768]{1,0:T(8,128)(2,1)} %slice.67.u_ref), channel_id=1, source_target_pairs={{0,8},{8,0},{1,9},{9,1},{2,10},{10,2},{3,11},{11,3},{4,12},{12,4},... | collective-permute-start | bytes 4718600 | tf_op jit(solution)/shard_map/ppermute | solution.py:26
  22.6 30.1 %all-to-all-start = ((bf16[4,1024,256]{2,1,0:T(8,128)(2,1)}), bf16[4,1024,256]{2,1,0:T(8,128)(2,1)S(1)}, u32[]{:S(2)}, u32[]{:S(2)}) async-start(bf16[4,1024,256]{2,1,0:T(8,128)(2,1)} %broadcast_in_dim.12), calls=%async_computation | async-start | bytes 4194304 | tf_op jit(solution)/shard_map/all_to_all | solution.py:67
  32.0 54.4 %collective-permute-start.4 = (bf16[1024,768]{1,0:T(8,128)(2,1)}, bf16[1024,768]{1,0:T(8,128)(2,1)}, u32[]{:S(2)}, u32[]{:S(2)}) collective-permute-start(bf16[1024,768]{1,0:T(8,128)(2,1)} %slice.54.u_ref), channel_id=1, source_target_pairs={{0,8},{8,0},{1,9},{9,1},{2,10},{10,2},{3,11},{11,3},{4,12},{12,4},... | collective-permute-start | bytes 4718600 | tf_op jit(solution)/shard_map/ppermute | solution.py:26
  53.4 9.5 %copy-start.4 = (bf16[1024,256]{1,0:T(8,128)(2,1)}, bf16[1024,256]{1,0:T(8,128)(2,1)S(1)}, u32[]{:S(2)}) copy-start(bf16[1024,256]{1,0:T(8,128)(2,1)S(1)} %get-tuple-element.69.second_ref) | copy-start | bytes 1572868
  53.4 9.6 %copy-start.6 = (bf16[1024,256]{1,0:T(8,128)(2,1)}, bf16[1024,256]{1,0:T(8,128)(2,1)S(1)}, u32[]{:S(2)}) copy-start(bf16[1024,256]{1,0:T(8,128)(2,1)S(1)} %get-tuple-element.68.first_ref) | copy-start | bytes 1572868
  55.0 8.0 %collective-permute-start.2 = (bf16[2,1024,256]{2,1,0:T(8,128)(2,1)}, bf16[2,1024,256]{2,1,0:T(8,128)(2,1)}, u32[]{:S(2)}, u32[]{:S(2)}) collective-permute-start(bf16[2,1024,256]{2,1,0:T(8,128)(2,1)} %get-tuple-element.110), channel_id=1, source_target_pairs={{0,1},{1,0},{2,3},{3,2},{4,5},{5,4},{6,7},{7,6},{8,9},{9,8},{10,11... | collective-permute-start | bytes 3145736 | tf_op jit(solution)/shard_map/ppermute | solution.py:53
  55.0 11.9 %collective-permute-start.3 = (bf16[2,1024,256]{2,1,0:T(8,128)(2,1)}, bf16[2,1024,256]{2,1,0:T(8,128)(2,1)}, u32[]{:S(2)}, u32[]{:S(2)}) collective-permute-start(bf16[2,1024,256]{2,1,0:T(8,128)(2,1)} %get-tuple-element.109), channel_id=1, source_target_pairs={{0,1},{1,0},{2,3},{3,2},{4,5},{5,4},{6,7},{7,6},{8,9},{9,8},{10,11... | collective-permute-start | bytes 3145736 | tf_op jit(solution)/shard_map/ppermute | solution.py:53
  57.8 38.7 %collective-permute-start.5 = (bf16[1024,256]{1,0:T(8,128)(2,1)S(1)}, bf16[1024,256]{1,0:T(8,128)(2,1)S(1)}, u32[]{:S(2)}, u32[]{:S(2)}) collective-permute-start(bf16[1024,256]{1,0:T(8,128)(2,1)S(1)} %slice.55.u_ref), channel_id=1, source_target_pairs={{0,8},{8,0},{1,9},{9,1},{2,10},{10,2},{3,11},{11,3},{4,12},{12,4},... | collective-permute-start | bytes 1572872 | tf_op jit(solution)/shard_map/ppermute | solution.py:26
  63.0 46.5 %collective-permute-start.12 = (bf16[1024,384]{1,0:T(8,128)(2,1)S(1)}, bf16[1024,384]{1,0:T(8,128)(2,1)S(1)}, u32[]{:S(2)}, u32[]{:S(2)}) collective-permute-start(bf16[1024,384]{1,0:T(8,128)(2,1)S(1)} %pad_maximum_fusion), channel_id=1, source_target_pairs={{0,64},{16,80},{32,96},{48,112},{64,0},{80,16},{96,32},{112,48},{1... | collective-permute-start | bytes 2359304 | tf_op jit(solution)/shard_map/ppermute | solution.py:22
  76.8 35.8 %copy-start = (f32[1024,768]{1,0:T(8,128)}, f32[1024,768]{1,0:T(8,128)S(1)}, u32[]{:S(2)}) copy-start(f32[1024,768]{1,0:T(8,128)S(1)} %get-tuple-element.61.grad_ref) | copy-start | bytes 9437188
  76.9 47.6 %collective-permute-start.14 = (bf16[1024,384]{1,0:T(8,128)(2,1)S(1)}, bf16[1024,384]{1,0:T(8,128)(2,1)}, u32[]{:S(2)}, u32[]{:S(2)}) collective-permute-start(bf16[1024,384]{1,0:T(8,128)(2,1)S(1)} %pad_maximum_fusion.1), channel_id=1, source_target_pairs={{0,64},{16,80},{32,96},{48,112},{64,0},{80,16},{96,32},{112,48},{1... | collective-permute-start | bytes 2359304 | tf_op jit(solution)/shard_map/ppermute | solution.py:22
  90.5 1.7 copy-start.1
  92.2 20.3 %copy-start.5 = (bf16[1024,256]{1,0:T(8,128)(2,1)S(1)}, bf16[1024,256]{1,0:T(8,128)(2,1)}, u32[]{:S(2)}) copy-start(bf16[1024,256]{1,0:T(8,128)(2,1)} %copy-done.4) | copy-start | bytes 1572868
  92.2 20.3 %copy-start.7 = (bf16[1024,256]{1,0:T(8,128)(2,1)S(1)}, bf16[1024,256]{1,0:T(8,128)(2,1)}, u32[]{:S(2)}) copy-start(bf16[1024,256]{1,0:T(8,128)(2,1)} %copy-done.6) | copy-start | bytes 1572868
  97.9 16.5 %copy-start.8 = (f32[1024,256]{1,0:T(8,128)}, f32[1024,256]{1,0:T(8,128)S(1)}, u32[]{:S(2)}) copy-start(f32[1024,256]{1,0:T(8,128)S(1)} %get-tuple-element.57.grad_ref) | copy-start | bytes 3145732
  97.9 1.2 collective-permute-start.7
  99.1 4.8 %collective-permute-start.10 = (f32[8,128]{1,0:T(8,128)S(1)}, f32[8,128]{1,0:T(8,128)S(1)}, u32[]{:S(2)}, u32[]{:S(2)}) collective-permute-start(f32[8,128]{1,0:T(8,128)S(1)} %add.34), channel_id=1, source_target_pairs={{0,6},{1,7},{2,4},{3,5},{4,2},{5,3},{6,0},{7,1},{8,14},{9,15},{10,... | collective-permute-start | bytes 12296 | tf_op jit(solution)/shard_map/ppermute | solution.py:53
  101.9 3.6 %collective-permute-start.8 = (f32[8,128]{1,0:T(8,128)S(1)}, f32[8,128]{1,0:T(8,128)S(1)}, u32[]{:S(2)}, u32[]{:S(2)}) collective-permute-start(f32[8,128]{1,0:T(8,128)S(1)} %add.34), channel_id=1, source_target_pairs={{0,2},{1,3},{2,0},{3,1},{4,6},{5,7},{6,4},{7,5},{8,10},{9,11},{10,... | collective-permute-start | bytes 12296 | tf_op jit(solution)/shard_map/ppermute | solution.py:53
  102.3 5.1 %collective-permute-start.9 = (f32[8,128]{1,0:T(8,128)S(1)}, f32[8,128]{1,0:T(8,128)S(1)}, u32[]{:S(2)}, u32[]{:S(2)}) collective-permute-start(f32[8,128]{1,0:T(8,128)S(1)} %add.34), channel_id=1, source_target_pairs={{0,4},{1,5},{2,6},{3,7},{4,0},{5,1},{6,2},{7,3},{8,12},{9,13},{10,... | collective-permute-start | bytes 12296 | tf_op jit(solution)/shard_map/ppermute | solution.py:53
  107.4 5.1 %collective-permute-start.11 = (f32[8,128]{1,0:T(8,128)S(1)}, f32[8,128]{1,0:T(8,128)S(1)}, u32[]{:S(2)}, u32[]{:S(2)}) collective-permute-start(f32[8,128]{1,0:T(8,128)S(1)} %add_add_fusion.one_ref), channel_id=1, source_target_pairs={{0,8},{8,0},{1,9},{9,1},{2,10},{10,2},{3,11},{11,3},{4,12},{12,4},... | collective-permute-start | bytes 12296 | tf_op jit(solution)/shard_map/ppermute | solution.py:26
  109.5 4.9 %copy-start.3 = (bf16[1024,384]{1,0:T(8,128)(2,1)}, bf16[1024,384]{1,0:T(8,128)(2,1)S(1)}, u32[]{:S(2)}) copy-start(bf16[1024,384]{1,0:T(8,128)(2,1)S(1)} %collective-permute-done.12.rest_0_.first_other_ref.second_other_ref) | copy-start | bytes 2359300
  112.5 5.7 %copy-start.16 = (f32[8,128]{1,0:T(8,128)}, f32[8,128]{1,0:T(8,128)S(1)}, u32[]{:S(2)}) copy-start(f32[8,128]{1,0:T(8,128)S(1)} %shard_map.84.total_ref) | copy-start | bytes 12292
  114.4 68.7 %collective-permute-start.18 = (bf16[2,1040,256]{2,1,0:T(8,128)(2,1)}, bf16[2,1040,256]{2,1,0:T(8,128)(2,1)S(1)}, u32[]{:S(2)}, u32[]{:S(2)}) collective-permute-start(bf16[2,1040,256]{2,1,0:T(8,128)(2,1)} %shard_map.93.pair_ref), channel_id=1, source_target_pairs={{0,64},{16,80},{32,96},{48,112},{64,0},{80,16},{96,32},{112,48},{1... | collective-permute-start | bytes 3194888 | tf_op jit(solution)/shard_map/ppermute | solution.py:22
  121.1 37.4 %collective-permute-start.13 = (bf16[2,1024,128]{2,1,0:T(8,128)(2,1)}, bf16[2,1024,128]{2,1,0:T(8,128)(2,1)S(1)}, u32[]{:S(2)}, u32[]{:S(2)}) collective-permute-start(bf16[2,1024,128]{2,1,0:T(8,128)(2,1)} %get-tuple-element.62.pair_ref), channel_id=1, source_target_pairs={{0,64},{16,80},{32,96},{48,112},{64,0},{80,16},{96,32},{112,48},{1... | collective-permute-start | bytes 1572872 | tf_op jit(solution)/shard_map/ppermute | solution.py:22
  125.3 44.5 %collective-permute-start.15 = (bf16[2,1024,128]{2,1,0:T(8,128)(2,1)}, bf16[2,1024,128]{2,1,0:T(8,128)(2,1)S(1)}, u32[]{:S(2)}, u32[]{:S(2)}) collective-permute-start(bf16[2,1024,128]{2,1,0:T(8,128)(2,1)} %shard_map.89.pair_ref), channel_id=1, source_target_pairs={{0,64},{16,80},{32,96},{48,112},{64,0},{80,16},{96,32},{112,48},{1... | collective-permute-start | bytes 1572872 | tf_op jit(solution)/shard_map/ppermute | solution.py:22
  133.8 49.2 %collective-permute-start.17 = (bf16[2,1024,128]{2,1,0:T(8,128)(2,1)}, bf16[2,1024,128]{2,1,0:T(8,128)(2,1)}, u32[]{:S(2)}, u32[]{:S(2)}) collective-permute-start(bf16[2,1024,128]{2,1,0:T(8,128)(2,1)} %get-tuple-element.66.pair_ref), channel_id=1, source_target_pairs={{0,64},{16,80},{32,96},{48,112},{64,0},{80,16},{96,32},{112,48},{1... | collective-permute-start | bytes 1572872 | tf_op jit(solution)/shard_map/ppermute | solution.py:22
  133.8 24.7 %copy-start.15 = (bf16[2,1024,128]{2,1,0:T(8,128)(2,1)S(1)}, bf16[2,1024,128]{2,1,0:T(8,128)(2,1)}, u32[]{:S(2)}) copy-start(bf16[2,1024,128]{2,1,0:T(8,128)(2,1)} %get-tuple-element.62.pair_ref) | copy-start | bytes 1572868
  133.8 24.7 %copy-start.20 = (bf16[1024,128]{1,0:T(8,128)(2,1)S(1)}, bf16[1024,128]{1,0:T(8,128)(2,1)}, u32[]{:S(2)}) copy-start(bf16[1024,128]{1,0:T(8,128)(2,1)} %get-tuple-element.64.step_ref) | copy-start | bytes 786436
  169.8 44.9 %collective-permute-start.16 = (bf16[2,1024,384]{2,1,0:T(8,128)(2,1)}, bf16[2,1024,384]{2,1,0:T(8,128)(2,1)S(1)}, u32[]{:S(2)}, u32[]{:S(2)}) collective-permute-start(bf16[2,1024,384]{2,1,0:T(8,128)(2,1)} %shard_map.91.pair_ref), channel_id=1, source_target_pairs={{0,64},{16,80},{32,96},{48,112},{64,0},{80,16},{96,32},{112,48},{1... | collective-permute-start | bytes 4718600 | tf_op jit(solution)/shard_map/ppermute | solution.py:22
  178.7 0.9 copy-start.11
  179.7 0.9 copy-start.19
  183.0 7.0 %copy-start.2 = (bf16[2,1040,256]{2,1,0:T(8,128)(2,1)}, bf16[2,1040,256]{2,1,0:T(8,128)(2,1)S(1)}, u32[]{:S(2)}) copy-start(bf16[2,1040,256]{2,1,0:T(8,128)(2,1)S(1)} %collective-permute-done.18.pair_other_ref.clip_other_ref.refs_1_) | copy-start | bytes 3194884
  184.4 64.1 %collective-permute-start.20 = (bf16[2,1024,384]{2,1,0:T(8,128)(2,1)}, bf16[2,1024,384]{2,1,0:T(8,128)(2,1)}, u32[]{:S(2)}, u32[]{:S(2)}) collective-permute-start(bf16[2,1024,384]{2,1,0:T(8,128)(2,1)} %shard_map.100.pair_ref), channel_id=1, source_target_pairs={{0,64},{16,80},{32,96},{48,112},{64,0},{80,16},{96,32},{112,48},{1... | collective-permute-start | bytes 4718600 | tf_op jit(solution)/shard_map/ppermute | solution.py:22
  193.7 6.3 %copy-start.10 = (bf16[1024,128]{1,0:T(8,128)(2,1)S(1)}, bf16[1024,128]{1,0:T(8,128)(2,1)}, u32[]{:S(2)}) copy-start(bf16[1024,128]{1,0:T(8,128)(2,1)} %get-tuple-element.103.old_other_ref) | copy-start | bytes 786436
  193.7 6.3 %copy-start.14 = (bf16[2,1024,128]{2,1,0:T(8,128)(2,1)S(1)}, bf16[2,1024,128]{2,1,0:T(8,128)(2,1)}, u32[]{:S(2)}) copy-start(bf16[2,1024,128]{2,1,0:T(8,128)(2,1)} %get-tuple-element.66.pair_ref) | copy-start | bytes 1572868
  193.7 6.3 %copy-start.17 = (bf16[1024,128]{1,0:T(8,128)(2,1)S(1)}, bf16[1024,128]{1,0:T(8,128)(2,1)}, u32[]{:S(2)}) copy-start(bf16[1024,128]{1,0:T(8,128)(2,1)} %get-tuple-element.67.step_ref) | copy-start | bytes 786436
  200.1 14.7 %copy-start.9 = (bf16[2,1024,128]{2,1,0:T(8,128)(2,1)S(1)}, bf16[2,1024,128]{2,1,0:T(8,128)(2,1)}, u32[]{:S(2)}) copy-start(bf16[2,1024,128]{2,1,0:T(8,128)(2,1)} %get-tuple-element.58.refs_0_) | copy-start | bytes 1572868
  200.1 18.2 %copy-start.12 = (bf16[1024,384]{1,0:T(8,128)(2,1)S(1)}, bf16[1024,384]{1,0:T(8,128)(2,1)}, u32[]{:S(2)}) copy-start(bf16[1024,384]{1,0:T(8,128)(2,1)} %get-tuple-element.88.step_ref) | copy-start | bytes 2359300
  214.7 43.8 %collective-permute-start.19 = (bf16[2,1024,128]{2,1,0:T(8,128)(2,1)S(1)}, bf16[2,1024,128]{2,1,0:T(8,128)(2,1)S(1)}, u32[]{:S(2)}, u32[]{:S(2)}) collective-permute-start(bf16[2,1024,128]{2,1,0:T(8,128)(2,1)S(1)} %shard_map.98.pair_ref), channel_id=1, source_target_pairs={{0,64},{16,80},{32,96},{48,112},{64,0},{80,16},{96,32},{112,48},{1... | collective-permute-start | bytes 1572872 | tf_op jit(solution)/shard_map/ppermute | solution.py:22
  218.3 30.2 %copy-start.13 = (bf16[1024,384]{1,0:T(8,128)(2,1)S(1)}, bf16[1024,384]{1,0:T(8,128)(2,1)}, u32[]{:S(2)}) copy-start(bf16[1024,384]{1,0:T(8,128)(2,1)} %get-tuple-element.87.step_ref) | copy-start | bytes 2359300
  248.5 10.0 %copy-start.18 = (bf16[1024,128]{1,0:T(8,128)(2,1)S(1)}, bf16[1024,128]{1,0:T(8,128)(2,1)}, u32[]{:S(2)}) copy-start(bf16[1024,128]{1,0:T(8,128)(2,1)} %get-tuple-element.84.step_ref) | copy-start | bytes 786436
